TPU v7x, 512 devices: a whole 4x4x16 slice. The times are simulated.
512 devices in a mesh: op: 16 (over z), sec: 32 (over y, x, core).
Axes of the slice: x: 4, y: 4, z: 16, core: 2. Of those that a mesh axis runs over, the one named last changes fastest.
Arguments:
- psi: bfloat16 [2, 64, 512, 512], P(None, 'sec'), may hold values from -6 to 6
- left_op: bfloat16 [48, 512, 512], P('op'), may hold values from -0.02734375 to 0.02734375
- right_op: bfloat16 [48, 512, 512], P('op'), may hold values from -0.25 to 0.25
- link: int32 [48, 64, 5], P('op', 'sec'), may hold values 0 or 1
Outputs:
- sigma: float32 [2, 64, 512, 512], P(None, 'sec', 'op')
All inputs are finite; a program needn't handle non-finite values. No bound on the sum of `link` on one device may be relied on, other than what follows from the above.
Results may differ from a plain program's by a relative error of at most 0.0041.
Values may be sent and summed in bfloat16 or wider, within the bound.
No kernel may reach another device: no remote copies, remote signals or barrier semaphores. Data moves between devices by JAX's collectives and lax.ppermute only.
A program may use at most 64 MiB of HBM per device.

v0:
```python
import jax
import jax.numpy as jnp
from jax import lax
from jax.sharding import PartitionSpec as P


def extended(block, sides, width):
    for axis, dim in sides:
        count = lax.axis_size(axis)
        forward = [(i, i + 1) for i in range(count - 1)]
        backward = [(target, source) for source, target in forward]
        low = lax.ppermute(
            lax.slice_in_dim(block, block.shape[dim] - width, None, axis=dim), axis, forward
        )
        high = lax.ppermute(lax.slice_in_dim(block, 0, width, axis=dim), axis, backward)
        block = jnp.concatenate([low, block, high], axis=dim)
    return block


def shards(psi, left_op, right_op, link):
    vectors, sectors, rows, columns = psi.shape
    reach_width = link.shape[2] // 2
    padded = extended(psi, (("sec", 1),), reach_width)
    summed = jnp.zeros((vectors, sectors, rows, columns), jnp.float32)
    for position in range(link.shape[0]):
        links = link[position].astype(jnp.float32)
        combined = jnp.zeros((vectors, sectors, rows, columns), jnp.float32)
        for offset in range(2 * reach_width + 1):
            combined = combined + links[:, offset][None, :, None, None] * padded[
                :, offset : offset + sectors
            ].astype(jnp.float32)
        combined = combined.astype(jnp.bfloat16)
        halved = jnp.einsum(
            "vtab,cb->vtac", combined, right_op[position], preferred_element_type=jnp.float32
        ).astype(jnp.bfloat16)
        summed = summed + jnp.einsum(
            "ea,vtac->vtec", left_op[position], halved, preferred_element_type=jnp.float32
        )
    whole = lax.psum(summed, "op")
    share_rows = rows // lax.axis_size("op")
    return lax.dynamic_slice_in_dim(whole, lax.axis_index("op") * share_rows, share_rows, 2)


def solution(mesh):
    placed = (
        P(None, "sec", None, None),
        P("op", None, None),
        P("op", None, None),
        P("op", "sec", None),
    )
    return jax.shard_map(
        shards, mesh=mesh, in_specs=placed, out_specs=P(None, "sec", "op", None), check_vma=False
    )
```

profile of v0, /device:TPU:24, one launch (start us, length us, event | category | flops | bytes accessed | tf_op | source)
XLA Modules:
  0.0 238.9 jit_solution(13856101179765914563)
XLA Ops:
  6.5 0.0 all-reduce.2.cloned.1.call-start
  6.5 1.9 collective-permute-start
  8.5 5.8 %collective-permute-start.1 = (bf16[2,2,512,512]{3,2,1,0:T(8,128)(2,1)}, bf16[2,2,512,512]{3,2,1,0:T(8,128)(2,1)S(1)}, u32[]{:S(2)}, u32[]{:S(2)}) collective-permute-start(bf16[2,2,512,512]{3,2,1,0:T(8,128)(2,1)} %param.4), channel_id=1, source_target_pairs={{1,0},{2,1},{3,2},{4,3},{5,4},{6,5},{7,6},{8,7},{9,8},{10,9},{11,1... | collective-permute-start | bytes 6291464 | tf_op jit(solution)/shard_map/ppermute | solution.py:15
  14.2 0.7 convert_bitcast_fusion
  14.9 0.2 slice_reduce_fusion.14
  15.2 0.3 slice_reduce_fusion.4
  15.5 20.7 %collective-permute-done = bf16[2,2,512,512]{3,2,1,0:T(8,128)(2,1)S(1)} collective-permute-done((bf16[2,2,512,512]{3,2,1,0:T(8,128)(2,1)}, bf16[2,2,512,512]{3,2,1,0:T(8,128)(2,1)S(1)}, u32[]{:S(2)}, u32[]{:S(2)}) %collective-permute-start) | collective-permute-done | bytes 2097184 | tf_op jit(solution)/shard_map/ppermute | solution.py:12
  36.2 0.0 copy-start.1
  36.2 1.9 collective-permute-done.1
  38.1 0.0 copy-start.2
  38.1 0.0 copy-done.1
  38.1 1.3 copy-done.2
  39.4 0.0 copy-start
  39.4 10.1 %fusion.33 = f32[2,2,512,512]{3,2,1,0:T(8,128)} fusion(bf16[2,2,512,512]{3,2,1,0:T(8,128)(2,1)} %copy-done.1, bf16[2,2,512,512]{3,2,1,0:T(8,128)(2,1)} %param.4, bf16[2,2,512,512]{3,2,1,0:T(8,128)(2,1)} %copy-done.2, f32[2]{0:T(128)S(1)} %get-tuple-element.26, f32[2]{0:T(128)S(1)} %get-tuple-element.25, f32[2]{0:T(128)S(1)} %get-tuple-element.24, ...), kind=kOutput, calls=%fused_computation.48 | convolution fusion | flops 2166358016 | bytes 11534376 | tf_op jit(solution)/shard_map/ea,vtac->vtec/dot_general | solution.py:36
  49.5 0.0 copy-done
  49.5 8.8 %fusion.40 = f32[2,2,512,512]{3,2,1,0:T(8,128)} fusion(bf16[2,2,512,512]{3,2,1,0:T(8,128)(2,1)} %copy-done.1, bf16[2,2,512,512]{3,2,1,0:T(8,128)(2,1)S(1)} %copy-done, bf16[2,2,512,512]{3,2,1,0:T(8,128)(2,1)} %copy-done.2, f32[2]{0:T(128)S(1)} %get-tuple-element.16, f32[2]{0:T(128)S(1)} %get-tuple-element.17, f32[2]{0:T(128)S(1)} %get-tuple-element.18, ...), kind=kOutput, calls=%fused_computation.55 | convolution fusion | flops 2166358016 | bytes 11534376 | tf_op jit(solution)/shard_map/ea,vtac->vtec/dot_general | solution.py:36
  58.3 9.4 %add_bitcast_fusion = f32[2,2,512,512]{2,3,1,0:T(8,128)} fusion(f32[2,2,512,512]{3,2,1,0:T(8,128)} %fusion.40, f32[2,2,512,512]{3,2,1,0:T(8,128)} %fusion.33, bf16[2,2,512,512]{3,2,1,0:T(8,128)(2,1)} %copy-done.1, bf16[2,2,512,512]{3,2,1,0:T(8,128)(2,1)S(1)} %copy-done, bf16[2,2,512,512]{3,2,1,0:T(8,128)(2,1)} %copy-done.2, f32[2]{0:T(128)S(1)} %get-tuple-element.6, ...), kind=kOutput, calls=%fused_computation.30 | convolution fusion | flops 2168455168 | bytes 19922984 | tf_op jit(solution)/shard_map/ea,vtac->vtec/dot_general | solution.py:36
  67.7 0.0 all-reduce.2.cloned.1.call-update
  67.7 161.7 %all-reduce.2.cloned.1.call-done = f32[2,2,512,512]{2,3,1,0:T(8,128)} async-done(((f32[2,2,512,512]{2,3,1,0:T(8,128)}), f32[2,2,512,512]{2,3,1,0:T(8,128)}) %all-reduce.2.cloned.1.call-update) | async-done | bytes 4194320 | tf_op jit(solution)/shard_map/psum | solution.py:39
  229.4 1.6 constant_dynamic-slice_fusion
  231.0 1.0 copy.6
Async XLA Ops:
  6.5 222.9 %all-reduce.2.cloned.1.call-start = ((), (), s32[]{:S(2)}) async-start(), calls=%async_computation | async-start | bytes 8388608 | tf_op jit(solution)/shard_map/psum | solution.py:39
  6.5 29.7 %collective-permute-start = (bf16[2,2,512,512]{3,2,1,0:T(8,128)(2,1)}, bf16[2,2,512,512]{3,2,1,0:T(8,128)(2,1)S(1)}, u32[]{:S(2)}, u32[]{:S(2)}) collective-permute-start(bf16[2,2,512,512]{3,2,1,0:T(8,128)(2,1)} %param.4), channel_id=1, source_target_pairs={{0,1},{1,2},{2,3},{3,4},{4,5},{5,6},{6,7},{7,8},{8,9},{9,10},{10,1... | collective-permute-start | bytes 6291464 | tf_op jit(solution)/shard_map/ppermute | solution.py:12
  8.5 29.6 %collective-permute-start.1 = (bf16[2,2,512,512]{3,2,1,0:T(8,128)(2,1)}, bf16[2,2,512,512]{3,2,1,0:T(8,128)(2,1)S(1)}, u32[]{:S(2)}, u32[]{:S(2)}) collective-permute-start(bf16[2,2,512,512]{3,2,1,0:T(8,128)(2,1)} %param.4), channel_id=1, source_target_pairs={{1,0},{2,1},{3,2},{4,3},{5,4},{6,5},{7,6},{8,7},{9,8},{10,9},{11,1... | collective-permute-start | bytes 6291464 | tf_op jit(solution)/shard_map/ppermute | solution.py:15
  36.2 1.9 copy-start.1
  38.1 1.3 copy-start.2
  39.4 10.1 %copy-start = (bf16[2,2,512,512]{3,2,1,0:T(8,128)(2,1)S(1)}, bf16[2,2,512,512]{3,2,1,0:T(8,128)(2,1)}, u32[]{:S(2)}) copy-start(bf16[2,2,512,512]{3,2,1,0:T(8,128)(2,1)} %param.4) | copy-start | bytes 6291460
Sparse Core Ops, SparseCore 0:
  67.8 161.5 all-reduce.1
where the time goes:
time: 239 us
  waiting for transfers between devices  184 us (77%)
  matrix products  28.3 us (12%)
  between operations  13.4 us (6%)
  starting transfers between devices  7.67 us (3%)
  local copies, waits for them, and re-layouts  4.42 us (2%)
    psum x1, waiting for transfers between devices, shards(): whole = lax.psum(summed, 'op')  162 us
    dot_general x3, matrix products, shards(): jnp.einsum('ea,vtac->vtec', left_op[position], halved, preferred_element_...  28.3 us
    ppermute x1, waiting for transfers between devices, extended(): lax.ppermute(lax.slice_in_dim(block, block.shape[dim] - width, None, axis...  20.7 us
    ppermute x1, starting transfers between devices, extended(): lax.ppermute(lax.slice_in_dim(block, 0, width, axis=dim), axis, backward)  5.75 us
  transfers between devices with their start and end apart: 3, of which 3 were waited for; matrix products, arithmetic and copies ran while one was open for 1% of the time, Pallas kernels for 0%

commit v1 on v0

v1 whole, which is shorter than its diff:
```python
import jax
import jax.numpy as jnp
from jax import lax
from jax.experimental import pallas as pl
from jax.experimental.pallas import tpu as pltpu
from jax.sharding import PartitionSpec as P

F32, BF16 = jnp.float32, jnp.bfloat16


def kernel(weight, across, own, chip, right, left, *rest):
    outs, (combined, halved) = rest[:4], rest[4:]
    terms, size = right.shape[0], right.shape[1]
    sources = (across, own, chip)
    v = pl.program_id(0)
    tile = 32
    for j in range(2):
        for start in range(0, size, tile):
            rows = pl.ds(start, tile)
            totals = [None] * terms
            for slot in range(6):
                block = sources[slot // 2][0, slot % 2, rows, :].astype(F32)
                for k in range(terms):
                    part = weight[k * 12 + j * 6 + slot] * block
                    totals[k] = part if totals[k] is None else totals[k] + part
            for k in range(terms):
                combined[k, rows, :] = totals[k].astype(BF16)
        for k in range(terms):
            halved[pl.ds(k * size, size), :] = jnp.dot(
                combined[k], right[k], preferred_element_type=F32
            ).astype(BF16)
        part = size // 4
        for c in range(4):
            outs[c][0, j] = jnp.dot(
                left[pl.ds(c * part, part), :], halved[...], preferred_element_type=F32
            ).astype(BF16)


def partials(weight, across, own, chip, right, left):
    terms, size = right.shape[0], right.shape[1]
    vectors = own.shape[0]
    source = pl.BlockSpec((1, 2, size, size), lambda v: (v, 0, 0, 0))
    share = pl.BlockSpec((1, 2, size // 4, size), lambda v: (v, 0, 0, 0))
    return pl.pallas_call(
        kernel,
        grid=(vectors,),
        in_specs=[
            pl.BlockSpec(memory_space=pltpu.SMEM),
            source,
            source,
            source,
            pl.BlockSpec(right.shape, lambda v: (0, 0, 0)),
            pl.BlockSpec(left.shape, lambda v: (0, 0)),
        ],
        out_specs=[share] * 4,
        out_shape=[jax.ShapeDtypeStruct((vectors, 2, size // 4, size), BF16)] * 4,
        scratch_shapes=[
            pltpu.VMEM((terms, size, size), BF16),
            pltpu.VMEM((terms * size, size), BF16),
        ],
        compiler_params=pltpu.CompilerParams(vmem_limit_bytes=40 * 2**20),
        cost_estimate=pl.CostEstimate(
            flops=4 * terms * vectors * 2 * size**3, bytes_accessed=12 * 2**20, transcendentals=0
        ),
    )(weight, across, own, chip, right, left)


def shards(psi, left_op, right_op, link):
    terms, size = left_op.shape[0], left_op.shape[1]
    z = lax.axis_index("op")
    place = lax.axis_index("sec")
    count = lax.axis_size("sec")
    core = place % 2

    chip = lax.ppermute(psi, "sec", [(i, i ^ 1) for i in range(count)])
    facing = [(i, (i + 1) % count) for i in range(1, count, 2)]
    across = lax.ppermute(psi, "sec", facing + [(b, a) for a, b in facing])

    window = jnp.stack([jnp.pad(link[:, j], ((0, 0), (j, 1 - j))) for j in range(2)], axis=1)
    slot = jnp.arange(6)
    outside = ((place == 0) & (slot < 2)) | ((place == count - 1) & (slot >= 4))
    window = jnp.where(outside, 0, window).astype(F32)
    swapped = jnp.concatenate([window[..., 4:], window[..., 2:4], window[..., :2]], axis=-1)
    weight = jnp.where(core == 0, window, swapped).reshape(-1)

    right = jnp.swapaxes(right_op, 1, 2)
    by_class = left_op.reshape(terms, 4, 4, size // 16, size)
    by_class = jnp.roll(by_class, -(z % 4), axis=2)
    left = by_class.transpose(2, 1, 3, 0, 4).reshape(size, terms * size)

    mine, up, two, down = partials(weight, across, psi, chip, right, left)

    def shift(x, by):
        n = lax.axis_size("op")
        return lax.ppermute(x, "op", [(i, (i + by) % n) for i in range(n)])

    up = shift(up, 1)
    down = shift(down, -1)
    two = jnp.stack([shift(two[:, 0], -2), shift(two[:, 1], 2)], axis=1)
    group = sum(x.astype(F32) for x in (mine, up, down, two)).astype(BF16)
    shares = group.reshape(2, 2, 4, size // 16, size).transpose(2, 0, 1, 3, 4)
    groups = [[a + 4 * i for i in range(4)] for a in range(4)]
    shares = lax.all_to_all(shares, "op", 0, 0, axis_index_groups=groups, tiled=True)
    return shares.astype(F32).sum(axis=0)


def solution(mesh):
    placed = (
        P(None, "sec", None, None),
        P("op", None, None),
        P("op", None, None),
        P("op", "sec", None),
    )
    return jax.shard_map(
        shards, mesh=mesh, in_specs=placed, out_specs=P(None, "sec", "op", None), check_vma=False
    )
```

time: 239 us -> 116 us (0.49)
  the two profiles are of different devices: /device:TPU:24 before, /device:TPU:54 now
where the time goes in v1:
time: 116 us
  blocking collectives  40 us (34%)
  waiting for transfers between devices  29.3 us (25%)
  starting transfers between devices  24 us (21%)
  Pallas kernels  11.7 us (10%)
  local copies, waits for them, and re-layouts  6.05 us (5%)
  other arithmetic  4.97 us (4%)
    all_to_all x1, blocking collectives, shards(): lax.all_to_all(shares, 'op', 0, 0, axis_index_groups=groups, tiled=True)  40 us
    ppermute x4, starting transfers between devices, shift(): return lax.ppermute(x, 'op', [(i, (i + by) % n) for i in range(n)])  18.7 us
    ppermute x4, waiting for transfers between devices, shift(): return lax.ppermute(x, 'op', [(i, (i + by) % n) for i in range(n)])  16.7 us
    ppermute x1, waiting for transfers between devices, shards(): across = lax.ppermute(psi, 'sec', facing + [(b, a) for a, b in facing])  12.5 us
    pallas_call x1, Pallas kernels, partials(): pl.pallas_call(kernel, grid=(vectors,), in_specs=[pl.BlockSpec(memory_spa...  11.7 us
    concatenate x1, other arithmetic, shards(): by_class = jnp.roll(by_class, -(z % 4), axis=2)  3.83 us
    ppermute x1, starting transfers between devices, shards(): chip = lax.ppermute(psi, 'sec', [(i, i ^ 1) for i in range(count)])  2.96 us
    reshape x1, local copies, waits for them, and re-layouts, shards(): by_class = left_op.reshape(terms, 4, 4, size // 16, size)  2.7 us
  transfers between devices with their start and end apart: 6, of which 3 were waited for; matrix products, arithmetic and copies ran while one was open for 9% of the time, Pallas kernels for 0%

profile of v1, /device:TPU:54, one launch (start us, length us, event | category | flops | bytes accessed | tf_op | source)
XLA Modules:
  0.0 116.1 jit_solution(4885143662107921579)
XLA Ops:
  0.0 0.0 copy-start.1
  0.0 2.3 %collective-permute-start = (bf16[2,2,512,512]{3,2,1,0:T(8,128)(2,1)}, bf16[2,2,512,512]{3,2,1,0:T(8,128)(2,1)}, u32[]{:S(2)}, u32[]{:S(2)}) collective-permute-start(bf16[2,2,512,512]{3,2,1,0:T(8,128)(2,1)} %own.1), channel_id=1, source_target_pairs={{1,2},{3,4},{5,6},{7,8},{9,10},{11,12},{13,14},{15,16},{17,18},{19... | collective-permute-start | bytes 6291464 | tf_op jit(solution)/shard_map/ppermute | solution.py:77
  2.3 3.0 %collective-permute-start.1 = (bf16[2,2,512,512]{3,2,1,0:T(8,128)(2,1)}, bf16[2,2,512,512]{3,2,1,0:T(8,128)(2,1)}, u32[]{:S(2)}, u32[]{:S(2)}) collective-permute-start(bf16[2,2,512,512]{3,2,1,0:T(8,128)(2,1)} %own.1), channel_id=1, source_target_pairs={{0,1},{1,0},{2,3},{3,2},{4,5},{5,4},{6,7},{7,6},{8,9},{9,8},{10,11... | collective-permute-start | bytes 6291464 | tf_op jit(solution)/shard_map/ppermute | solution.py:75
  5.3 0.8 fusion.3
  6.1 0.1 pad_bitcast_fusion
  6.2 0.1 fusion.2
  6.3 0.1 maximum_select_fusion
  6.4 0.1 select_n.45.weight
  6.4 1.7 %copy.18 = bf16[3,512,512]{1,2,0:T(8,128)(2,1)S(1)} copy(bf16[3,512,512]{2,1,0:T(8,128)(2,1)} %param.6) | data formatting | bytes 3145728 | tf_op args[2]
  8.2 0.0 copy-done.1
  8.2 2.7 %copy.19 = bf16[3,4,4,32,512]{4,0,3,1,2:T(4,128)(2,1)} copy(bf16[3,4,4,32,512]{4,3,2,1,0:T(8,128)(2,1)S(1)} %bitcast.29) | data formatting | bytes 3145728 | tf_op jit(solution)/shard_map/reshape | solution.py:87
  10.9 3.8 %fusion = bf16[3,4,4,32,512]{4,0,3,1,2:T(4,128)(2,1)S(1)} fusion(s32[]{:T(128)S(6)} %select_n.48, bf16[3,4,4,32,512]{4,0,3,1,2:T(4,128)(2,1)} %copy.19), kind=kLoop, calls=%fused_computation.2 | loop fusion | flops 786432 | bytes 3145732 | tf_op jit(solution)/shard_map/jit(_roll_dynamic)/concatenate | solution.py:88
  14.7 0.0 copy-start
  14.7 0.5 copy.26
  15.3 12.5 %collective-permute-done.across = bf16[2,2,512,512]{3,2,1,0:T(8,128)(2,1)} collective-permute-done((bf16[2,2,512,512]{3,2,1,0:T(8,128)(2,1)}, bf16[2,2,512,512]{3,2,1,0:T(8,128)(2,1)}, u32[]{:S(2)}, u32[]{:S(2)}) %collective-permute-start) | collective-permute-done | bytes 2097184 | tf_op jit(solution)/shard_map/ppermute | solution.py:77
  27.8 0.0 collective-permute-done.1.chip
  27.8 0.0 copy-done
  27.8 11.7 %shard_map.46 = (bf16[2,2,128,512]{3,2,1,0:T(8,128)(2,1)S(1)}, bf16[2,2,128,512]{3,2,1,0:T(8,128)(2,1)S(1)}, bf16[2,2,128,512]{3,2,1,0:T(8,128)(2,1)S(1)}, bf16[2,2,128,512]{3,2,1,0:T(8,128)(2,1)S(1)}) custom-call(f32[36]{0:T(128)S(1)} %select_n.45.weight, bf16[2,2,512,512]{3,2,1,0:T(8,128)(2,1)} %collective-permute-done.across, ...), custom_call_target="tpu_custom_call" | custom-call | flops 6442450944 | bytes 12582912 | tf_op jit(solution)/shard_map/pallas_call | solution.py:44
  39.5 3.8 %collective-permute-start.2 = (bf16[2,2,128,512]{3,2,1,0:T(8,128)(2,1)S(1)}, bf16[2,2,128,512]{3,2,1,0:T(8,128)(2,1)S(1)}, u32[]{:S(2)}, u32[]{:S(2)}) collective-permute-start(bf16[2,2,128,512]{3,2,1,0:T(8,128)(2,1)S(1)} %get-tuple-element.10), channel_id=1, source_target_pairs={{0,32},{32,64},{64,96},{96,128},{128,160},{160,192},{192,224},{224... | collective-permute-start | bytes 1572872 | tf_op jit(solution)/shard_map/ppermute | solution.py:95
  43.4 2.0 %collective-permute-start.3 = (bf16[2,2,128,512]{3,2,1,0:T(8,128)(2,1)S(1)}, bf16[2,2,128,512]{3,2,1,0:T(8,128)(2,1)S(1)}, u32[]{:S(2)}, u32[]{:S(2)}) collective-permute-start(bf16[2,2,128,512]{3,2,1,0:T(8,128)(2,1)S(1)} %get-tuple-element.11), channel_id=1, source_target_pairs={{0,480},{32,0},{64,32},{96,64},{128,96},{160,128},{192,160},{224,1... | collective-permute-start | bytes 1572872 | tf_op jit(solution)/shard_map/ppermute | solution.py:95
  45.4 10.9 %collective-permute-start.4 = (bf16[2,128,512]{2,1,0:T(8,128)(2,1)S(1)}, bf16[2,128,512]{2,1,0:T(8,128)(2,1)S(1)}, u32[]{:S(2)}, u32[]{:S(2)}) collective-permute-start(bf16[2,128,512]{2,1,0:T(8,128)(2,1)S(1)} %get-tuple-element.13), channel_id=1, source_target_pairs={{0,448},{32,480},{64,0},{96,32},{128,64},{160,96},{192,128},{224,1... | collective-permute-start | bytes 786440 | tf_op jit(solution)/shard_map/ppermute | solution.py:95
  56.4 1.9 %collective-permute-start.5 = (bf16[2,128,512]{2,1,0:T(8,128)(2,1)S(1)}, bf16[2,128,512]{2,1,0:T(8,128)(2,1)S(1)}, u32[]{:S(2)}, u32[]{:S(2)}) collective-permute-start(bf16[2,128,512]{2,1,0:T(8,128)(2,1)S(1)} %get-tuple-element.14), channel_id=1, source_target_pairs={{0,64},{32,96},{64,128},{96,160},{128,192},{160,224},{192,256},{22... | collective-permute-start | bytes 786440 | tf_op jit(solution)/shard_map/ppermute | solution.py:95
  58.3 11.2 %collective-permute-done.4 = bf16[2,128,512]{2,1,0:T(8,128)(2,1)S(1)} collective-permute-done((bf16[2,128,512]{2,1,0:T(8,128)(2,1)S(1)}, bf16[2,128,512]{2,1,0:T(8,128)(2,1)S(1)}, u32[]{:S(2)}, u32[]{:S(2)}) %collective-permute-start.4) | collective-permute-done | bytes 262176 | tf_op jit(solution)/shard_map/ppermute | solution.py:95
  69.5 5.5 %collective-permute-done.5 = bf16[2,128,512]{2,1,0:T(8,128)(2,1)S(1)} collective-permute-done((bf16[2,128,512]{2,1,0:T(8,128)(2,1)S(1)}, bf16[2,128,512]{2,1,0:T(8,128)(2,1)S(1)}, u32[]{:S(2)}, u32[]{:S(2)}) %collective-permute-start.5) | collective-permute-done | bytes 262176 | tf_op jit(solution)/shard_map/ppermute | solution.py:95
  75.0 0.0 collective-permute-done.2
  75.0 0.0 collective-permute-done.3
  75.1 0.3 add_convert_fusion
  75.4 40.0 %all_to_all.5 = bf16[4,2,2,32,512]{4,3,2,1,0:T(8,128)(2,1)S(1)} all-to-all(bf16[4,2,2,32,512]{4,3,2,1,0:T(8,128)(2,1)S(1)} %bitcast.28), channel_id=1, replica_groups={{0,128,256,384},{32,160,288,416},{64,192,320,448},{96,224,352,480},{1,1..., dimensions={0} | all-to-all | bytes 1048576 | tf_op jit(solution)/shard_map/all_to_all | solution.py:103
  115.3 0.8 convert_reduce_fusion
  (7 shorter events, 0.1 us)
Async XLA Ops:
  0.0 8.2 %copy-start.1 = (bf16[3,512,512]{2,1,0:T(8,128)(2,1)S(1)}, bf16[3,512,512]{2,1,0:T(8,128)(2,1)}, u32[]{:S(2)}) copy-start(bf16[3,512,512]{2,1,0:T(8,128)(2,1)} %param.5) | copy-start | bytes 4718596
  0.0 27.8 %collective-permute-start = (bf16[2,2,512,512]{3,2,1,0:T(8,128)(2,1)}, bf16[2,2,512,512]{3,2,1,0:T(8,128)(2,1)}, u32[]{:S(2)}, u32[]{:S(2)}) collective-permute-start(bf16[2,2,512,512]{3,2,1,0:T(8,128)(2,1)} %own.1), channel_id=1, source_target_pairs={{1,2},{3,4},{5,6},{7,8},{9,10},{11,12},{13,14},{15,16},{17,18},{19... | collective-permute-start | bytes 6291464 | tf_op jit(solution)/shard_map/ppermute | solution.py:77
  2.3 25.5 %collective-permute-start.1 = (bf16[2,2,512,512]{3,2,1,0:T(8,128)(2,1)}, bf16[2,2,512,512]{3,2,1,0:T(8,128)(2,1)}, u32[]{:S(2)}, u32[]{:S(2)}) collective-permute-start(bf16[2,2,512,512]{3,2,1,0:T(8,128)(2,1)} %own.1), channel_id=1, source_target_pairs={{0,1},{1,0},{2,3},{3,2},{4,5},{5,4},{6,7},{7,6},{8,9},{9,8},{10,11... | collective-permute-start | bytes 6291464 | tf_op jit(solution)/shard_map/ppermute | solution.py:75
  14.7 13.1 %copy-start = (bf16[2,2,512,512]{3,2,1,0:T(8,128)(2,1)S(1)}, bf16[2,2,512,512]{3,2,1,0:T(8,128)(2,1)}, u32[]{:S(2)}) copy-start(bf16[2,2,512,512]{3,2,1,0:T(8,128)(2,1)} %own.1) | copy-start | bytes 6291460
  39.5 35.5 %collective-permute-start.2 = (bf16[2,2,128,512]{3,2,1,0:T(8,128)(2,1)S(1)}, bf16[2,2,128,512]{3,2,1,0:T(8,128)(2,1)S(1)}, u32[]{:S(2)}, u32[]{:S(2)}) collective-permute-start(bf16[2,2,128,512]{3,2,1,0:T(8,128)(2,1)S(1)} %get-tuple-element.10), channel_id=1, source_target_pairs={{0,32},{32,64},{64,96},{96,128},{128,160},{160,192},{192,224},{224... | collective-permute-start | bytes 1572872 | tf_op jit(solution)/shard_map/ppermute | solution.py:95
  43.4 31.7 %collective-permute-start.3 = (bf16[2,2,128,512]{3,2,1,0:T(8,128)(2,1)S(1)}, bf16[2,2,128,512]{3,2,1,0:T(8,128)(2,1)S(1)}, u32[]{:S(2)}, u32[]{:S(2)}) collective-permute-start(bf16[2,2,128,512]{3,2,1,0:T(8,128)(2,1)S(1)} %get-tuple-element.11), channel_id=1, source_target_pairs={{0,480},{32,0},{64,32},{96,64},{128,96},{160,128},{192,160},{224,1... | collective-permute-start | bytes 1572872 | tf_op jit(solution)/shard_map/ppermute | solution.py:95
  45.4 24.1 %collective-permute-start.4 = (bf16[2,128,512]{2,1,0:T(8,128)(2,1)S(1)}, bf16[2,128,512]{2,1,0:T(8,128)(2,1)S(1)}, u32[]{:S(2)}, u32[]{:S(2)}) collective-permute-start(bf16[2,128,512]{2,1,0:T(8,128)(2,1)S(1)} %get-tuple-element.13), channel_id=1, source_target_pairs={{0,448},{32,480},{64,0},{96,32},{128,64},{160,96},{192,128},{224,1... | collective-permute-start | bytes 786440 | tf_op jit(solution)/shard_map/ppermute | solution.py:95
  56.4 18.7 %collective-permute-start.5 = (bf16[2,128,512]{2,1,0:T(8,128)(2,1)S(1)}, bf16[2,128,512]{2,1,0:T(8,128)(2,1)S(1)}, u32[]{:S(2)}, u32[]{:S(2)}) collective-permute-start(bf16[2,128,512]{2,1,0:T(8,128)(2,1)S(1)} %get-tuple-element.14), channel_id=1, source_target_pairs={{0,64},{32,96},{64,128},{96,160},{128,192},{160,224},{192,256},{22... | collective-permute-start | bytes 786440 | tf_op jit(solution)/shard_map/ppermute | solution.py:95

commit v2 on v0

v2 whole, which is shorter than its diff:
```python
import jax
import jax.numpy as jnp
from jax import lax
from jax.experimental import pallas as pl
from jax.experimental.pallas import tpu as pltpu
from jax.sharding import PartitionSpec as P

F32, BF16 = jnp.float32, jnp.bfloat16
RING = 16
LEADERS = (0, 3, -3, 6, -6)
ORDER = [1 - p for p in LEADERS] + [-1 - p for p in LEADERS] + [-p for p in LEADERS] + [8]


def split_kernel(psi, *rest):
    outs, sems = rest[:-1], rest[-1]
    copies = [pltpu.make_async_copy(psi.at[v], out, sems.at[v]) for v, out in enumerate(outs)]
    for copy in copies:
        copy.start()
    for copy in copies:
        copy.wait()


def split(psi):
    vectors = psi.shape[0]
    return pl.pallas_call(
        split_kernel,
        in_specs=[pl.BlockSpec(memory_space=pl.ANY)],
        out_specs=[pl.BlockSpec(memory_space=pl.ANY)] * vectors,
        out_shape=[jax.ShapeDtypeStruct(psi.shape[1:], BF16)] * vectors,
        scratch_shapes=[pltpu.SemaphoreType.DMA((vectors,))],
        compiler_params=pltpu.CompilerParams(vmem_limit_bytes=56 * 2**20),
        cost_estimate=pl.CostEstimate(flops=0, bytes_accessed=4 * 2**20, transcendentals=0),
    )(psi)


def arrange_kernel(at, left, right, left_out, right_out):
    terms, size = left.shape[0], left.shape[1]
    share = size // RING
    sign = 1 - 2 * (at[0] % 2)
    for place, j in enumerate(ORDER):
        start = pl.multiple_of(lax.rem(at[2] + sign * j + RING, RING) * share, share)
        for k in range(terms):
            left_out[pl.ds(place * share, share), pl.ds(k * size, size)] = left[
                k, pl.ds(start, share), :
            ]
    for k in range(terms):
        right_out[k] = right[k].T


def arrange(at, left, right):
    terms, size = left.shape[0], left.shape[1]
    whole = pl.BlockSpec(memory_space=pltpu.VMEM)
    return pl.pallas_call(
        arrange_kernel,
        in_specs=[pl.BlockSpec(memory_space=pltpu.SMEM), whole, whole],
        out_specs=[whole, whole],
        out_shape=[
            jax.ShapeDtypeStruct((size, terms * size), BF16),
            jax.ShapeDtypeStruct(right.shape, BF16),
        ],
        compiler_params=pltpu.CompilerParams(vmem_limit_bytes=16 * 2**20),
        cost_estimate=pl.CostEstimate(flops=0, bytes_accessed=6 * 2**20, transcendentals=0),
    )(at, left, right)


def kernel(v, place, link, across, own, chip, right, left, up, down, mine, opposite, combined, halved):
    terms, size = right.shape[0], right.shape[1]
    first_core = place[0] % 2 == 0
    lowest, highest = place[0] == 0, place[0] == place[1] - 1
    half, tall, wide, high = size // 2, 16, 256, 128

    def weight(k, j, if_first, if_second):
        reach = jnp.where(first_core, if_first, if_second)
        outside = (lowest & (reach < 2 - j)) | (highest & (reach > 3 - j))
        return jnp.where(outside, 0, link[(k * 2 + j) * 5 + reach]).astype(F32)

    reaches = (((0, 4), (2, 2), (3, 3), (4, 0), (1, 1)), ((0, 4), (1, 1), (2, 2), (4, 0), (3, 3)))
    weights = [
        [[weight(k, j, *pair) for pair in reaches[j]] for k in range(terms)] for j in range(2)
    ]

    def combine(part):
        for row in range(0, half, tall):
            rows = pl.ds(part * half + row, tall)
            for column in range(0, size, wide):
                columns = pl.ds(column, wide)
                a0, a1 = (across[i, rows, columns].astype(F32) for i in range(2))
                o0, o1 = (own[i, rows, columns].astype(F32) for i in range(2))
                c0, c1 = (chip[v, i, rows, columns].astype(F32) for i in range(2))
                fifth = (jnp.where(first_core, a1, c1), jnp.where(first_core, c0, a0))
                for j, blocks in enumerate(((a0, o0, o1, c0, fifth[0]), (a1, o0, o1, c1, fifth[1]))):
                    for k in range(terms):
                        total = weights[j][k][0] * blocks[0]
                        for slot in range(1, 5):
                            total += weights[j][k][slot] * blocks[slot]
                        combined[part, j * terms + k, pl.ds(row, tall), columns] = total.astype(BF16)

    def multiply_right(part):
        for j in range(2):
            for k in range(terms):
                halved[j, pl.ds(k * size + part * half, half), :] = jnp.dot(
                    combined[part, j * terms + k], right[k], preferred_element_type=F32
                ).astype(BF16)

    combine(0)
    combine(1)
    multiply_right(0)
    multiply_right(1)
    for j in range(2):
        for top in range(0, size, high):
            sums = jnp.dot(
                left[pl.ds(top, high), :], halved[j], preferred_element_type=F32
            ).astype(BF16)
            start = 0
            for out in (up, down, mine, opposite):
                end = start + out.shape[1]
                low, stop = max(top, start), min(top + high, end)
                if low < stop:
                    out[j, pl.ds(low - start, stop - low)] = sums[low - top : stop - top]
                start = end


def partials(v, place, link, across, own, chip, right, left):
    terms, size = right.shape[0], right.shape[1]
    share = size // RING
    whole = pl.BlockSpec(memory_space=pltpu.VMEM)
    scalars = pl.BlockSpec(memory_space=pltpu.SMEM)
    counts = [len(LEADERS)] * 3 + [1]
    return pl.pallas_call(
        lambda *refs: kernel(v, *refs),
        in_specs=[scalars, scalars] + [whole] * 5,
        out_specs=[whole] * 4,
        out_shape=[jax.ShapeDtypeStruct((2, n * share, size), BF16) for n in counts],
        scratch_shapes=[
            pltpu.VMEM((2, 2 * terms, size // 2, size), BF16),
            pltpu.VMEM((2, terms * size, size), BF16),
        ],
        compiler_params=pltpu.CompilerParams(vmem_limit_bytes=32 * 2**20),
        cost_estimate=pl.CostEstimate(
            flops=8 * terms * size**3, bytes_accessed=8 * 2**20, transcendentals=0
        ),
    )(place, link, across, own, chip, right, left)


def shift(x, by):
    n, m = lax.axis_size("op"), lax.axis_size("sec")
    pairs = [
        (i * m + q, (i + (-by if q % 2 else by)) % n * m + q) for i in range(n) for q in range(m)
    ]
    return lax.ppermute(x, ("op", "sec"), pairs)


def shards(psi, left_op, right_op, link):
    place = lax.axis_index("sec")
    count = lax.axis_size("sec")
    vectors = psi.shape[0]
    share = psi.shape[2] // RING
    at = jnp.stack([place, count, lax.axis_index("op")]).astype(jnp.int32)

    facing = [(i, i + 1) for i in range(1, count - 1, 2)]
    facing += [(b, a) for a, b in facing]
    own = split(psi)
    across = [lax.ppermute(block, "sec", facing) for block in own]
    chip = lax.ppermute(psi, "sec", [(i, i ^ 1) for i in range(count)])

    left, right = arrange(at, left_op, right_op)
    totals, opposites = [], []
    for v in range(vectors):
        up, down, mine, opposite = partials(
            v, at, link.reshape(-1), across[v], own[v], chip, right, left
        )
        total = mine.astype(F32) + shift(up, 1).astype(F32) + shift(down, -1).astype(F32)
        totals.append(total.reshape(2, len(LEADERS), share, -1))
        opposites.append(opposite)
    opposite = shift(jnp.stack(opposites), -2).astype(F32)
    here, above, below, far_above, far_below = (
        jnp.stack([total[:, i] for total in totals]) for i in range(len(LEADERS))
    )
    far_above = shift((far_above + opposite).astype(BF16), -3).astype(F32)
    far_below = shift(far_below.astype(BF16), 3).astype(F32)
    above = shift((above + far_above).astype(BF16), -3).astype(F32)
    below = shift((below + far_below).astype(BF16), 3).astype(F32)
    return here + above + below


def solution(mesh):
    placed = (
        P(None, "sec", None, None),
        P("op", None, None),
        P("op", None, None),
        P("op", "sec", None),
    )
    return jax.shard_map(
        shards, mesh=mesh, in_specs=placed, out_specs=P(None, "sec", "op", None), check_vma=False
    )
```

time: 239 us -> 160 us (0.67)
  waiting for transfers between devices: 184 us -> 24.5 us
  Pallas kernels: 0 us -> 78.4 us
  starting transfers between devices: 7.67 us -> 52.4 us
  matrix products: 28.3 us -> 0 us
  between operations: 13.4 us -> 0.28 us
  local copies, waits for them, and re-layouts: 4.42 us -> 1.71 us
    psum x1 -> x0, waiting for transfers between devices: 162 us -> none  [shards(): whole = lax.psum(summed, 'op')]
    pallas_call x0 -> x4, Pallas kernels: none -> 78.4 us  [the longest x1 64.6 us: split(): pl.pallas_call(split_kernel, in_specs=[pl.BlockSpec(memory_space=pl.ANY)]...]
    ppermute x2 -> x12, starting transfers between devices: 7.66 us -> 52.4 us  [the longest x9 42.7 us: shift(): return lax.ppermute(x, ('op', 'sec'), pairs)]
    dot_general x3 -> x0, matrix products: 28.3 us -> none  [shards(): jnp.einsum('ea,vtac->vtec', left_op[position], halved, preferred_element_...]
    dynamic_slice x2 -> x0, local copies, waits for them, and re-layouts: 2.58 us -> none  [shards(): lax.dynamic_slice_in_dim(whole, lax.axis_index('op') * share_rows, share_...]
    ppermute x2 -> x12, waiting for transfers between devices: 22.6 us -> 24.5 us  [the longest x9 16.3 us: shift(): return lax.ppermute(x, ('op', 'sec'), pairs)]
  transfers between devices with their start and end apart: 3 -> 12, of which waited for: 3 -> 6; matrix products, arithmetic and copies ran while one was open for 1% -> 0% of each run, Pallas kernels for 0% -> 49%
where the time goes in v2:
time: 160 us; the launch traced here: 158 us
  Pallas kernels  78.4 us (49%)
  starting transfers between devices  52.4 us (33%)
  waiting for transfers between devices  24.5 us (15%)
  local copies, waits for them, and re-layouts  1.71 us (1%)
    pallas_call x1, Pallas kernels, split(): pl.pallas_call(split_kernel, in_specs=[pl.BlockSpec(memory_space=pl.ANY)]...  64.6 us
    ppermute x9, starting transfers between devices, shift(): return lax.ppermute(x, ('op', 'sec'), pairs)  42.7 us
    ppermute x9, waiting for transfers between devices, shift(): return lax.ppermute(x, ('op', 'sec'), pairs)  16.3 us
    pallas_call x2, Pallas kernels, partials(): pl.pallas_call(lambda *refs: kernel(v, *refs), in_specs=[scalars, scalars...  12.7 us
    ppermute x2, waiting for transfers between devices, shards(): across = [lax.ppermute(block, 'sec', facing) for block in own]  8.21 us
    ppermute x2, starting transfers between devices, shards(): across = [lax.ppermute(block, 'sec', facing) for block in own]  7.67 us
  transfers between devices with their start and end apart: 12, of which 6 were waited for; matrix products, arithmetic and copies ran while one was open for 0% of the time, Pallas kernels for 49%

profile of v2, /device:TPU:24, one launch (start us, length us, event | category | flops | bytes accessed | tf_op | source)
XLA Modules:
  0.0 158.4 jit_solution(6648660974599297140)
XLA Ops:
  0.0 2.0 %collective-permute-start.1 = (bf16[2,2,512,512]{3,2,1,0:T(8,128)(2,1)}, bf16[2,2,512,512]{3,2,1,0:T(8,128)(2,1)}, u32[]{:S(2)}, u32[]{:S(2)}) collective-permute-start(bf16[2,2,512,512]{3,2,1,0:T(8,128)(2,1)} %psi.1), channel_id=1, source_target_pairs={{0,1},{1,0},{2,3},{3,2},{4,5},{5,4},{6,7},{7,6},{8,9},{9,8},{10,11... | collective-permute-start | bytes 6291464 | tf_op jit(solution)/shard_map/ppermute | solution.py:164
  2.1 64.6 %shard_map.46 = (bf16[2,512,512]{2,1,0:T(8,128)(2,1)}, bf16[2,512,512]{2,1,0:T(8,128)(2,1)}) custom-call(bf16[2,2,512,512]{3,2,1,0:T(8,128)(2,1)} %psi.1), custom_call_target="tpu_custom_call" | custom-call | bytes 4194304 | tf_op jit(solution)/shard_map/pallas_call | solution.py:25
  66.7 5.0 %collective-permute-start = (bf16[2,512,512]{2,1,0:T(8,128)(2,1)}, bf16[2,512,512]{2,1,0:T(8,128)(2,1)}, u32[]{:S(2)}, u32[]{:S(2)}) collective-permute-start(bf16[2,512,512]{2,1,0:T(8,128)(2,1)} %get-tuple-element.17.refs_3_), channel_id=1, source_target_pairs={{1,2},{3,4},{5,6},{7,8},{9,10},{11,12},{13,14},{15,16},{17,18},{19... | collective-permute-start | bytes 3145736 | tf_op jit(solution)/shard_map/ppermute | solution.py:163
  71.7 2.7 %collective-permute-start.4 = (bf16[2,512,512]{2,1,0:T(8,128)(2,1)}, bf16[2,512,512]{2,1,0:T(8,128)(2,1)S(1)}, u32[]{:S(2)}, u32[]{:S(2)}) collective-permute-start(bf16[2,512,512]{2,1,0:T(8,128)(2,1)} %get-tuple-element.23.refs_3_), channel_id=1, source_target_pairs={{1,2},{3,4},{5,6},{7,8},{9,10},{11,12},{13,14},{15,16},{17,18},{19... | collective-permute-start | bytes 3145736 | tf_op jit(solution)/shard_map/ppermute | solution.py:163
  74.4 0.1 reshape.10.refs_1_
  74.5 0.1 pad_add_fusion.at.refs_0_
  74.6 1.4 copy-done.1
  76.0 1.0 shard_map.47
  77.0 8.2 %collective-permute-done.refs_2_ = bf16[2,512,512]{2,1,0:T(8,128)(2,1)} collective-permute-done((bf16[2,512,512]{2,1,0:T(8,128)(2,1)}, bf16[2,512,512]{2,1,0:T(8,128)(2,1)}, u32[]{:S(2)}, u32[]{:S(2)}) %collective-permute-start) | collective-permute-done | bytes 1048608 | tf_op jit(solution)/shard_map/ppermute | solution.py:163
  85.3 0.0 collective-permute-done.1.refs_4_
  85.3 6.5 %shard_map.48 = (bf16[2,160,512]{2,1,0:T(8,128)(2,1)S(1)}, bf16[2,160,512]{2,1,0:T(8,128)(2,1)S(1)}, bf16[2,160,512]{2,1,0:T(8,128)(2,1)S(1)}, bf16[2,32,512]{2,1,0:T(8,128)(2,1)S(1)}) custom-call(s32[3]{0:T(128)S(1)} %pad_add_fusion.at.refs_0_, s32[30]{0:T(128)S(1)} %reshape.10.refs_1_, bf16[2,512,512]{2,1,0:T(8,128)(2,1)} %collective-permute-done.refs_2_, ...), custom_call_target="tpu_custom_call" | custom-call | flops 3221225472 | bytes 8388608 | tf_op jit(solution)/shard_map/pallas_call | solution.py:129
  91.8 3.8 %collective-permute-start.2 = (bf16[2,160,512]{2,1,0:T(8,128)(2,1)S(1)}, bf16[2,160,512]{2,1,0:T(8,128)(2,1)S(1)}, u32[]{:S(2)}, u32[]{:S(2)}) collective-permute-start(bf16[2,160,512]{2,1,0:T(8,128)(2,1)S(1)} %get-tuple-element.21), channel_id=1, source_target_pairs={{0,32},{1,481},{2,34},{3,483},{4,36},{5,485},{6,38},{7,487},{8,40}... | collective-permute-start | bytes 983048 | tf_op jit(solution)/shard_map/ppermute | solution.py:150
  95.6 9.5 %collective-permute-start.3 = (bf16[2,160,512]{2,1,0:T(8,128)(2,1)S(1)}, bf16[2,160,512]{2,1,0:T(8,128)(2,1)S(1)}, u32[]{:S(2)}, u32[]{:S(2)}) collective-permute-start(bf16[2,160,512]{2,1,0:T(8,128)(2,1)S(1)} %get-tuple-element.22), channel_id=1, source_target_pairs={{0,480},{1,33},{2,482},{3,35},{4,484},{5,37},{6,486},{7,39},{8,488... | collective-permute-start | bytes 983048 | tf_op jit(solution)/shard_map/ppermute | solution.py:150
  105.1 0.0 collective-permute-done.4.refs_2_
  105.1 6.1 %shard_map.49 = (bf16[2,160,512]{2,1,0:T(8,128)(2,1)S(1)}, bf16[2,160,512]{2,1,0:T(8,128)(2,1)S(1)}, bf16[2,160,512]{2,1,0:T(8,128)(2,1)S(1)}, bf16[2,32,512]{2,1,0:T(8,128)(2,1)S(1)}) custom-call(s32[3]{0:T(128)S(1)} %pad_add_fusion.at.refs_0_, s32[30]{0:T(128)S(1)} %reshape.10.refs_1_, bf16[2,512,512]{2,1,0:T(8,128)(2,1)S(1)} %collective-permute-done.4.refs_2_, ...), custom_call_target="tpu_custom_call" | custom-call | flops 3221225472 | bytes 8388608 | tf_op jit(solution)/shard_map/pallas_call | solution.py:129
  111.3 1.9 %collective-permute-start.5 = (bf16[2,160,512]{2,1,0:T(8,128)(2,1)S(1)}, bf16[2,160,512]{2,1,0:T(8,128)(2,1)S(1)}, u32[]{:S(2)}, u32[]{:S(2)}) collective-permute-start(bf16[2,160,512]{2,1,0:T(8,128)(2,1)S(1)} %get-tuple-element.25), channel_id=1, source_target_pairs={{0,32},{1,481},{2,34},{3,483},{4,36},{5,485},{6,38},{7,487},{8,40}... | collective-permute-start | bytes 983048 | tf_op jit(solution)/shard_map/ppermute | solution.py:150
  113.2 5.1 %collective-permute-start.6 = (bf16[2,160,512]{2,1,0:T(8,128)(2,1)S(1)}, bf16[2,160,512]{2,1,0:T(8,128)(2,1)S(1)}, u32[]{:S(2)}, u32[]{:S(2)}) collective-permute-start(bf16[2,160,512]{2,1,0:T(8,128)(2,1)S(1)} %get-tuple-element.26), channel_id=1, source_target_pairs={{0,480},{1,33},{2,482},{3,35},{4,484},{5,37},{6,486},{7,39},{8,488... | collective-permute-start | bytes 983048 | tf_op jit(solution)/shard_map/ppermute | solution.py:150
  118.4 3.2 %collective-permute-start.7 = (bf16[2,2,32,512]{3,2,1,0:T(8,128)(2,1)S(1)}, bf16[2,2,32,512]{3,2,1,0:T(8,128)(2,1)S(1)}, u32[]{:S(2)}, u32[]{:S(2)}) collective-permute-start(bf16[2,2,32,512]{3,2,1,0:T(8,128)(2,1)S(1)} %pad_maximum_fusion), channel_id=1, source_target_pairs={{0,448},{1,65},{2,450},{3,67},{4,452},{5,69},{6,454},{7,71},{8,456... | collective-permute-start | bytes 393224 | tf_op jit(solution)/shard_map/ppermute | solution.py:150
  121.5 0.0 collective-permute-done.2
  121.6 0.1 convert_add_fusion.1
  121.7 1.2 collective-permute-done.5
  122.9 0.0 collective-permute-done.6
  122.9 0.1 convert_add_fusion
  123.2 3.1 %collective-permute-done.7 = bf16[2,2,32,512]{3,2,1,0:T(8,128)(2,1)S(1)} collective-permute-done((bf16[2,2,32,512]{3,2,1,0:T(8,128)(2,1)S(1)}, bf16[2,2,32,512]{3,2,1,0:T(8,128)(2,1)S(1)}, u32[]{:S(2)}, u32[]{:S(2)}) %collective-permute-start.7) | collective-permute-done | bytes 131104 | tf_op jit(solution)/shard_map/ppermute | solution.py:150
  126.3 3.7 %collective-permute-start.8 = (bf16[2,2,32,512]{3,2,1,0:T(8,128)(2,1)S(1)}, bf16[2,2,32,512]{3,2,1,0:T(8,128)(2,1)S(1)}, u32[]{:S(2)}, u32[]{:S(2)}) collective-permute-start(bf16[2,2,32,512]{3,2,1,0:T(8,128)(2,1)S(1)} %fusion.2), channel_id=1, source_target_pairs={{0,416},{1,97},{2,418},{3,99},{4,420},{5,101},{6,422},{7,103},{8,4... | collective-permute-start | bytes 393224 | tf_op jit(solution)/shard_map/ppermute | solution.py:150
  130.0 3.9 %collective-permute-start.10 = (bf16[2,2,32,512]{3,2,1,0:T(8,128)(2,1)S(1)}, bf16[2,2,32,512]{3,2,1,0:T(8,128)(2,1)S(1)}, u32[]{:S(2)}, u32[]{:S(2)}) collective-permute-start(bf16[2,2,32,512]{3,2,1,0:T(8,128)(2,1)S(1)} %pad_maximum_fusion.1), channel_id=1, source_target_pairs={{0,96},{1,417},{2,98},{3,419},{4,100},{5,421},{6,102},{7,423},{8,1... | collective-permute-start | bytes 393224 | tf_op jit(solution)/shard_map/ppermute | solution.py:150
  134.0 3.9 %collective-permute-done.8 = bf16[2,2,32,512]{3,2,1,0:T(8,128)(2,1)S(1)} collective-permute-done((bf16[2,2,32,512]{3,2,1,0:T(8,128)(2,1)S(1)}, bf16[2,2,32,512]{3,2,1,0:T(8,128)(2,1)S(1)}, u32[]{:S(2)}, u32[]{:S(2)}) %collective-permute-start.8) | collective-permute-done | bytes 131104 | tf_op jit(solution)/shard_map/ppermute | solution.py:150
  138.0 9.2 %collective-permute-start.9 = (bf16[2,2,32,512]{3,2,1,0:T(8,128)(2,1)S(1)}, bf16[2,2,32,512]{3,2,1,0:T(8,128)(2,1)S(1)}, u32[]{:S(2)}, u32[]{:S(2)}) collective-permute-start(bf16[2,2,32,512]{3,2,1,0:T(8,128)(2,1)S(1)} %fusion.1), channel_id=1, source_target_pairs={{0,416},{1,97},{2,418},{3,99},{4,420},{5,101},{6,422},{7,103},{8,4... | collective-permute-start | bytes 393224 | tf_op jit(solution)/shard_map/ppermute | solution.py:150
  147.3 2.3 %collective-permute-start.11 = (bf16[2,2,32,512]{3,2,1,0:T(8,128)(2,1)S(1)}, bf16[2,2,32,512]{3,2,1,0:T(8,128)(2,1)S(1)}, u32[]{:S(2)}, u32[]{:S(2)}) collective-permute-start(bf16[2,2,32,512]{3,2,1,0:T(8,128)(2,1)S(1)} %fusion.3), channel_id=1, source_target_pairs={{0,96},{1,417},{2,98},{3,419},{4,100},{5,421},{6,102},{7,423},{8,1... | collective-permute-start | bytes 393224 | tf_op jit(solution)/shard_map/ppermute | solution.py:150
  149.6 5.2 %collective-permute-done.9 = bf16[2,2,32,512]{3,2,1,0:T(8,128)(2,1)S(1)} collective-permute-done((bf16[2,2,32,512]{3,2,1,0:T(8,128)(2,1)S(1)}, bf16[2,2,32,512]{3,2,1,0:T(8,128)(2,1)S(1)}, u32[]{:S(2)}, u32[]{:S(2)}) %collective-permute-start.9) | collective-permute-done | bytes 131104 | tf_op jit(solution)/shard_map/ppermute | solution.py:150
  154.8 2.9 %collective-permute-done.11 = bf16[2,2,32,512]{3,2,1,0:T(8,128)(2,1)S(1)} collective-permute-done((bf16[2,2,32,512]{3,2,1,0:T(8,128)(2,1)S(1)}, bf16[2,2,32,512]{3,2,1,0:T(8,128)(2,1)S(1)}, u32[]{:S(2)}, u32[]{:S(2)}) %collective-permute-start.11) | collective-permute-done | bytes 131104 | tf_op jit(solution)/shard_map/ppermute | solution.py:150
  157.7 0.7 fusion
  (23 shorter events, 0.3 us)
Async XLA Ops:
  0.0 74.4 %copy-start.4 = (s32[3,2,5]{2,1,0:T(2,128)S(1)}, s32[3,2,5]{2,1,0:T(2,128)}, u32[]{:S(2)}) copy-start(s32[3,2,5]{2,1,0:T(2,128)} %param.7) | copy-start | bytes 364
  0.0 74.6 %copy-start = (bf16[3,512,512]{2,1,0:T(8,128)(2,1)S(1)}, bf16[3,512,512]{2,1,0:T(8,128)(2,1)}, u32[]{:S(2)}) copy-start(bf16[3,512,512]{2,1,0:T(8,128)(2,1)} %left.1) | copy-start | bytes 4718596
  0.0 85.3 %collective-permute-start.1 = (bf16[2,2,512,512]{3,2,1,0:T(8,128)(2,1)}, bf16[2,2,512,512]{3,2,1,0:T(8,128)(2,1)}, u32[]{:S(2)}, u32[]{:S(2)}) collective-permute-start(bf16[2,2,512,512]{3,2,1,0:T(8,128)(2,1)} %psi.1), channel_id=1, source_target_pairs={{0,1},{1,0},{2,3},{3,2},{4,5},{5,4},{6,7},{7,6},{8,9},{9,8},{10,11... | collective-permute-start | bytes 6291464 | tf_op jit(solution)/shard_map/ppermute | solution.py:164
  66.7 18.5 %collective-permute-start = (bf16[2,512,512]{2,1,0:T(8,128)(2,1)}, bf16[2,512,512]{2,1,0:T(8,128)(2,1)}, u32[]{:S(2)}, u32[]{:S(2)}) collective-permute-start(bf16[2,512,512]{2,1,0:T(8,128)(2,1)} %get-tuple-element.17.refs_3_), channel_id=1, source_target_pairs={{1,2},{3,4},{5,6},{7,8},{9,10},{11,12},{13,14},{15,16},{17,18},{19... | collective-permute-start | bytes 3145736 | tf_op jit(solution)/shard_map/ppermute | solution.py:163
  71.7 33.5 %collective-permute-start.4 = (bf16[2,512,512]{2,1,0:T(8,128)(2,1)}, bf16[2,512,512]{2,1,0:T(8,128)(2,1)S(1)}, u32[]{:S(2)}, u32[]{:S(2)}) collective-permute-start(bf16[2,512,512]{2,1,0:T(8,128)(2,1)} %get-tuple-element.23.refs_3_), channel_id=1, source_target_pairs={{1,2},{3,4},{5,6},{7,8},{9,10},{11,12},{13,14},{15,16},{17,18},{19... | collective-permute-start | bytes 3145736 | tf_op jit(solution)/shard_map/ppermute | solution.py:163
  74.6 1.4 copy-start.1
  76.0 9.3 %copy-start.3 = (bf16[2,512,512]{2,1,0:T(8,128)(2,1)S(1)}, bf16[2,512,512]{2,1,0:T(8,128)(2,1)}, u32[]{:S(2)}) copy-start(bf16[2,512,512]{2,1,0:T(8,128)(2,1)} %get-tuple-element.17.refs_3_) | copy-start | bytes 3145732
  85.3 19.9 %copy-start.2 = (bf16[2,512,512]{2,1,0:T(8,128)(2,1)S(1)}, bf16[2,512,512]{2,1,0:T(8,128)(2,1)}, u32[]{:S(2)}) copy-start(bf16[2,512,512]{2,1,0:T(8,128)(2,1)} %get-tuple-element.23.refs_3_) | copy-start | bytes 3145732
  91.8 29.8 %collective-permute-start.2 = (bf16[2,160,512]{2,1,0:T(8,128)(2,1)S(1)}, bf16[2,160,512]{2,1,0:T(8,128)(2,1)S(1)}, u32[]{:S(2)}, u32[]{:S(2)}) collective-permute-start(bf16[2,160,512]{2,1,0:T(8,128)(2,1)S(1)} %get-tuple-element.21), channel_id=1, source_target_pairs={{0,32},{1,481},{2,34},{3,483},{4,36},{5,485},{6,38},{7,487},{8,40}... | collective-permute-start | bytes 983048 | tf_op jit(solution)/shard_map/ppermute | solution.py:150
  95.6 25.9 %collective-permute-start.3 = (bf16[2,160,512]{2,1,0:T(8,128)(2,1)S(1)}, bf16[2,160,512]{2,1,0:T(8,128)(2,1)S(1)}, u32[]{:S(2)}, u32[]{:S(2)}) collective-permute-start(bf16[2,160,512]{2,1,0:T(8,128)(2,1)S(1)} %get-tuple-element.22), channel_id=1, source_target_pairs={{0,480},{1,33},{2,482},{3,35},{4,484},{5,37},{6,486},{7,39},{8,488... | collective-permute-start | bytes 983048 | tf_op jit(solution)/shard_map/ppermute | solution.py:150
  111.3 11.6 %collective-permute-start.5 = (bf16[2,160,512]{2,1,0:T(8,128)(2,1)S(1)}, bf16[2,160,512]{2,1,0:T(8,128)(2,1)S(1)}, u32[]{:S(2)}, u32[]{:S(2)}) collective-permute-start(bf16[2,160,512]{2,1,0:T(8,128)(2,1)S(1)} %get-tuple-element.25), channel_id=1, source_target_pairs={{0,32},{1,481},{2,34},{3,483},{4,36},{5,485},{6,38},{7,487},{8,40}... | collective-permute-start | bytes 983048 | tf_op jit(solution)/shard_map/ppermute | solution.py:150
  113.2 9.7 %collective-permute-start.6 = (bf16[2,160,512]{2,1,0:T(8,128)(2,1)S(1)}, bf16[2,160,512]{2,1,0:T(8,128)(2,1)S(1)}, u32[]{:S(2)}, u32[]{:S(2)}) collective-permute-start(bf16[2,160,512]{2,1,0:T(8,128)(2,1)S(1)} %get-tuple-element.26), channel_id=1, source_target_pairs={{0,480},{1,33},{2,482},{3,35},{4,484},{5,37},{6,486},{7,39},{8,488... | collective-permute-start | bytes 983048 | tf_op jit(solution)/shard_map/ppermute | solution.py:150
  118.4 7.9 %collective-permute-start.7 = (bf16[2,2,32,512]{3,2,1,0:T(8,128)(2,1)S(1)}, bf16[2,2,32,512]{3,2,1,0:T(8,128)(2,1)S(1)}, u32[]{:S(2)}, u32[]{:S(2)}) collective-permute-start(bf16[2,2,32,512]{3,2,1,0:T(8,128)(2,1)S(1)} %pad_maximum_fusion), channel_id=1, source_target_pairs={{0,448},{1,65},{2,450},{3,67},{4,452},{5,69},{6,454},{7,71},{8,456... | collective-permute-start | bytes 393224 | tf_op jit(solution)/shard_map/ppermute | solution.py:150
  126.3 11.7 %collective-permute-start.8 = (bf16[2,2,32,512]{3,2,1,0:T(8,128)(2,1)S(1)}, bf16[2,2,32,512]{3,2,1,0:T(8,128)(2,1)S(1)}, u32[]{:S(2)}, u32[]{:S(2)}) collective-permute-start(bf16[2,2,32,512]{3,2,1,0:T(8,128)(2,1)S(1)} %fusion.2), channel_id=1, source_target_pairs={{0,416},{1,97},{2,418},{3,99},{4,420},{5,101},{6,422},{7,103},{8,4... | collective-permute-start | bytes 393224 | tf_op jit(solution)/shard_map/ppermute | solution.py:150
  130.0 17.2 %collective-permute-start.10 = (bf16[2,2,32,512]{3,2,1,0:T(8,128)(2,1)S(1)}, bf16[2,2,32,512]{3,2,1,0:T(8,128)(2,1)S(1)}, u32[]{:S(2)}, u32[]{:S(2)}) collective-permute-start(bf16[2,2,32,512]{3,2,1,0:T(8,128)(2,1)S(1)} %pad_maximum_fusion.1), channel_id=1, source_target_pairs={{0,96},{1,417},{2,98},{3,419},{4,100},{5,421},{6,102},{7,423},{8,1... | collective-permute-start | bytes 393224 | tf_op jit(solution)/shard_map/ppermute | solution.py:150
  138.0 16.8 %collective-permute-start.9 = (bf16[2,2,32,512]{3,2,1,0:T(8,128)(2,1)S(1)}, bf16[2,2,32,512]{3,2,1,0:T(8,128)(2,1)S(1)}, u32[]{:S(2)}, u32[]{:S(2)}) collective-permute-start(bf16[2,2,32,512]{3,2,1,0:T(8,128)(2,1)S(1)} %fusion.1), channel_id=1, source_target_pairs={{0,416},{1,97},{2,418},{3,99},{4,420},{5,101},{6,422},{7,103},{8,4... | collective-permute-start | bytes 393224 | tf_op jit(solution)/shard_map/ppermute | solution.py:150
  147.3 10.4 %collective-permute-start.11 = (bf16[2,2,32,512]{3,2,1,0:T(8,128)(2,1)S(1)}, bf16[2,2,32,512]{3,2,1,0:T(8,128)(2,1)S(1)}, u32[]{:S(2)}, u32[]{:S(2)}) collective-permute-start(bf16[2,2,32,512]{3,2,1,0:T(8,128)(2,1)S(1)} %fusion.3), channel_id=1, source_target_pairs={{0,96},{1,417},{2,98},{3,419},{4,100},{5,421},{6,102},{7,423},{8,1... | collective-permute-start | bytes 393224 | tf_op jit(solution)/shard_map/ppermute | solution.py:150

commit v3 on v2

--- a/solution.py
+++ b/solution.py
@@ -25,10 +25,10 @@
     return pl.pallas_call(
         split_kernel,
         in_specs=[pl.BlockSpec(memory_space=pl.ANY)],
-        out_specs=[pl.BlockSpec(memory_space=pl.ANY)] * vectors,
+        out_specs=[pl.BlockSpec(memory_space=pltpu.VMEM)] * vectors,
         out_shape=[jax.ShapeDtypeStruct(psi.shape[1:], BF16)] * vectors,
         scratch_shapes=[pltpu.SemaphoreType.DMA((vectors,))],
-        compiler_params=pltpu.CompilerParams(vmem_limit_bytes=56 * 2**20),
+        compiler_params=pltpu.CompilerParams(vmem_limit_bytes=60 * 10**6),
         cost_estimate=pl.CostEstimate(flops=0, bytes_accessed=4 * 2**20, transcendentals=0),
     )(psi)
 

time: 160 us -> 98.6 us (0.62)
  the two profiles are of different devices: /device:TPU:24 before, /device:TPU:14 now
where the time goes in v3:
time: 98.6 us; the launch traced here: 98.1 us
  starting transfers between devices  46.4 us (47%)
  waiting for transfers between devices  31.9 us (32%)
  Pallas kernels  16.6 us (17%)
  local copies, waits for them, and re-layouts  1.71 us (2%)
  other arithmetic  1.18 us (1%)
    ppermute x9, starting transfers between devices, shift(): return lax.ppermute(x, ('op', 'sec'), pairs)  38.8 us
    ppermute x9, waiting for transfers between devices, shift(): return lax.ppermute(x, ('op', 'sec'), pairs)  23.7 us
    pallas_call x2, Pallas kernels, partials(): pl.pallas_call(lambda *refs: kernel(v, *refs), in_specs=[scalars, scalars...  12.6 us
    ppermute x2, waiting for transfers between devices, shards(): across = [lax.ppermute(block, 'sec', facing) for block in own]  8.21 us
    ppermute x2, starting transfers between devices, shards(): across = [lax.ppermute(block, 'sec', facing) for block in own]  5.56 us
    pallas_call x1, Pallas kernels, split(): pl.pallas_call(split_kernel, in_specs=[pl.BlockSpec(memory_space=pl.ANY)]...  2.87 us
    ppermute x1, starting transfers between devices, shards(): chip = lax.ppermute(psi, 'sec', [(i, i ^ 1) for i in range(count)])  2.04 us
  transfers between devices with their start and end apart: 12, of which 6 were waited for; matrix products, arithmetic and copies ran while one was open for 1% of the time, Pallas kernels for 17%

profile of v3, /device:TPU:14, one launch (start us, length us, event | category | flops | bytes accessed | tf_op | source)
XLA Modules:
  0.0 98.1 jit_solution(18418364481051177345)
XLA Ops:
  0.0 2.0 %collective-permute-start.1 = (bf16[2,2,512,512]{3,2,1,0:T(8,128)(2,1)}, bf16[2,2,512,512]{3,2,1,0:T(8,128)(2,1)}, u32[]{:S(2)}, u32[]{:S(2)}) collective-permute-start(bf16[2,2,512,512]{3,2,1,0:T(8,128)(2,1)} %psi.1), channel_id=1, source_target_pairs={{0,1},{1,0},{2,3},{3,2},{4,5},{5,4},{6,7},{7,6},{8,9},{9,8},{10,11... | collective-permute-start | bytes 6291464 | tf_op jit(solution)/shard_map/ppermute | solution.py:164
  2.1 2.9 %shard_map.46 = (bf16[2,512,512]{2,1,0:T(8,128)(2,1)}, bf16[2,512,512]{2,1,0:T(8,128)(2,1)}) custom-call(bf16[2,2,512,512]{3,2,1,0:T(8,128)(2,1)} %psi.1), custom_call_target="tpu_custom_call" | custom-call | bytes 4194304 | tf_op jit(solution)/shard_map/pallas_call | solution.py:25
  4.9 2.8 %collective-permute-start = (bf16[2,512,512]{2,1,0:T(8,128)(2,1)}, bf16[2,512,512]{2,1,0:T(8,128)(2,1)}, u32[]{:S(2)}, u32[]{:S(2)}) collective-permute-start(bf16[2,512,512]{2,1,0:T(8,128)(2,1)} %get-tuple-element.17.refs_3_), channel_id=1, source_target_pairs={{1,2},{3,4},{5,6},{7,8},{9,10},{11,12},{13,14},{15,16},{17,18},{19... | collective-permute-start | bytes 3145736 | tf_op jit(solution)/shard_map/ppermute | solution.py:163
  7.8 2.7 %collective-permute-start.4 = (bf16[2,512,512]{2,1,0:T(8,128)(2,1)}, bf16[2,512,512]{2,1,0:T(8,128)(2,1)S(1)}, u32[]{:S(2)}, u32[]{:S(2)}) collective-permute-start(bf16[2,512,512]{2,1,0:T(8,128)(2,1)} %get-tuple-element.23.refs_3_), channel_id=1, source_target_pairs={{1,2},{3,4},{5,6},{7,8},{9,10},{11,12},{13,14},{15,16},{17,18},{19... | collective-permute-start | bytes 3145736 | tf_op jit(solution)/shard_map/ppermute | solution.py:163
  10.5 0.1 reshape.10.refs_1_
  10.6 0.1 pad_add_fusion.at.refs_0_
  10.7 1.4 %copy-done.1 = bf16[3,512,512]{2,1,0:T(8,128)(2,1)S(1)} copy-done((bf16[3,512,512]{2,1,0:T(8,128)(2,1)S(1)}, bf16[3,512,512]{2,1,0:T(8,128)(2,1)}, u32[]{:S(2)}) %copy-start.1) | copy-done | bytes 1572888
  12.1 1.0 %shard_map.47 = (bf16[512,1536]{1,0:T(8,128)(2,1)S(1)}, bf16[3,512,512]{2,1,0:T(8,128)(2,1)S(1)}) custom-call(s32[3]{0:T(128)S(1)} %pad_add_fusion.at.refs_0_, bf16[3,512,512]{2,1,0:T(8,128)(2,1)S(1)} %copy-done, bf16[3,512,512]{2,1,0:T(8,128)(2,1)S(1)} %copy-done.1), custom_call_target="tpu_custom_call" | custom-call | bytes 6291456 | tf_op jit(solution)/shard_map/pallas_call | solution.py:53
  13.2 8.2 %collective-permute-done.refs_2_ = bf16[2,512,512]{2,1,0:T(8,128)(2,1)} collective-permute-done((bf16[2,512,512]{2,1,0:T(8,128)(2,1)}, bf16[2,512,512]{2,1,0:T(8,128)(2,1)}, u32[]{:S(2)}, u32[]{:S(2)}) %collective-permute-start) | collective-permute-done | bytes 1048608 | tf_op jit(solution)/shard_map/ppermute | solution.py:163
  21.4 0.0 collective-permute-done.1.refs_4_
  21.4 6.5 %shard_map.48 = (bf16[2,160,512]{2,1,0:T(8,128)(2,1)S(1)}, bf16[2,160,512]{2,1,0:T(8,128)(2,1)S(1)}, bf16[2,160,512]{2,1,0:T(8,128)(2,1)S(1)}, bf16[2,32,512]{2,1,0:T(8,128)(2,1)S(1)}) custom-call(s32[3]{0:T(128)S(1)} %pad_add_fusion.at.refs_0_, s32[30]{0:T(128)S(1)} %reshape.10.refs_1_, bf16[2,512,512]{2,1,0:T(8,128)(2,1)} %collective-permute-done.refs_2_, ...), custom_call_target="tpu_custom_call" | custom-call | flops 3221225472 | bytes 8388608 | tf_op jit(solution)/shard_map/pallas_call | solution.py:129
  27.9 3.8 %collective-permute-start.2 = (bf16[2,160,512]{2,1,0:T(8,128)(2,1)S(1)}, bf16[2,160,512]{2,1,0:T(8,128)(2,1)S(1)}, u32[]{:S(2)}, u32[]{:S(2)}) collective-permute-start(bf16[2,160,512]{2,1,0:T(8,128)(2,1)S(1)} %get-tuple-element.21), channel_id=1, source_target_pairs={{0,32},{1,481},{2,34},{3,483},{4,36},{5,485},{6,38},{7,487},{8,40}... | collective-permute-start | bytes 983048 | tf_op jit(solution)/shard_map/ppermute | solution.py:150
  31.7 9.5 %collective-permute-start.3 = (bf16[2,160,512]{2,1,0:T(8,128)(2,1)S(1)}, bf16[2,160,512]{2,1,0:T(8,128)(2,1)S(1)}, u32[]{:S(2)}, u32[]{:S(2)}) collective-permute-start(bf16[2,160,512]{2,1,0:T(8,128)(2,1)S(1)} %get-tuple-element.22), channel_id=1, source_target_pairs={{0,480},{1,33},{2,482},{3,35},{4,484},{5,37},{6,486},{7,39},{8,488... | collective-permute-start | bytes 983048 | tf_op jit(solution)/shard_map/ppermute | solution.py:150
  41.2 0.0 collective-permute-done.4.refs_2_
  41.3 6.1 %shard_map.49 = (bf16[2,160,512]{2,1,0:T(8,128)(2,1)S(1)}, bf16[2,160,512]{2,1,0:T(8,128)(2,1)S(1)}, bf16[2,160,512]{2,1,0:T(8,128)(2,1)S(1)}, bf16[2,32,512]{2,1,0:T(8,128)(2,1)S(1)}) custom-call(s32[3]{0:T(128)S(1)} %pad_add_fusion.at.refs_0_, s32[30]{0:T(128)S(1)} %reshape.10.refs_1_, bf16[2,512,512]{2,1,0:T(8,128)(2,1)S(1)} %collective-permute-done.4.refs_2_, ...), custom_call_target="tpu_custom_call" | custom-call | flops 3221225472 | bytes 8388608 | tf_op jit(solution)/shard_map/pallas_call | solution.py:129
  47.4 1.9 %collective-permute-start.5 = (bf16[2,160,512]{2,1,0:T(8,128)(2,1)S(1)}, bf16[2,160,512]{2,1,0:T(8,128)(2,1)S(1)}, u32[]{:S(2)}, u32[]{:S(2)}) collective-permute-start(bf16[2,160,512]{2,1,0:T(8,128)(2,1)S(1)} %get-tuple-element.25), channel_id=1, source_target_pairs={{0,32},{1,481},{2,34},{3,483},{4,36},{5,485},{6,38},{7,487},{8,40}... | collective-permute-start | bytes 983048 | tf_op jit(solution)/shard_map/ppermute | solution.py:150
  49.3 5.1 %collective-permute-start.6 = (bf16[2,160,512]{2,1,0:T(8,128)(2,1)S(1)}, bf16[2,160,512]{2,1,0:T(8,128)(2,1)S(1)}, u32[]{:S(2)}, u32[]{:S(2)}) collective-permute-start(bf16[2,160,512]{2,1,0:T(8,128)(2,1)S(1)} %get-tuple-element.26), channel_id=1, source_target_pairs={{0,480},{1,33},{2,482},{3,35},{4,484},{5,37},{6,486},{7,39},{8,488... | collective-permute-start | bytes 983048 | tf_op jit(solution)/shard_map/ppermute | solution.py:150
  54.5 3.2 %collective-permute-start.7 = (bf16[2,2,32,512]{3,2,1,0:T(8,128)(2,1)S(1)}, bf16[2,2,32,512]{3,2,1,0:T(8,128)(2,1)S(1)}, u32[]{:S(2)}, u32[]{:S(2)}) collective-permute-start(bf16[2,2,32,512]{3,2,1,0:T(8,128)(2,1)S(1)} %pad_maximum_fusion), channel_id=1, source_target_pairs={{0,448},{1,65},{2,450},{3,67},{4,452},{5,69},{6,454},{7,71},{8,456... | collective-permute-start | bytes 393224 | tf_op jit(solution)/shard_map/ppermute | solution.py:150
  57.7 0.0 collective-permute-done.3
  57.7 0.1 convert_add_fusion.1
  57.9 0.0 collective-permute-done.5
  57.9 4.8 %collective-permute-done.6 = bf16[2,160,512]{2,1,0:T(8,128)(2,1)S(1)} collective-permute-done((bf16[2,160,512]{2,1,0:T(8,128)(2,1)S(1)}, bf16[2,160,512]{2,1,0:T(8,128)(2,1)S(1)}, u32[]{:S(2)}, u32[]{:S(2)}) %collective-permute-start.6) | collective-permute-done | bytes 327712 | tf_op jit(solution)/shard_map/ppermute | solution.py:150
  62.7 0.1 convert_add_fusion
  62.9 1.6 %collective-permute-done.7 = bf16[2,2,32,512]{3,2,1,0:T(8,128)(2,1)S(1)} collective-permute-done((bf16[2,2,32,512]{3,2,1,0:T(8,128)(2,1)S(1)}, bf16[2,2,32,512]{3,2,1,0:T(8,128)(2,1)S(1)}, u32[]{:S(2)}, u32[]{:S(2)}) %collective-permute-start.7) | collective-permute-done | bytes 131104 | tf_op jit(solution)/shard_map/ppermute | solution.py:150
  64.6 3.7 %collective-permute-start.8 = (bf16[2,2,32,512]{3,2,1,0:T(8,128)(2,1)S(1)}, bf16[2,2,32,512]{3,2,1,0:T(8,128)(2,1)S(1)}, u32[]{:S(2)}, u32[]{:S(2)}) collective-permute-start(bf16[2,2,32,512]{3,2,1,0:T(8,128)(2,1)S(1)} %fusion.2), channel_id=1, source_target_pairs={{0,416},{1,97},{2,418},{3,99},{4,420},{5,101},{6,422},{7,103},{8,4... | collective-permute-start | bytes 393224 | tf_op jit(solution)/shard_map/ppermute | solution.py:150
  68.3 3.9 %collective-permute-start.10 = (bf16[2,2,32,512]{3,2,1,0:T(8,128)(2,1)S(1)}, bf16[2,2,32,512]{3,2,1,0:T(8,128)(2,1)S(1)}, u32[]{:S(2)}, u32[]{:S(2)}) collective-permute-start(bf16[2,2,32,512]{3,2,1,0:T(8,128)(2,1)S(1)} %pad_maximum_fusion.1), channel_id=1, source_target_pairs={{0,96},{1,417},{2,98},{3,419},{4,100},{5,421},{6,102},{7,423},{8,1... | collective-permute-start | bytes 393224 | tf_op jit(solution)/shard_map/ppermute | solution.py:150
  72.3 7.5 %collective-permute-done.8 = bf16[2,2,32,512]{3,2,1,0:T(8,128)(2,1)S(1)} collective-permute-done((bf16[2,2,32,512]{3,2,1,0:T(8,128)(2,1)S(1)}, bf16[2,2,32,512]{3,2,1,0:T(8,128)(2,1)S(1)}, u32[]{:S(2)}, u32[]{:S(2)}) %collective-permute-start.8) | collective-permute-done | bytes 131104 | tf_op jit(solution)/shard_map/ppermute | solution.py:150
  79.8 5.3 %collective-permute-start.9 = (bf16[2,2,32,512]{3,2,1,0:T(8,128)(2,1)S(1)}, bf16[2,2,32,512]{3,2,1,0:T(8,128)(2,1)S(1)}, u32[]{:S(2)}, u32[]{:S(2)}) collective-permute-start(bf16[2,2,32,512]{3,2,1,0:T(8,128)(2,1)S(1)} %fusion.1), channel_id=1, source_target_pairs={{0,416},{1,97},{2,418},{3,99},{4,420},{5,101},{6,422},{7,103},{8,4... | collective-permute-start | bytes 393224 | tf_op jit(solution)/shard_map/ppermute | solution.py:150
  85.1 2.3 %collective-permute-start.11 = (bf16[2,2,32,512]{3,2,1,0:T(8,128)(2,1)S(1)}, bf16[2,2,32,512]{3,2,1,0:T(8,128)(2,1)S(1)}, u32[]{:S(2)}, u32[]{:S(2)}) collective-permute-start(bf16[2,2,32,512]{3,2,1,0:T(8,128)(2,1)S(1)} %fusion.3), channel_id=1, source_target_pairs={{0,96},{1,417},{2,98},{3,419},{4,100},{5,421},{6,102},{7,423},{8,1... | collective-permute-start | bytes 393224 | tf_op jit(solution)/shard_map/ppermute | solution.py:150
  87.5 6.7 %collective-permute-done.9 = bf16[2,2,32,512]{3,2,1,0:T(8,128)(2,1)S(1)} collective-permute-done((bf16[2,2,32,512]{3,2,1,0:T(8,128)(2,1)S(1)}, bf16[2,2,32,512]{3,2,1,0:T(8,128)(2,1)S(1)}, u32[]{:S(2)}, u32[]{:S(2)}) %collective-permute-start.9) | collective-permute-done | bytes 131104 | tf_op jit(solution)/shard_map/ppermute | solution.py:150
  94.2 3.2 %collective-permute-done.11 = bf16[2,2,32,512]{3,2,1,0:T(8,128)(2,1)S(1)} collective-permute-done((bf16[2,2,32,512]{3,2,1,0:T(8,128)(2,1)S(1)}, bf16[2,2,32,512]{3,2,1,0:T(8,128)(2,1)S(1)}, u32[]{:S(2)}, u32[]{:S(2)}) %collective-permute-start.11) | collective-permute-done | bytes 131104 | tf_op jit(solution)/shard_map/ppermute | solution.py:150
  97.3 0.7 fusion
  (23 shorter events, 0.3 us)
Async XLA Ops:
  0.0 10.5 %copy-start.4 = (s32[3,2,5]{2,1,0:T(2,128)S(1)}, s32[3,2,5]{2,1,0:T(2,128)}, u32[]{:S(2)}) copy-start(s32[3,2,5]{2,1,0:T(2,128)} %param.7) | copy-start | bytes 364
  0.0 10.7 %copy-start = (bf16[3,512,512]{2,1,0:T(8,128)(2,1)S(1)}, bf16[3,512,512]{2,1,0:T(8,128)(2,1)}, u32[]{:S(2)}) copy-start(bf16[3,512,512]{2,1,0:T(8,128)(2,1)} %left.1) | copy-start | bytes 4718596
  0.0 21.4 %collective-permute-start.1 = (bf16[2,2,512,512]{3,2,1,0:T(8,128)(2,1)}, bf16[2,2,512,512]{3,2,1,0:T(8,128)(2,1)}, u32[]{:S(2)}, u32[]{:S(2)}) collective-permute-start(bf16[2,2,512,512]{3,2,1,0:T(8,128)(2,1)} %psi.1), channel_id=1, source_target_pairs={{0,1},{1,0},{2,3},{3,2},{4,5},{5,4},{6,7},{7,6},{8,9},{9,8},{10,11... | collective-permute-start | bytes 6291464 | tf_op jit(solution)/shard_map/ppermute | solution.py:164
  4.9 16.4 %collective-permute-start = (bf16[2,512,512]{2,1,0:T(8,128)(2,1)}, bf16[2,512,512]{2,1,0:T(8,128)(2,1)}, u32[]{:S(2)}, u32[]{:S(2)}) collective-permute-start(bf16[2,512,512]{2,1,0:T(8,128)(2,1)} %get-tuple-element.17.refs_3_), channel_id=1, source_target_pairs={{1,2},{3,4},{5,6},{7,8},{9,10},{11,12},{13,14},{15,16},{17,18},{19... | collective-permute-start | bytes 3145736 | tf_op jit(solution)/shard_map/ppermute | solution.py:163
  7.8 33.5 %collective-permute-start.4 = (bf16[2,512,512]{2,1,0:T(8,128)(2,1)}, bf16[2,512,512]{2,1,0:T(8,128)(2,1)S(1)}, u32[]{:S(2)}, u32[]{:S(2)}) collective-permute-start(bf16[2,512,512]{2,1,0:T(8,128)(2,1)} %get-tuple-element.23.refs_3_), channel_id=1, source_target_pairs={{1,2},{3,4},{5,6},{7,8},{9,10},{11,12},{13,14},{15,16},{17,18},{19... | collective-permute-start | bytes 3145736 | tf_op jit(solution)/shard_map/ppermute | solution.py:163
  10.7 1.4 %copy-start.1 = (bf16[3,512,512]{2,1,0:T(8,128)(2,1)S(1)}, bf16[3,512,512]{2,1,0:T(8,128)(2,1)}, u32[]{:S(2)}) copy-start(bf16[3,512,512]{2,1,0:T(8,128)(2,1)} %right.1) | copy-start | bytes 4718596
  12.1 9.3 %copy-start.3 = (bf16[2,512,512]{2,1,0:T(8,128)(2,1)S(1)}, bf16[2,512,512]{2,1,0:T(8,128)(2,1)}, u32[]{:S(2)}) copy-start(bf16[2,512,512]{2,1,0:T(8,128)(2,1)} %get-tuple-element.17.refs_3_) | copy-start | bytes 3145732
  21.4 19.9 %copy-start.2 = (bf16[2,512,512]{2,1,0:T(8,128)(2,1)S(1)}, bf16[2,512,512]{2,1,0:T(8,128)(2,1)}, u32[]{:S(2)}) copy-start(bf16[2,512,512]{2,1,0:T(8,128)(2,1)} %get-tuple-element.23.refs_3_) | copy-start | bytes 3145732
  27.9 29.8 %collective-permute-start.2 = (bf16[2,160,512]{2,1,0:T(8,128)(2,1)S(1)}, bf16[2,160,512]{2,1,0:T(8,128)(2,1)S(1)}, u32[]{:S(2)}, u32[]{:S(2)}) collective-permute-start(bf16[2,160,512]{2,1,0:T(8,128)(2,1)S(1)} %get-tuple-element.21), channel_id=1, source_target_pairs={{0,32},{1,481},{2,34},{3,483},{4,36},{5,485},{6,38},{7,487},{8,40}... | collective-permute-start | bytes 983048 | tf_op jit(solution)/shard_map/ppermute | solution.py:150
  31.7 26.0 %collective-permute-start.3 = (bf16[2,160,512]{2,1,0:T(8,128)(2,1)S(1)}, bf16[2,160,512]{2,1,0:T(8,128)(2,1)S(1)}, u32[]{:S(2)}, u32[]{:S(2)}) collective-permute-start(bf16[2,160,512]{2,1,0:T(8,128)(2,1)S(1)} %get-tuple-element.22), channel_id=1, source_target_pairs={{0,480},{1,33},{2,482},{3,35},{4,484},{5,37},{6,486},{7,39},{8,488... | collective-permute-start | bytes 983048 | tf_op jit(solution)/shard_map/ppermute | solution.py:150
  47.4 10.5 %collective-permute-start.5 = (bf16[2,160,512]{2,1,0:T(8,128)(2,1)S(1)}, bf16[2,160,512]{2,1,0:T(8,128)(2,1)S(1)}, u32[]{:S(2)}, u32[]{:S(2)}) collective-permute-start(bf16[2,160,512]{2,1,0:T(8,128)(2,1)S(1)} %get-tuple-element.25), channel_id=1, source_target_pairs={{0,32},{1,481},{2,34},{3,483},{4,36},{5,485},{6,38},{7,487},{8,40}... | collective-permute-start | bytes 983048 | tf_op jit(solution)/shard_map/ppermute | solution.py:150
  49.3 13.3 %collective-permute-start.6 = (bf16[2,160,512]{2,1,0:T(8,128)(2,1)S(1)}, bf16[2,160,512]{2,1,0:T(8,128)(2,1)S(1)}, u32[]{:S(2)}, u32[]{:S(2)}) collective-permute-start(bf16[2,160,512]{2,1,0:T(8,128)(2,1)S(1)} %get-tuple-element.26), channel_id=1, source_target_pairs={{0,480},{1,33},{2,482},{3,35},{4,484},{5,37},{6,486},{7,39},{8,488... | collective-permute-start | bytes 983048 | tf_op jit(solution)/shard_map/ppermute | solution.py:150
  54.5 10.0 %collective-permute-start.7 = (bf16[2,2,32,512]{3,2,1,0:T(8,128)(2,1)S(1)}, bf16[2,2,32,512]{3,2,1,0:T(8,128)(2,1)S(1)}, u32[]{:S(2)}, u32[]{:S(2)}) collective-permute-start(bf16[2,2,32,512]{3,2,1,0:T(8,128)(2,1)S(1)} %pad_maximum_fusion), channel_id=1, source_target_pairs={{0,448},{1,65},{2,450},{3,67},{4,452},{5,69},{6,454},{7,71},{8,456... | collective-permute-start | bytes 393224 | tf_op jit(solution)/shard_map/ppermute | solution.py:150
  64.6 15.2 %collective-permute-start.8 = (bf16[2,2,32,512]{3,2,1,0:T(8,128)(2,1)S(1)}, bf16[2,2,32,512]{3,2,1,0:T(8,128)(2,1)S(1)}, u32[]{:S(2)}, u32[]{:S(2)}) collective-permute-start(bf16[2,2,32,512]{3,2,1,0:T(8,128)(2,1)S(1)} %fusion.2), channel_id=1, source_target_pairs={{0,416},{1,97},{2,418},{3,99},{4,420},{5,101},{6,422},{7,103},{8,4... | collective-permute-start | bytes 393224 | tf_op jit(solution)/shard_map/ppermute | solution.py:150
  68.3 16.8 %collective-permute-start.10 = (bf16[2,2,32,512]{3,2,1,0:T(8,128)(2,1)S(1)}, bf16[2,2,32,512]{3,2,1,0:T(8,128)(2,1)S(1)}, u32[]{:S(2)}, u32[]{:S(2)}) collective-permute-start(bf16[2,2,32,512]{3,2,1,0:T(8,128)(2,1)S(1)} %pad_maximum_fusion.1), channel_id=1, source_target_pairs={{0,96},{1,417},{2,98},{3,419},{4,100},{5,421},{6,102},{7,423},{8,1... | collective-permute-start | bytes 393224 | tf_op jit(solution)/shard_map/ppermute | solution.py:150
  79.8 14.4 %collective-permute-start.9 = (bf16[2,2,32,512]{3,2,1,0:T(8,128)(2,1)S(1)}, bf16[2,2,32,512]{3,2,1,0:T(8,128)(2,1)S(1)}, u32[]{:S(2)}, u32[]{:S(2)}) collective-permute-start(bf16[2,2,32,512]{3,2,1,0:T(8,128)(2,1)S(1)} %fusion.1), channel_id=1, source_target_pairs={{0,416},{1,97},{2,418},{3,99},{4,420},{5,101},{6,422},{7,103},{8,4... | collective-permute-start | bytes 393224 | tf_op jit(solution)/shard_map/ppermute | solution.py:150
  85.1 12.2 %collective-permute-start.11 = (bf16[2,2,32,512]{3,2,1,0:T(8,128)(2,1)S(1)}, bf16[2,2,32,512]{3,2,1,0:T(8,128)(2,1)S(1)}, u32[]{:S(2)}, u32[]{:S(2)}) collective-permute-start(bf16[2,2,32,512]{3,2,1,0:T(8,128)(2,1)S(1)} %fusion.3), channel_id=1, source_target_pairs={{0,96},{1,417},{2,98},{3,419},{4,100},{5,421},{6,102},{7,423},{8,1... | collective-permute-start | bytes 393224 | tf_op jit(solution)/shard_map/ppermute | solution.py:150

commit v4 on v3

--- a/solution.py
+++ b/solution.py
@@ -1,3 +1,5 @@
+import functools
+
 import jax
 import jax.numpy as jnp
 from jax import lax
@@ -7,8 +9,9 @@
 
 F32, BF16 = jnp.float32, jnp.bfloat16
 RING = 16
-LEADERS = (0, 3, -3, 6, -6)
-ORDER = [1 - p for p in LEADERS] + [-1 - p for p in LEADERS] + [-p for p in LEADERS] + [8]
+LEADERS = (0, 4, -3, 7, -6)
+SPARE = 2
+ORDER = [1 - p for p in LEADERS] + [-1 - p for p in LEADERS] + [-p for p in LEADERS] + [-SPARE]
 
 
 def split_kernel(psi, *rest):
@@ -63,7 +66,12 @@
     )(at, left, right)
 
 
-def kernel(v, place, link, across, own, chip, right, left, up, down, mine, opposite, combined, halved):
+def kernel(v, place, link, across, own, chip, right, left, *rest):
+    earlier, outs, (combined, halved) = rest[: 2 * v], rest[2 * v : -2], rest[-2:]
+    up, down, mine, spare = outs
+    if v:
+        down[0], spare[0] = earlier[0][...], earlier[1][...]
+        down, spare = down.at[1], spare.at[1]
     terms, size = right.shape[0], right.shape[1]
     first_core = place[0] % 2 == 0
     lowest, highest = place[0] == 0, place[0] == place[1] - 1
@@ -112,7 +120,7 @@
                 left[pl.ds(top, high), :], halved[j], preferred_element_type=F32
             ).astype(BF16)
             start = 0
-            for out in (up, down, mine, opposite):
+            for out in (up, down, mine, spare):
                 end = start + out.shape[1]
                 low, stop = max(top, start), min(top + high, end)
                 if low < stop:
@@ -120,17 +128,19 @@
                 start = end
 
 
-def partials(v, place, link, across, own, chip, right, left):
+def partials(v, place, link, across, own, chip, right, left, earlier=()):
     terms, size = right.shape[0], right.shape[1]
     share = size // RING
     whole = pl.BlockSpec(memory_space=pltpu.VMEM)
     scalars = pl.BlockSpec(memory_space=pltpu.SMEM)
-    counts = [len(LEADERS)] * 3 + [1]
+    many, one = (2, len(LEADERS) * share, size), (2, share, size)
+    both = (2,) * v
+    shapes = [many, both + many, many, both + one]
     return pl.pallas_call(
-        lambda *refs: kernel(v, *refs),
-        in_specs=[scalars, scalars] + [whole] * 5,
+        functools.partial(kernel, v),
+        in_specs=[scalars, scalars] + [whole] * (5 + len(earlier)),
         out_specs=[whole] * 4,
-        out_shape=[jax.ShapeDtypeStruct((2, n * share, size), BF16) for n in counts],
+        out_shape=[jax.ShapeDtypeStruct(shape, BF16) for shape in shapes],
         scratch_shapes=[
             pltpu.VMEM((2, 2 * terms, size // 2, size), BF16),
             pltpu.VMEM((2, terms * size, size), BF16),
@@ -139,7 +149,7 @@
         cost_estimate=pl.CostEstimate(
             flops=8 * terms * size**3, bytes_accessed=8 * 2**20, transcendentals=0
         ),
-    )(place, link, across, own, chip, right, left)
+    )(place, link, across, own, chip, right, left, *earlier)
 
 
 def shift(x, by):
@@ -153,7 +163,6 @@
 def shards(psi, left_op, right_op, link):
     place = lax.axis_index("sec")
     count = lax.axis_size("sec")
-    vectors = psi.shape[0]
     share = psi.shape[2] // RING
     at = jnp.stack([place, count, lax.axis_index("op")]).astype(jnp.int32)
 
@@ -164,23 +173,23 @@
     chip = lax.ppermute(psi, "sec", [(i, i ^ 1) for i in range(count)])
 
     left, right = arrange(at, left_op, right_op)
-    totals, opposites = [], []
-    for v in range(vectors):
-        up, down, mine, opposite = partials(
-            v, at, link.reshape(-1), across[v], own[v], chip, right, left
-        )
-        total = mine.astype(F32) + shift(up, 1).astype(F32) + shift(down, -1).astype(F32)
-        totals.append(total.reshape(2, len(LEADERS), share, -1))
-        opposites.append(opposite)
-    opposite = shift(jnp.stack(opposites), -2).astype(F32)
-    here, above, below, far_above, far_below = (
-        jnp.stack([total[:, i] for total in totals]) for i in range(len(LEADERS))
+    link = link.reshape(-1)
+    up0, down, mine0, spare = partials(0, at, link, across[0], own[0], chip, right, left)
+    up0 = shift(up0, 1)
+    up1, down, mine1, spare = partials(
+        1, at, link, across[1], own[1], chip, right, left, (down, spare)
     )
-    far_above = shift((far_above + opposite).astype(BF16), -3).astype(F32)
-    far_below = shift(far_below.astype(BF16), 3).astype(F32)
-    above = shift((above + far_above).astype(BF16), -3).astype(F32)
-    below = shift((below + far_below).astype(BF16), 3).astype(F32)
-    return here + above + below
+    up1 = shift(up1, 1)
+    down = shift(down, -1)
+    spare = shift(spare, -SPARE)
+    total = jnp.stack(
+        [x.astype(F32) + y.astype(F32) + z.astype(F32) for x, y, z in ((mine0, up0, down[0]), (mine1, up1, down[1]))]
+    ).reshape(2, 2, len(LEADERS), share, -1)
+    far_above = shift(total[:, :, 3].astype(BF16), -3).astype(F32)
+    far_below = shift(total[:, :, 4].astype(BF16), 3).astype(F32)
+    above = shift((total[:, :, 1] + far_above).astype(BF16), -4).astype(F32)
+    below = shift((total[:, :, 2] + far_below).astype(BF16), 3).astype(F32)
+    return total[:, :, 0] + spare.astype(F32) + above + below
 
 
 def solution(mesh):

time: 98.6 us -> 104 us (1.055)
  the two profiles are of different devices: /device:TPU:14 before, /device:TPU:7 now
where the time goes in v4:
time: 104 us
  starting transfers between devices  46 us (44%)
  waiting for transfers between devices  38.2 us (37%)
  Pallas kernels  16.6 us (16%)
  local copies, waits for them, and re-layouts  1.51 us (1%)
  other arithmetic  1.2 us (1%)
    ppermute x8, starting transfers between devices, shift(): return lax.ppermute(x, ('op', 'sec'), pairs)  35.6 us
    ppermute x8, waiting for transfers between devices, shift(): return lax.ppermute(x, ('op', 'sec'), pairs)  25.4 us
    ppermute x2, waiting for transfers between devices, shards(): across = [lax.ppermute(block, 'sec', facing) for block in own]  12.8 us
    pallas_call x2, Pallas kernels, partials(): pl.pallas_call(functools.partial(kernel, v), in_specs=[scalars, scalars]...  12.7 us
    ppermute x2, starting transfers between devices, shards(): across = [lax.ppermute(block, 'sec', facing) for block in own]  7.67 us
    pallas_call x1, Pallas kernels, split(): pl.pallas_call(split_kernel, in_specs=[pl.BlockSpec(memory_space=pl.ANY)]...  2.88 us
    ppermute x1, starting transfers between devices, shards(): chip = lax.ppermute(psi, 'sec', [(i, i ^ 1) for i in range(count)])  2.7 us
  transfers between devices with their start and end apart: 11, of which 7 were waited for; matrix products, arithmetic and copies ran while one was open for 0% of the time, Pallas kernels for 10%

profile of v4, /device:TPU:7, one launch (start us, length us, event | category | flops | bytes accessed | tf_op | source)
XLA Modules:
  0.0 103.7 jit_solution(4832183170168993676)
XLA Ops:
  0.0 2.7 %collective-permute-start.1 = (bf16[2,2,512,512]{3,2,1,0:T(8,128)(2,1)}, bf16[2,2,512,512]{3,2,1,0:T(8,128)(2,1)}, u32[]{:S(2)}, u32[]{:S(2)}) collective-permute-start(bf16[2,2,512,512]{3,2,1,0:T(8,128)(2,1)} %psi.1), channel_id=1, source_target_pairs={{0,1},{1,0},{2,3},{3,2},{4,5},{5,4},{6,7},{7,6},{8,9},{9,8},{10,11... | collective-permute-start | bytes 6291464 | tf_op jit(solution)/shard_map/ppermute | solution.py:173
  2.7 2.9 %shard_map.46 = (bf16[2,512,512]{2,1,0:T(8,128)(2,1)}, bf16[2,512,512]{2,1,0:T(8,128)(2,1)}) custom-call(bf16[2,2,512,512]{3,2,1,0:T(8,128)(2,1)} %psi.1), custom_call_target="tpu_custom_call" | custom-call | bytes 4194304 | tf_op jit(solution)/shard_map/pallas_call | solution.py:28
  5.6 3.0 %collective-permute-start = (bf16[2,512,512]{2,1,0:T(8,128)(2,1)}, bf16[2,512,512]{2,1,0:T(8,128)(2,1)}, u32[]{:S(2)}, u32[]{:S(2)}) collective-permute-start(bf16[2,512,512]{2,1,0:T(8,128)(2,1)} %get-tuple-element.17.own), channel_id=1, source_target_pairs={{1,2},{3,4},{5,6},{7,8},{9,10},{11,12},{13,14},{15,16},{17,18},{19... | collective-permute-start | bytes 3145736 | tf_op jit(solution)/shard_map/ppermute | solution.py:172
  8.6 4.7 %collective-permute-start.3 = (bf16[2,512,512]{2,1,0:T(8,128)(2,1)}, bf16[2,512,512]{2,1,0:T(8,128)(2,1)S(1)}, u32[]{:S(2)}, u32[]{:S(2)}) collective-permute-start(bf16[2,512,512]{2,1,0:T(8,128)(2,1)} %get-tuple-element.22.own), channel_id=1, source_target_pairs={{1,2},{3,4},{5,6},{7,8},{9,10},{11,12},{13,14},{15,16},{17,18},{19... | collective-permute-start | bytes 3145736 | tf_op jit(solution)/shard_map/ppermute | solution.py:172
  13.3 0.1 reshape.14.link
  13.4 0.1 pad_add_fusion.at.place
  13.5 1.4 %copy-done.1 = bf16[3,512,512]{2,1,0:T(8,128)(2,1)S(1)} copy-done((bf16[3,512,512]{2,1,0:T(8,128)(2,1)S(1)}, bf16[3,512,512]{2,1,0:T(8,128)(2,1)}, u32[]{:S(2)}) %copy-start.1) | copy-done | bytes 1572888
  14.9 1.0 %shard_map.47 = (bf16[512,1536]{1,0:T(8,128)(2,1)S(1)}, bf16[3,512,512]{2,1,0:T(8,128)(2,1)S(1)}) custom-call(s32[3]{0:T(128)S(1)} %pad_add_fusion.at.place, bf16[3,512,512]{2,1,0:T(8,128)(2,1)S(1)} %copy-done, bf16[3,512,512]{2,1,0:T(8,128)(2,1)S(1)} %copy-done.1), custom_call_target="tpu_custom_call" | custom-call | bytes 6291456 | tf_op jit(solution)/shard_map/pallas_call | solution.py:56
  15.9 8.2 %collective-permute-done.across = bf16[2,512,512]{2,1,0:T(8,128)(2,1)} collective-permute-done((bf16[2,512,512]{2,1,0:T(8,128)(2,1)}, bf16[2,512,512]{2,1,0:T(8,128)(2,1)}, u32[]{:S(2)}, u32[]{:S(2)}) %collective-permute-start) | collective-permute-done | bytes 1048608 | tf_op jit(solution)/shard_map/ppermute | solution.py:172
  24.1 0.0 collective-permute-done.1.chip
  24.2 6.5 %shard_map.48 = (bf16[2,160,512]{2,1,0:T(8,128)(2,1)S(1)}, bf16[2,160,512]{2,1,0:T(8,128)(2,1)S(1)}, bf16[2,160,512]{2,1,0:T(8,128)(2,1)S(1)}, bf16[2,32,512]{2,1,0:T(8,128)(2,1)S(1)}) custom-call(s32[3]{0:T(128)S(1)} %pad_add_fusion.at.place, s32[30]{0:T(128)S(1)} %reshape.14.link, bf16[2,512,512]{2,1,0:T(8,128)(2,1)} %collective-permute-done.across, ...), custom_call_target="tpu_custom_call" | custom-call | flops 3221225472 | bytes 8388608 | tf_op jit(solution)/shard_map/pallas_call | solution.py:139
  30.7 4.6 %collective-permute-done.3.across = bf16[2,512,512]{2,1,0:T(8,128)(2,1)S(1)} collective-permute-done((bf16[2,512,512]{2,1,0:T(8,128)(2,1)}, bf16[2,512,512]{2,1,0:T(8,128)(2,1)S(1)}, u32[]{:S(2)}, u32[]{:S(2)}) %collective-permute-start.3) | collective-permute-done | bytes 1048608 | tf_op jit(solution)/shard_map/ppermute | solution.py:172
  35.3 6.2 %shard_map.49 = (bf16[2,160,512]{2,1,0:T(8,128)(2,1)S(1)}, bf16[2,2,160,512]{3,2,1,0:T(8,128)(2,1)S(1)}, bf16[2,160,512]{2,1,0:T(8,128)(2,1)S(1)}, bf16[2,2,32,512]{3,2,1,0:T(8,128)(2,1)S(1)}) custom-call(s32[3]{0:T(128)S(1)} %pad_add_fusion.at.place, s32[30]{0:T(128)S(1)} %reshape.14.link, bf16[2,512,512]{2,1,0:T(8,128)(2,1)S(1)} %collective-permute-done.3.across, ...), custom_call_target="tpu_custom_call" | custom-call | flops 3221225472 | bytes 8388608 | tf_op jit(solution)/shard_map/pallas_call | solution.py:139
  41.4 3.5 %collective-permute-start.4 = (bf16[2,2,160,512]{3,2,1,0:T(8,128)(2,1)S(1)}, bf16[2,2,160,512]{3,2,1,0:T(8,128)(2,1)S(1)}, u32[]{:S(2)}, u32[]{:S(2)}) collective-permute-start(bf16[2,2,160,512]{3,2,1,0:T(8,128)(2,1)S(1)} %get-tuple-element.25), channel_id=1, source_target_pairs={{0,480},{1,33},{2,482},{3,35},{4,484},{5,37},{6,486},{7,39},{8,488... | collective-permute-start | bytes 1966088 | tf_op jit(solution)/shard_map/ppermute | solution.py:160
  45.0 9.5 %collective-permute-start.2 = (bf16[2,160,512]{2,1,0:T(8,128)(2,1)S(1)}, bf16[2,160,512]{2,1,0:T(8,128)(2,1)S(1)}, u32[]{:S(2)}, u32[]{:S(2)}) collective-permute-start(bf16[2,160,512]{2,1,0:T(8,128)(2,1)S(1)} %get-tuple-element.21), channel_id=1, source_target_pairs={{0,32},{1,481},{2,34},{3,483},{4,36},{5,485},{6,38},{7,487},{8,40}... | collective-permute-start | bytes 983048 | tf_op jit(solution)/shard_map/ppermute | solution.py:160
  54.5 3.4 %collective-permute-start.5 = (bf16[2,160,512]{2,1,0:T(8,128)(2,1)S(1)}, bf16[2,160,512]{2,1,0:T(8,128)(2,1)S(1)}, u32[]{:S(2)}, u32[]{:S(2)}) collective-permute-start(bf16[2,160,512]{2,1,0:T(8,128)(2,1)S(1)} %get-tuple-element.27), channel_id=1, source_target_pairs={{0,32},{1,481},{2,34},{3,483},{4,36},{5,485},{6,38},{7,487},{8,40}... | collective-permute-start | bytes 983048 | tf_op jit(solution)/shard_map/ppermute | solution.py:160
  57.9 4.1 %collective-permute-done.2 = bf16[2,160,512]{2,1,0:T(8,128)(2,1)S(1)} collective-permute-done((bf16[2,160,512]{2,1,0:T(8,128)(2,1)S(1)}, bf16[2,160,512]{2,1,0:T(8,128)(2,1)S(1)}, u32[]{:S(2)}, u32[]{:S(2)}) %collective-permute-start.2) | collective-permute-done | bytes 327712 | tf_op jit(solution)/shard_map/ppermute | solution.py:160
  62.0 3.5 %collective-permute-done.5 = bf16[2,160,512]{2,1,0:T(8,128)(2,1)S(1)} collective-permute-done((bf16[2,160,512]{2,1,0:T(8,128)(2,1)S(1)}, bf16[2,160,512]{2,1,0:T(8,128)(2,1)S(1)}, u32[]{:S(2)}, u32[]{:S(2)}) %collective-permute-start.5) | collective-permute-done | bytes 327712 | tf_op jit(solution)/shard_map/ppermute | solution.py:160
  65.5 0.0 collective-permute-done.4
  65.5 0.2 convert_add_fusion.1
  65.8 1.9 %collective-permute-start.7 = (bf16[2,2,32,512]{3,2,1,0:T(8,128)(2,1)S(1)}, bf16[2,2,32,512]{3,2,1,0:T(8,128)(2,1)S(1)}, u32[]{:S(2)}, u32[]{:S(2)}) collective-permute-start(bf16[2,2,32,512]{3,2,1,0:T(8,128)(2,1)S(1)} %get-tuple-element.31), channel_id=1, source_target_pairs={{0,416},{1,97},{2,418},{3,99},{4,420},{5,101},{6,422},{7,103},{8,4... | collective-permute-start | bytes 393224 | tf_op jit(solution)/shard_map/ppermute | solution.py:160
  67.7 6.4 %collective-permute-start.9 = (bf16[2,2,32,512]{3,2,1,0:T(8,128)(2,1)S(1)}, bf16[2,2,32,512]{3,2,1,0:T(8,128)(2,1)S(1)}, u32[]{:S(2)}, u32[]{:S(2)}) collective-permute-start(bf16[2,2,32,512]{3,2,1,0:T(8,128)(2,1)S(1)} %get-tuple-element.32), channel_id=1, source_target_pairs={{0,96},{1,417},{2,98},{3,419},{4,100},{5,421},{6,102},{7,423},{8,1... | collective-permute-start | bytes 393224 | tf_op jit(solution)/shard_map/ppermute | solution.py:160
  74.1 2.6 %collective-permute-start.6 = (bf16[2,2,32,512]{3,2,1,0:T(8,128)(2,1)S(1)}, bf16[2,2,32,512]{3,2,1,0:T(8,128)(2,1)S(1)}, u32[]{:S(2)}, u32[]{:S(2)}) collective-permute-start(bf16[2,2,32,512]{3,2,1,0:T(8,128)(2,1)S(1)} %get-tuple-element.28), channel_id=1, source_target_pairs={{0,448},{1,65},{2,450},{3,67},{4,452},{5,69},{6,454},{7,71},{8,456... | collective-permute-start | bytes 393224 | tf_op jit(solution)/shard_map/ppermute | solution.py:160
  76.7 0.0 collective-permute-done.7
  76.7 3.4 %collective-permute-done.9 = bf16[2,2,32,512]{3,2,1,0:T(8,128)(2,1)S(1)} collective-permute-done((bf16[2,2,32,512]{3,2,1,0:T(8,128)(2,1)S(1)}, bf16[2,2,32,512]{3,2,1,0:T(8,128)(2,1)S(1)}, u32[]{:S(2)}, u32[]{:S(2)}) %collective-permute-start.9) | collective-permute-done | bytes 131104 | tf_op jit(solution)/shard_map/ppermute | solution.py:160
  80.2 0.1 fusion.3
  80.3 6.3 %collective-permute-start.10 = (bf16[2,2,32,512]{3,2,1,0:T(8,128)(2,1)S(1)}, bf16[2,2,32,512]{3,2,1,0:T(8,128)(2,1)S(1)}, u32[]{:S(2)}, u32[]{:S(2)}) collective-permute-start(bf16[2,2,32,512]{3,2,1,0:T(8,128)(2,1)S(1)} %get-tuple-element.30), channel_id=1, source_target_pairs={{0,96},{1,417},{2,98},{3,419},{4,100},{5,421},{6,102},{7,423},{8,1... | collective-permute-start | bytes 393224 | tf_op jit(solution)/shard_map/ppermute | solution.py:160
  86.6 1.9 %collective-permute-start.8 = (bf16[2,2,32,512]{3,2,1,0:T(8,128)(2,1)S(1)}, bf16[2,2,32,512]{3,2,1,0:T(8,128)(2,1)S(1)}, u32[]{:S(2)}, u32[]{:S(2)}) collective-permute-start(bf16[2,2,32,512]{3,2,1,0:T(8,128)(2,1)S(1)} %get-tuple-element.29), channel_id=1, source_target_pairs={{0,384},{1,129},{2,386},{3,131},{4,388},{5,133},{6,390},{7,135},{8... | collective-permute-start | bytes 393224 | tf_op jit(solution)/shard_map/ppermute | solution.py:160
  88.5 0.0 collective-permute-done.6
  88.5 1.0 collective-permute-done.10
  89.5 13.4 %collective-permute-done.8 = bf16[2,2,32,512]{3,2,1,0:T(8,128)(2,1)S(1)} collective-permute-done((bf16[2,2,32,512]{3,2,1,0:T(8,128)(2,1)S(1)}, bf16[2,2,32,512]{3,2,1,0:T(8,128)(2,1)S(1)}, u32[]{:S(2)}, u32[]{:S(2)}) %collective-permute-start.8) | collective-permute-done | bytes 131104 | tf_op jit(solution)/shard_map/ppermute | solution.py:160
  102.9 0.8 fusion.6
  (10 shorter events, 0.1 us)
Async XLA Ops:
  0.0 13.3 %copy-start.4 = (s32[3,2,5]{2,1,0:T(2,128)S(1)}, s32[3,2,5]{2,1,0:T(2,128)}, u32[]{:S(2)}) copy-start(s32[3,2,5]{2,1,0:T(2,128)} %param.7) | copy-start | bytes 364
  0.0 13.5 %copy-start = (bf16[3,512,512]{2,1,0:T(8,128)(2,1)S(1)}, bf16[3,512,512]{2,1,0:T(8,128)(2,1)}, u32[]{:S(2)}) copy-start(bf16[3,512,512]{2,1,0:T(8,128)(2,1)} %left.1) | copy-start | bytes 4718596
  0.0 24.1 %collective-permute-start.1 = (bf16[2,2,512,512]{3,2,1,0:T(8,128)(2,1)}, bf16[2,2,512,512]{3,2,1,0:T(8,128)(2,1)}, u32[]{:S(2)}, u32[]{:S(2)}) collective-permute-start(bf16[2,2,512,512]{3,2,1,0:T(8,128)(2,1)} %psi.1), channel_id=1, source_target_pairs={{0,1},{1,0},{2,3},{3,2},{4,5},{5,4},{6,7},{7,6},{8,9},{9,8},{10,11... | collective-permute-start | bytes 6291464 | tf_op jit(solution)/shard_map/ppermute | solution.py:173
  5.6 18.5 %collective-permute-start = (bf16[2,512,512]{2,1,0:T(8,128)(2,1)}, bf16[2,512,512]{2,1,0:T(8,128)(2,1)}, u32[]{:S(2)}, u32[]{:S(2)}) collective-permute-start(bf16[2,512,512]{2,1,0:T(8,128)(2,1)} %get-tuple-element.17.own), channel_id=1, source_target_pairs={{1,2},{3,4},{5,6},{7,8},{9,10},{11,12},{13,14},{15,16},{17,18},{19... | collective-permute-start | bytes 3145736 | tf_op jit(solution)/shard_map/ppermute | solution.py:172
  8.6 26.6 %collective-permute-start.3 = (bf16[2,512,512]{2,1,0:T(8,128)(2,1)}, bf16[2,512,512]{2,1,0:T(8,128)(2,1)S(1)}, u32[]{:S(2)}, u32[]{:S(2)}) collective-permute-start(bf16[2,512,512]{2,1,0:T(8,128)(2,1)} %get-tuple-element.22.own), channel_id=1, source_target_pairs={{1,2},{3,4},{5,6},{7,8},{9,10},{11,12},{13,14},{15,16},{17,18},{19... | collective-permute-start | bytes 3145736 | tf_op jit(solution)/shard_map/ppermute | solution.py:172
  13.5 1.4 %copy-start.1 = (bf16[3,512,512]{2,1,0:T(8,128)(2,1)S(1)}, bf16[3,512,512]{2,1,0:T(8,128)(2,1)}, u32[]{:S(2)}) copy-start(bf16[3,512,512]{2,1,0:T(8,128)(2,1)} %right.1) | copy-start | bytes 4718596
  14.9 9.3 %copy-start.3 = (bf16[2,512,512]{2,1,0:T(8,128)(2,1)S(1)}, bf16[2,512,512]{2,1,0:T(8,128)(2,1)}, u32[]{:S(2)}) copy-start(bf16[2,512,512]{2,1,0:T(8,128)(2,1)} %get-tuple-element.17.own) | copy-start | bytes 3145732
  24.2 11.1 %copy-start.2 = (bf16[2,512,512]{2,1,0:T(8,128)(2,1)S(1)}, bf16[2,512,512]{2,1,0:T(8,128)(2,1)}, u32[]{:S(2)}) copy-start(bf16[2,512,512]{2,1,0:T(8,128)(2,1)} %get-tuple-element.22.own) | copy-start | bytes 3145732
  41.4 24.0 %collective-permute-start.4 = (bf16[2,2,160,512]{3,2,1,0:T(8,128)(2,1)S(1)}, bf16[2,2,160,512]{3,2,1,0:T(8,128)(2,1)S(1)}, u32[]{:S(2)}, u32[]{:S(2)}) collective-permute-start(bf16[2,2,160,512]{3,2,1,0:T(8,128)(2,1)S(1)} %get-tuple-element.25), channel_id=1, source_target_pairs={{0,480},{1,33},{2,482},{3,35},{4,484},{5,37},{6,486},{7,39},{8,488... | collective-permute-start | bytes 1966088 | tf_op jit(solution)/shard_map/ppermute | solution.py:160
  45.0 17.0 %collective-permute-start.2 = (bf16[2,160,512]{2,1,0:T(8,128)(2,1)S(1)}, bf16[2,160,512]{2,1,0:T(8,128)(2,1)S(1)}, u32[]{:S(2)}, u32[]{:S(2)}) collective-permute-start(bf16[2,160,512]{2,1,0:T(8,128)(2,1)S(1)} %get-tuple-element.21), channel_id=1, source_target_pairs={{0,32},{1,481},{2,34},{3,483},{4,36},{5,485},{6,38},{7,487},{8,40}... | collective-permute-start | bytes 983048 | tf_op jit(solution)/shard_map/ppermute | solution.py:160
  54.5 11.0 %collective-permute-start.5 = (bf16[2,160,512]{2,1,0:T(8,128)(2,1)S(1)}, bf16[2,160,512]{2,1,0:T(8,128)(2,1)S(1)}, u32[]{:S(2)}, u32[]{:S(2)}) collective-permute-start(bf16[2,160,512]{2,1,0:T(8,128)(2,1)S(1)} %get-tuple-element.27), channel_id=1, source_target_pairs={{0,32},{1,481},{2,34},{3,483},{4,36},{5,485},{6,38},{7,487},{8,40}... | collective-permute-start | bytes 983048 | tf_op jit(solution)/shard_map/ppermute | solution.py:160
  65.8 11.0 %collective-permute-start.7 = (bf16[2,2,32,512]{3,2,1,0:T(8,128)(2,1)S(1)}, bf16[2,2,32,512]{3,2,1,0:T(8,128)(2,1)S(1)}, u32[]{:S(2)}, u32[]{:S(2)}) collective-permute-start(bf16[2,2,32,512]{3,2,1,0:T(8,128)(2,1)S(1)} %get-tuple-element.31), channel_id=1, source_target_pairs={{0,416},{1,97},{2,418},{3,99},{4,420},{5,101},{6,422},{7,103},{8,4... | collective-permute-start | bytes 393224 | tf_op jit(solution)/shard_map/ppermute | solution.py:160
  67.7 12.5 %collective-permute-start.9 = (bf16[2,2,32,512]{3,2,1,0:T(8,128)(2,1)S(1)}, bf16[2,2,32,512]{3,2,1,0:T(8,128)(2,1)S(1)}, u32[]{:S(2)}, u32[]{:S(2)}) collective-permute-start(bf16[2,2,32,512]{3,2,1,0:T(8,128)(2,1)S(1)} %get-tuple-element.32), channel_id=1, source_target_pairs={{0,96},{1,417},{2,98},{3,419},{4,100},{5,421},{6,102},{7,423},{8,1... | collective-permute-start | bytes 393224 | tf_op jit(solution)/shard_map/ppermute | solution.py:160
  74.1 14.5 %collective-permute-start.6 = (bf16[2,2,32,512]{3,2,1,0:T(8,128)(2,1)S(1)}, bf16[2,2,32,512]{3,2,1,0:T(8,128)(2,1)S(1)}, u32[]{:S(2)}, u32[]{:S(2)}) collective-permute-start(bf16[2,2,32,512]{3,2,1,0:T(8,128)(2,1)S(1)} %get-tuple-element.28), channel_id=1, source_target_pairs={{0,448},{1,65},{2,450},{3,67},{4,452},{5,69},{6,454},{7,71},{8,456... | collective-permute-start | bytes 393224 | tf_op jit(solution)/shard_map/ppermute | solution.py:160
  80.3 9.2 %collective-permute-start.10 = (bf16[2,2,32,512]{3,2,1,0:T(8,128)(2,1)S(1)}, bf16[2,2,32,512]{3,2,1,0:T(8,128)(2,1)S(1)}, u32[]{:S(2)}, u32[]{:S(2)}) collective-permute-start(bf16[2,2,32,512]{3,2,1,0:T(8,128)(2,1)S(1)} %get-tuple-element.30), channel_id=1, source_target_pairs={{0,96},{1,417},{2,98},{3,419},{4,100},{5,421},{6,102},{7,423},{8,1... | collective-permute-start | bytes 393224 | tf_op jit(solution)/shard_map/ppermute | solution.py:160
  86.6 16.3 %collective-permute-start.8 = (bf16[2,2,32,512]{3,2,1,0:T(8,128)(2,1)S(1)}, bf16[2,2,32,512]{3,2,1,0:T(8,128)(2,1)S(1)}, u32[]{:S(2)}, u32[]{:S(2)}) collective-permute-start(bf16[2,2,32,512]{3,2,1,0:T(8,128)(2,1)S(1)} %get-tuple-element.29), channel_id=1, source_target_pairs={{0,384},{1,129},{2,386},{3,131},{4,388},{5,133},{6,390},{7,135},{8... | collective-permute-start | bytes 393224 | tf_op jit(solution)/shard_map/ppermute | solution.py:160

commit v5 on v3

--- a/solution.py
+++ b/solution.py
@@ -1,3 +1,5 @@
+import functools
+
 import jax
 import jax.numpy as jnp
 from jax import lax
@@ -7,8 +9,9 @@
 
 F32, BF16 = jnp.float32, jnp.bfloat16
 RING = 16
-LEADERS = (0, 3, -3, 6, -6)
-ORDER = [1 - p for p in LEADERS] + [-1 - p for p in LEADERS] + [-p for p in LEADERS] + [8]
+LEADERS = (0, 4, -3, 7, -6)
+SPARE = 2
+ORDER = [1 - p for p in LEADERS] + [-1 - p for p in LEADERS] + [-p for p in LEADERS] + [-SPARE]
 
 
 def split_kernel(psi, *rest):
@@ -63,7 +66,7 @@
     )(at, left, right)
 
 
-def kernel(v, place, link, across, own, chip, right, left, up, down, mine, opposite, combined, halved):
+def kernel(v, place, link, across, own, chip, right, left, up, down, mine, spare, combined, halved):
     terms, size = right.shape[0], right.shape[1]
     first_core = place[0] % 2 == 0
     lowest, highest = place[0] == 0, place[0] == place[1] - 1
@@ -112,7 +115,7 @@
                 left[pl.ds(top, high), :], halved[j], preferred_element_type=F32
             ).astype(BF16)
             start = 0
-            for out in (up, down, mine, opposite):
+            for out in (up, down, mine, spare):
                 end = start + out.shape[1]
                 low, stop = max(top, start), min(top + high, end)
                 if low < stop:
@@ -127,7 +130,7 @@
     scalars = pl.BlockSpec(memory_space=pltpu.SMEM)
     counts = [len(LEADERS)] * 3 + [1]
     return pl.pallas_call(
-        lambda *refs: kernel(v, *refs),
+        functools.partial(kernel, v),
         in_specs=[scalars, scalars] + [whole] * 5,
         out_specs=[whole] * 4,
         out_shape=[jax.ShapeDtypeStruct((2, n * share, size), BF16) for n in counts],
@@ -153,7 +156,6 @@
 def shards(psi, left_op, right_op, link):
     place = lax.axis_index("sec")
     count = lax.axis_size("sec")
-    vectors = psi.shape[0]
     share = psi.shape[2] // RING
     at = jnp.stack([place, count, lax.axis_index("op")]).astype(jnp.int32)
 
@@ -164,23 +166,22 @@
     chip = lax.ppermute(psi, "sec", [(i, i ^ 1) for i in range(count)])
 
     left, right = arrange(at, left_op, right_op)
-    totals, opposites = [], []
-    for v in range(vectors):
-        up, down, mine, opposite = partials(
-            v, at, link.reshape(-1), across[v], own[v], chip, right, left
-        )
+    link = link.reshape(-1)
+    here, above, below, spares = [], [], [], []
+    for v in range(2):
+        up, down, mine, spare = partials(v, at, link, across[v], own[v], chip, right, left)
         total = mine.astype(F32) + shift(up, 1).astype(F32) + shift(down, -1).astype(F32)
-        totals.append(total.reshape(2, len(LEADERS), share, -1))
-        opposites.append(opposite)
-    opposite = shift(jnp.stack(opposites), -2).astype(F32)
-    here, above, below, far_above, far_below = (
-        jnp.stack([total[:, i] for total in totals]) for i in range(len(LEADERS))
-    )
-    far_above = shift((far_above + opposite).astype(BF16), -3).astype(F32)
-    far_below = shift(far_below.astype(BF16), 3).astype(F32)
-    above = shift((above + far_above).astype(BF16), -3).astype(F32)
-    below = shift((below + far_below).astype(BF16), 3).astype(F32)
-    return here + above + below
+        total = total.reshape(2, len(LEADERS), share, -1)
+        far_above = shift(total[:, 3].astype(BF16), -3).astype(F32)
+        far_below = shift(total[:, 4].astype(BF16), 3).astype(F32)
+        here.append(total[:, 0])
+        above.append((total[:, 1] + far_above).astype(BF16))
+        below.append((total[:, 2] + far_below).astype(BF16))
+        spares.append(spare)
+    spare = shift(jnp.stack(spares), -SPARE).astype(F32)
+    above = shift(jnp.stack(above), -4).astype(F32)
+    below = shift(jnp.stack(below), 3).astype(F32)
+    return jnp.stack(here) + spare + above + below
 
 
 def solution(mesh):

time: 98.6 us -> 100 us (1.014)
  the two profiles are of different devices: /device:TPU:14 before, /device:TPU:40 now
where the time goes in v5:
time: 100 us; the launch traced here: 99.4 us
  starting transfers between devices  60.4 us (60%)
  waiting for transfers between devices  19.4 us (19%)
  Pallas kernels  16.6 us (17%)
  local copies, waits for them, and re-layouts  1.57 us (2%)
  other arithmetic  1.2 us (1%)
    ppermute x11, starting transfers between devices, shift(): return lax.ppermute(x, ('op', 'sec'), pairs)  50.7 us
    pallas_call x2, Pallas kernels, partials(): pl.pallas_call(functools.partial(kernel, v), in_specs=[scalars, scalars]...  12.7 us
    ppermute x11, waiting for transfers between devices, shift(): return lax.ppermute(x, ('op', 'sec'), pairs)  11.2 us
    ppermute x2, waiting for transfers between devices, shards(): across = [lax.ppermute(block, 'sec', facing) for block in own]  8.21 us
    ppermute x2, starting transfers between devices, shards(): across = [lax.ppermute(block, 'sec', facing) for block in own]  7.67 us
    pallas_call x1, Pallas kernels, split(): pl.pallas_call(split_kernel, in_specs=[pl.BlockSpec(memory_space=pl.ANY)]...  2.86 us
    ppermute x1, starting transfers between devices, shards(): chip = lax.ppermute(psi, 'sec', [(i, i ^ 1) for i in range(count)])  2.04 us
  transfers between devices with their start and end apart: 14, of which 4 were waited for; matrix products, arithmetic and copies ran while one was open for 1% of the time, Pallas kernels for 17%

profile of v5, /device:TPU:40, one launch (start us, length us, event | category | flops | bytes accessed | tf_op | source)
XLA Modules:
  0.0 99.4 jit_solution(3168165797874525019)
XLA Ops:
  0.0 2.0 %collective-permute-start.1 = (bf16[2,2,512,512]{3,2,1,0:T(8,128)(2,1)}, bf16[2,2,512,512]{3,2,1,0:T(8,128)(2,1)}, u32[]{:S(2)}, u32[]{:S(2)}) collective-permute-start(bf16[2,2,512,512]{3,2,1,0:T(8,128)(2,1)} %psi.1), channel_id=1, source_target_pairs={{0,1},{1,0},{2,3},{3,2},{4,5},{5,4},{6,7},{7,6},{8,9},{9,8},{10,11... | collective-permute-start | bytes 6291464 | tf_op jit(solution)/shard_map/ppermute | solution.py:166
  2.1 2.9 %shard_map.46 = (bf16[2,512,512]{2,1,0:T(8,128)(2,1)}, bf16[2,512,512]{2,1,0:T(8,128)(2,1)}) custom-call(bf16[2,2,512,512]{3,2,1,0:T(8,128)(2,1)} %psi.1), custom_call_target="tpu_custom_call" | custom-call | bytes 4194304 | tf_op jit(solution)/shard_map/pallas_call | solution.py:28
  4.9 4.7 %collective-permute-start = (bf16[2,512,512]{2,1,0:T(8,128)(2,1)}, bf16[2,512,512]{2,1,0:T(8,128)(2,1)}, u32[]{:S(2)}, u32[]{:S(2)}) collective-permute-start(bf16[2,512,512]{2,1,0:T(8,128)(2,1)} %get-tuple-element.17.own), channel_id=1, source_target_pairs={{1,2},{3,4},{5,6},{7,8},{9,10},{11,12},{13,14},{15,16},{17,18},{19... | collective-permute-start | bytes 3145736 | tf_op jit(solution)/shard_map/ppermute | solution.py:165
  9.6 3.0 %collective-permute-start.4 = (bf16[2,512,512]{2,1,0:T(8,128)(2,1)}, bf16[2,512,512]{2,1,0:T(8,128)(2,1)S(1)}, u32[]{:S(2)}, u32[]{:S(2)}) collective-permute-start(bf16[2,512,512]{2,1,0:T(8,128)(2,1)} %get-tuple-element.23.own), channel_id=1, source_target_pairs={{1,2},{3,4},{5,6},{7,8},{9,10},{11,12},{13,14},{15,16},{17,18},{19... | collective-permute-start | bytes 3145736 | tf_op jit(solution)/shard_map/ppermute | solution.py:165
  12.6 0.1 reshape.13.link
  12.7 0.1 pad_add_fusion.at.place
  12.8 1.4 %copy-done.1 = bf16[3,512,512]{2,1,0:T(8,128)(2,1)S(1)} copy-done((bf16[3,512,512]{2,1,0:T(8,128)(2,1)S(1)}, bf16[3,512,512]{2,1,0:T(8,128)(2,1)}, u32[]{:S(2)}) %copy-start.1) | copy-done | bytes 1572888
  14.2 1.0 %shard_map.47 = (bf16[512,1536]{1,0:T(8,128)(2,1)S(1)}, bf16[3,512,512]{2,1,0:T(8,128)(2,1)S(1)}) custom-call(s32[3]{0:T(128)S(1)} %pad_add_fusion.at.place, bf16[3,512,512]{2,1,0:T(8,128)(2,1)S(1)} %copy-done, bf16[3,512,512]{2,1,0:T(8,128)(2,1)S(1)} %copy-done.1), custom_call_target="tpu_custom_call" | custom-call | bytes 6291456 | tf_op jit(solution)/shard_map/pallas_call | solution.py:56
  15.3 8.2 %collective-permute-done.across = bf16[2,512,512]{2,1,0:T(8,128)(2,1)} collective-permute-done((bf16[2,512,512]{2,1,0:T(8,128)(2,1)}, bf16[2,512,512]{2,1,0:T(8,128)(2,1)}, u32[]{:S(2)}, u32[]{:S(2)}) %collective-permute-start) | collective-permute-done | bytes 1048608 | tf_op jit(solution)/shard_map/ppermute | solution.py:165
  23.5 0.0 collective-permute-done.1.chip
  23.5 6.5 %shard_map.48 = (bf16[2,160,512]{2,1,0:T(8,128)(2,1)S(1)}, bf16[2,160,512]{2,1,0:T(8,128)(2,1)S(1)}, bf16[2,160,512]{2,1,0:T(8,128)(2,1)S(1)}, bf16[2,32,512]{2,1,0:T(8,128)(2,1)S(1)}) custom-call(s32[3]{0:T(128)S(1)} %pad_add_fusion.at.place, s32[30]{0:T(128)S(1)} %reshape.13.link, bf16[2,512,512]{2,1,0:T(8,128)(2,1)} %collective-permute-done.across, ...), custom_call_target="tpu_custom_call" | custom-call | flops 3221225472 | bytes 8388608 | tf_op jit(solution)/shard_map/pallas_call | solution.py:132
  30.0 3.8 %collective-permute-start.2 = (bf16[2,160,512]{2,1,0:T(8,128)(2,1)S(1)}, bf16[2,160,512]{2,1,0:T(8,128)(2,1)S(1)}, u32[]{:S(2)}, u32[]{:S(2)}) collective-permute-start(bf16[2,160,512]{2,1,0:T(8,128)(2,1)S(1)} %get-tuple-element.21), channel_id=1, source_target_pairs={{0,32},{1,481},{2,34},{3,483},{4,36},{5,485},{6,38},{7,487},{8,40}... | collective-permute-start | bytes 983048 | tf_op jit(solution)/shard_map/ppermute | solution.py:153
  33.8 2.0 %collective-permute-start.3 = (bf16[2,160,512]{2,1,0:T(8,128)(2,1)S(1)}, bf16[2,160,512]{2,1,0:T(8,128)(2,1)S(1)}, u32[]{:S(2)}, u32[]{:S(2)}) collective-permute-start(bf16[2,160,512]{2,1,0:T(8,128)(2,1)S(1)} %get-tuple-element.22), channel_id=1, source_target_pairs={{0,480},{1,33},{2,482},{3,35},{4,484},{5,37},{6,486},{7,39},{8,488... | collective-permute-start | bytes 983048 | tf_op jit(solution)/shard_map/ppermute | solution.py:153
  35.9 0.0 collective-permute-done.4.across
  35.9 6.1 %shard_map.49 = (bf16[2,160,512]{2,1,0:T(8,128)(2,1)S(1)}, bf16[2,160,512]{2,1,0:T(8,128)(2,1)S(1)}, bf16[2,160,512]{2,1,0:T(8,128)(2,1)S(1)}, bf16[2,32,512]{2,1,0:T(8,128)(2,1)S(1)}) custom-call(s32[3]{0:T(128)S(1)} %pad_add_fusion.at.place, s32[30]{0:T(128)S(1)} %reshape.13.link, bf16[2,512,512]{2,1,0:T(8,128)(2,1)S(1)} %collective-permute-done.4.across, ...), custom_call_target="tpu_custom_call" | custom-call | flops 3221225472 | bytes 8388608 | tf_op jit(solution)/shard_map/pallas_call | solution.py:132
  42.0 3.8 %collective-permute-start.5 = (bf16[2,160,512]{2,1,0:T(8,128)(2,1)S(1)}, bf16[2,160,512]{2,1,0:T(8,128)(2,1)S(1)}, u32[]{:S(2)}, u32[]{:S(2)}) collective-permute-start(bf16[2,160,512]{2,1,0:T(8,128)(2,1)S(1)} %get-tuple-element.25), channel_id=1, source_target_pairs={{0,32},{1,481},{2,34},{3,483},{4,36},{5,485},{6,38},{7,487},{8,40}... | collective-permute-start | bytes 983048 | tf_op jit(solution)/shard_map/ppermute | solution.py:153
  45.9 7.6 %collective-permute-start.6 = (bf16[2,160,512]{2,1,0:T(8,128)(2,1)S(1)}, bf16[2,160,512]{2,1,0:T(8,128)(2,1)S(1)}, u32[]{:S(2)}, u32[]{:S(2)}) collective-permute-start(bf16[2,160,512]{2,1,0:T(8,128)(2,1)S(1)} %get-tuple-element.26), channel_id=1, source_target_pairs={{0,480},{1,33},{2,482},{3,35},{4,484},{5,37},{6,486},{7,39},{8,488... | collective-permute-start | bytes 983048 | tf_op jit(solution)/shard_map/ppermute | solution.py:153
  53.5 5.4 %collective-permute-start.7 = (bf16[2,2,32,512]{3,2,1,0:T(8,128)(2,1)S(1)}, bf16[2,2,32,512]{3,2,1,0:T(8,128)(2,1)S(1)}, u32[]{:S(2)}, u32[]{:S(2)}) collective-permute-start(bf16[2,2,32,512]{3,2,1,0:T(8,128)(2,1)S(1)} %pad_maximum_fusion), channel_id=1, source_target_pairs={{0,448},{1,65},{2,450},{3,67},{4,452},{5,69},{6,454},{7,71},{8,456... | collective-permute-start | bytes 393224 | tf_op jit(solution)/shard_map/ppermute | solution.py:153
  58.9 0.0 collective-permute-done.3
  58.9 0.1 convert_add_fusion.1
  59.0 1.9 %collective-permute-start.11 = (bf16[2,32,512]{2,1,0:T(8,128)(2,1)S(1)}, bf16[2,32,512]{2,1,0:T(8,128)(2,1)S(1)}, u32[]{:S(2)}, u32[]{:S(2)}) collective-permute-start(bf16[2,32,512]{2,1,0:T(8,128)(2,1)S(1)} %get-tuple-element.34), channel_id=1, source_target_pairs={{0,96},{1,417},{2,98},{3,419},{4,100},{5,421},{6,102},{7,423},{8,1... | collective-permute-start | bytes 196616 | tf_op jit(solution)/shard_map/ppermute | solution.py:153
  61.0 6.9 %collective-permute-start.8 = (bf16[2,32,512]{2,1,0:T(8,128)(2,1)S(1)}, bf16[2,32,512]{2,1,0:T(8,128)(2,1)S(1)}, u32[]{:S(2)}, u32[]{:S(2)}) collective-permute-start(bf16[2,32,512]{2,1,0:T(8,128)(2,1)S(1)} %get-tuple-element.33), channel_id=1, source_target_pairs={{0,416},{1,97},{2,418},{3,99},{4,420},{5,101},{6,422},{7,103},{8,4... | collective-permute-start | bytes 196616 | tf_op jit(solution)/shard_map/ppermute | solution.py:153
  67.9 0.0 collective-permute-done.5
  67.9 0.1 convert_add_fusion
  68.1 1.9 %collective-permute-start.12 = (bf16[2,32,512]{2,1,0:T(8,128)(2,1)S(1)}, bf16[2,32,512]{2,1,0:T(8,128)(2,1)S(1)}, u32[]{:S(2)}, u32[]{:S(2)}) collective-permute-start(bf16[2,32,512]{2,1,0:T(8,128)(2,1)S(1)} %get-tuple-element.36), channel_id=1, source_target_pairs={{0,96},{1,417},{2,98},{3,419},{4,100},{5,421},{6,102},{7,423},{8,1... | collective-permute-start | bytes 196616 | tf_op jit(solution)/shard_map/ppermute | solution.py:153
  70.0 6.9 %collective-permute-start.9 = (bf16[2,32,512]{2,1,0:T(8,128)(2,1)S(1)}, bf16[2,32,512]{2,1,0:T(8,128)(2,1)S(1)}, u32[]{:S(2)}, u32[]{:S(2)}) collective-permute-start(bf16[2,32,512]{2,1,0:T(8,128)(2,1)S(1)} %get-tuple-element.35), channel_id=1, source_target_pairs={{0,416},{1,97},{2,418},{3,99},{4,420},{5,101},{6,422},{7,103},{8,4... | collective-permute-start | bytes 196616 | tf_op jit(solution)/shard_map/ppermute | solution.py:153
  77.0 2.5 %collective-permute-done.12 = bf16[2,32,512]{2,1,0:T(8,128)(2,1)S(1)} collective-permute-done((bf16[2,32,512]{2,1,0:T(8,128)(2,1)S(1)}, bf16[2,32,512]{2,1,0:T(8,128)(2,1)S(1)}, u32[]{:S(2)}, u32[]{:S(2)}) %collective-permute-start.12) | collective-permute-done | bytes 65568 | tf_op jit(solution)/shard_map/ppermute | solution.py:153
  79.6 8.4 %collective-permute-start.10 = (bf16[2,2,32,512]{3,2,1,0:T(8,128)(2,1)S(1)}, bf16[2,2,32,512]{3,2,1,0:T(8,128)(2,1)S(1)}, u32[]{:S(2)}, u32[]{:S(2)}) collective-permute-start(bf16[2,2,32,512]{3,2,1,0:T(8,128)(2,1)S(1)} %pad_maximum_fusion.1), channel_id=1, source_target_pairs={{0,384},{1,129},{2,386},{3,131},{4,388},{5,133},{6,390},{7,135},{8... | collective-permute-start | bytes 393224 | tf_op jit(solution)/shard_map/ppermute | solution.py:153
  88.1 1.9 %collective-permute-start.13 = (bf16[2,2,32,512]{3,2,1,0:T(8,128)(2,1)S(1)}, bf16[2,2,32,512]{3,2,1,0:T(8,128)(2,1)S(1)}, u32[]{:S(2)}, u32[]{:S(2)}) collective-permute-start(bf16[2,2,32,512]{3,2,1,0:T(8,128)(2,1)S(1)} %pad_maximum_fusion.2), channel_id=1, source_target_pairs={{0,96},{1,417},{2,98},{3,419},{4,100},{5,421},{6,102},{7,423},{8,1... | collective-permute-start | bytes 393224 | tf_op jit(solution)/shard_map/ppermute | solution.py:153
  90.0 5.6 %collective-permute-done.10 = bf16[2,2,32,512]{3,2,1,0:T(8,128)(2,1)S(1)} collective-permute-done((bf16[2,2,32,512]{3,2,1,0:T(8,128)(2,1)S(1)}, bf16[2,2,32,512]{3,2,1,0:T(8,128)(2,1)S(1)}, u32[]{:S(2)}, u32[]{:S(2)}) %collective-permute-start.10) | collective-permute-done | bytes 131104 | tf_op jit(solution)/shard_map/ppermute | solution.py:153
  95.6 3.0 %collective-permute-done.13 = bf16[2,2,32,512]{3,2,1,0:T(8,128)(2,1)S(1)} collective-permute-done((bf16[2,2,32,512]{3,2,1,0:T(8,128)(2,1)S(1)}, bf16[2,2,32,512]{3,2,1,0:T(8,128)(2,1)S(1)}, u32[]{:S(2)}, u32[]{:S(2)}) %collective-permute-start.13) | collective-permute-done | bytes 131104 | tf_op jit(solution)/shard_map/ppermute | solution.py:153
  98.7 0.8 fusion.1
  (24 shorter events, 0.2 us)
Async XLA Ops:
  0.0 12.6 %copy-start.4 = (s32[3,2,5]{2,1,0:T(2,128)S(1)}, s32[3,2,5]{2,1,0:T(2,128)}, u32[]{:S(2)}) copy-start(s32[3,2,5]{2,1,0:T(2,128)} %param.7) | copy-start | bytes 364
  0.0 12.8 %copy-start = (bf16[3,512,512]{2,1,0:T(8,128)(2,1)S(1)}, bf16[3,512,512]{2,1,0:T(8,128)(2,1)}, u32[]{:S(2)}) copy-start(bf16[3,512,512]{2,1,0:T(8,128)(2,1)} %left.1) | copy-start | bytes 4718596
  0.0 23.5 %collective-permute-start.1 = (bf16[2,2,512,512]{3,2,1,0:T(8,128)(2,1)}, bf16[2,2,512,512]{3,2,1,0:T(8,128)(2,1)}, u32[]{:S(2)}, u32[]{:S(2)}) collective-permute-start(bf16[2,2,512,512]{3,2,1,0:T(8,128)(2,1)} %psi.1), channel_id=1, source_target_pairs={{0,1},{1,0},{2,3},{3,2},{4,5},{5,4},{6,7},{7,6},{8,9},{9,8},{10,11... | collective-permute-start | bytes 6291464 | tf_op jit(solution)/shard_map/ppermute | solution.py:166
  4.9 18.5 %collective-permute-start = (bf16[2,512,512]{2,1,0:T(8,128)(2,1)}, bf16[2,512,512]{2,1,0:T(8,128)(2,1)}, u32[]{:S(2)}, u32[]{:S(2)}) collective-permute-start(bf16[2,512,512]{2,1,0:T(8,128)(2,1)} %get-tuple-element.17.own), channel_id=1, source_target_pairs={{1,2},{3,4},{5,6},{7,8},{9,10},{11,12},{13,14},{15,16},{17,18},{19... | collective-permute-start | bytes 3145736 | tf_op jit(solution)/shard_map/ppermute | solution.py:165
  9.6 26.3 %collective-permute-start.4 = (bf16[2,512,512]{2,1,0:T(8,128)(2,1)}, bf16[2,512,512]{2,1,0:T(8,128)(2,1)S(1)}, u32[]{:S(2)}, u32[]{:S(2)}) collective-permute-start(bf16[2,512,512]{2,1,0:T(8,128)(2,1)} %get-tuple-element.23.own), channel_id=1, source_target_pairs={{1,2},{3,4},{5,6},{7,8},{9,10},{11,12},{13,14},{15,16},{17,18},{19... | collective-permute-start | bytes 3145736 | tf_op jit(solution)/shard_map/ppermute | solution.py:165
  12.8 1.4 %copy-start.1 = (bf16[3,512,512]{2,1,0:T(8,128)(2,1)S(1)}, bf16[3,512,512]{2,1,0:T(8,128)(2,1)}, u32[]{:S(2)}) copy-start(bf16[3,512,512]{2,1,0:T(8,128)(2,1)} %right.1) | copy-start | bytes 4718596
  14.2 9.3 %copy-start.3 = (bf16[2,512,512]{2,1,0:T(8,128)(2,1)S(1)}, bf16[2,512,512]{2,1,0:T(8,128)(2,1)}, u32[]{:S(2)}) copy-start(bf16[2,512,512]{2,1,0:T(8,128)(2,1)} %get-tuple-element.17.own) | copy-start | bytes 3145732
  23.5 12.4 %copy-start.2 = (bf16[2,512,512]{2,1,0:T(8,128)(2,1)S(1)}, bf16[2,512,512]{2,1,0:T(8,128)(2,1)}, u32[]{:S(2)}) copy-start(bf16[2,512,512]{2,1,0:T(8,128)(2,1)} %get-tuple-element.23.own) | copy-start | bytes 3145732
  30.0 28.9 %collective-permute-start.2 = (bf16[2,160,512]{2,1,0:T(8,128)(2,1)S(1)}, bf16[2,160,512]{2,1,0:T(8,128)(2,1)S(1)}, u32[]{:S(2)}, u32[]{:S(2)}) collective-permute-start(bf16[2,160,512]{2,1,0:T(8,128)(2,1)S(1)} %get-tuple-element.21), channel_id=1, source_target_pairs={{0,32},{1,481},{2,34},{3,483},{4,36},{5,485},{6,38},{7,487},{8,40}... | collective-permute-start | bytes 983048 | tf_op jit(solution)/shard_map/ppermute | solution.py:153
  33.8 25.0 %collective-permute-start.3 = (bf16[2,160,512]{2,1,0:T(8,128)(2,1)S(1)}, bf16[2,160,512]{2,1,0:T(8,128)(2,1)S(1)}, u32[]{:S(2)}, u32[]{:S(2)}) collective-permute-start(bf16[2,160,512]{2,1,0:T(8,128)(2,1)S(1)} %get-tuple-element.22), channel_id=1, source_target_pairs={{0,480},{1,33},{2,482},{3,35},{4,484},{5,37},{6,486},{7,39},{8,488... | collective-permute-start | bytes 983048 | tf_op jit(solution)/shard_map/ppermute | solution.py:153
  42.0 25.9 %collective-permute-start.5 = (bf16[2,160,512]{2,1,0:T(8,128)(2,1)S(1)}, bf16[2,160,512]{2,1,0:T(8,128)(2,1)S(1)}, u32[]{:S(2)}, u32[]{:S(2)}) collective-permute-start(bf16[2,160,512]{2,1,0:T(8,128)(2,1)S(1)} %get-tuple-element.25), channel_id=1, source_target_pairs={{0,32},{1,481},{2,34},{3,483},{4,36},{5,485},{6,38},{7,487},{8,40}... | collective-permute-start | bytes 983048 | tf_op jit(solution)/shard_map/ppermute | solution.py:153
  45.9 22.1 %collective-permute-start.6 = (bf16[2,160,512]{2,1,0:T(8,128)(2,1)S(1)}, bf16[2,160,512]{2,1,0:T(8,128)(2,1)S(1)}, u32[]{:S(2)}, u32[]{:S(2)}) collective-permute-start(bf16[2,160,512]{2,1,0:T(8,128)(2,1)S(1)} %get-tuple-element.26), channel_id=1, source_target_pairs={{0,480},{1,33},{2,482},{3,35},{4,484},{5,37},{6,486},{7,39},{8,488... | collective-permute-start | bytes 983048 | tf_op jit(solution)/shard_map/ppermute | solution.py:153
  53.5 36.5 %collective-permute-start.7 = (bf16[2,2,32,512]{3,2,1,0:T(8,128)(2,1)S(1)}, bf16[2,2,32,512]{3,2,1,0:T(8,128)(2,1)S(1)}, u32[]{:S(2)}, u32[]{:S(2)}) collective-permute-start(bf16[2,2,32,512]{3,2,1,0:T(8,128)(2,1)S(1)} %pad_maximum_fusion), channel_id=1, source_target_pairs={{0,448},{1,65},{2,450},{3,67},{4,452},{5,69},{6,454},{7,71},{8,456... | collective-permute-start | bytes 393224 | tf_op jit(solution)/shard_map/ppermute | solution.py:153
  59.0 17.9 %collective-permute-start.11 = (bf16[2,32,512]{2,1,0:T(8,128)(2,1)S(1)}, bf16[2,32,512]{2,1,0:T(8,128)(2,1)S(1)}, u32[]{:S(2)}, u32[]{:S(2)}) collective-permute-start(bf16[2,32,512]{2,1,0:T(8,128)(2,1)S(1)} %get-tuple-element.34), channel_id=1, source_target_pairs={{0,96},{1,417},{2,98},{3,419},{4,100},{5,421},{6,102},{7,423},{8,1... | collective-permute-start | bytes 196616 | tf_op jit(solution)/shard_map/ppermute | solution.py:153
  61.0 16.0 %collective-permute-start.8 = (bf16[2,32,512]{2,1,0:T(8,128)(2,1)S(1)}, bf16[2,32,512]{2,1,0:T(8,128)(2,1)S(1)}, u32[]{:S(2)}, u32[]{:S(2)}) collective-permute-start(bf16[2,32,512]{2,1,0:T(8,128)(2,1)S(1)} %get-tuple-element.33), channel_id=1, source_target_pairs={{0,416},{1,97},{2,418},{3,99},{4,420},{5,101},{6,422},{7,103},{8,4... | collective-permute-start | bytes 196616 | tf_op jit(solution)/shard_map/ppermute | solution.py:153
  68.1 11.5 %collective-permute-start.12 = (bf16[2,32,512]{2,1,0:T(8,128)(2,1)S(1)}, bf16[2,32,512]{2,1,0:T(8,128)(2,1)S(1)}, u32[]{:S(2)}, u32[]{:S(2)}) collective-permute-start(bf16[2,32,512]{2,1,0:T(8,128)(2,1)S(1)} %get-tuple-element.36), channel_id=1, source_target_pairs={{0,96},{1,417},{2,98},{3,419},{4,100},{5,421},{6,102},{7,423},{8,1... | collective-permute-start | bytes 196616 | tf_op jit(solution)/shard_map/ppermute | solution.py:153
  70.0 9.5 %collective-permute-start.9 = (bf16[2,32,512]{2,1,0:T(8,128)(2,1)S(1)}, bf16[2,32,512]{2,1,0:T(8,128)(2,1)S(1)}, u32[]{:S(2)}, u32[]{:S(2)}) collective-permute-start(bf16[2,32,512]{2,1,0:T(8,128)(2,1)S(1)} %get-tuple-element.35), channel_id=1, source_target_pairs={{0,416},{1,97},{2,418},{3,99},{4,420},{5,101},{6,422},{7,103},{8,4... | collective-permute-start | bytes 196616 | tf_op jit(solution)/shard_map/ppermute | solution.py:153
  79.6 16.0 %collective-permute-start.10 = (bf16[2,2,32,512]{3,2,1,0:T(8,128)(2,1)S(1)}, bf16[2,2,32,512]{3,2,1,0:T(8,128)(2,1)S(1)}, u32[]{:S(2)}, u32[]{:S(2)}) collective-permute-start(bf16[2,2,32,512]{3,2,1,0:T(8,128)(2,1)S(1)} %pad_maximum_fusion.1), channel_id=1, source_target_pairs={{0,384},{1,129},{2,386},{3,131},{4,388},{5,133},{6,390},{7,135},{8... | collective-permute-start | bytes 393224 | tf_op jit(solution)/shard_map/ppermute | solution.py:153
  88.1 10.6 %collective-permute-start.13 = (bf16[2,2,32,512]{3,2,1,0:T(8,128)(2,1)S(1)}, bf16[2,2,32,512]{3,2,1,0:T(8,128)(2,1)S(1)}, u32[]{:S(2)}, u32[]{:S(2)}) collective-permute-start(bf16[2,2,32,512]{3,2,1,0:T(8,128)(2,1)S(1)} %pad_maximum_fusion.2), channel_id=1, source_target_pairs={{0,96},{1,417},{2,98},{3,419},{4,100},{5,421},{6,102},{7,423},{8,1... | collective-permute-start | bytes 393224 | tf_op jit(solution)/shard_map/ppermute | solution.py:153

commit v6 on v5

--- a/solution.py
+++ b/solution.py
@@ -1,5 +1,3 @@
-import functools
-
 import jax
 import jax.numpy as jnp
 from jax import lax
@@ -14,26 +12,23 @@
 ORDER = [1 - p for p in LEADERS] + [-1 - p for p in LEADERS] + [-p for p in LEADERS] + [-SPARE]
 
 
-def split_kernel(psi, *rest):
-    outs, sems = rest[:-1], rest[-1]
-    copies = [pltpu.make_async_copy(psi.at[v], out, sems.at[v]) for v, out in enumerate(outs)]
-    for copy in copies:
+def take(psi, v, after=None):
+    operands = [psi] + [x for x in (after,) if x is not None]
+
+    def kernel(source, *rest):
+        copy = pltpu.make_async_copy(source.at[v], rest[-2], rest[-1])
         copy.start()
-    for copy in copies:
         copy.wait()
 
-
-def split(psi):
-    vectors = psi.shape[0]
     return pl.pallas_call(
-        split_kernel,
-        in_specs=[pl.BlockSpec(memory_space=pl.ANY)],
-        out_specs=[pl.BlockSpec(memory_space=pltpu.VMEM)] * vectors,
-        out_shape=[jax.ShapeDtypeStruct(psi.shape[1:], BF16)] * vectors,
-        scratch_shapes=[pltpu.SemaphoreType.DMA((vectors,))],
+        kernel,
+        in_specs=[pl.BlockSpec(memory_space=pl.ANY)] * len(operands),
+        out_specs=pl.BlockSpec(memory_space=pltpu.VMEM),
+        out_shape=jax.ShapeDtypeStruct(psi.shape[1:], BF16),
+        scratch_shapes=[pltpu.SemaphoreType.DMA],
         compiler_params=pltpu.CompilerParams(vmem_limit_bytes=60 * 10**6),
         cost_estimate=pl.CostEstimate(flops=0, bytes_accessed=4 * 2**20, transcendentals=0),
-    )(psi)
+    )(*operands)
 
 
 def arrange_kernel(at, left, right, left_out, right_out):
@@ -66,7 +61,7 @@
     )(at, left, right)
 
 
-def kernel(v, place, link, across, own, chip, right, left, up, down, mine, spare, combined, halved):
+def kernel(place, link, chip, own, across, right, left, up, down, mine, spare, combined, halved):
     terms, size = right.shape[0], right.shape[1]
     first_core = place[0] % 2 == 0
     lowest, highest = place[0] == 0, place[0] == place[1] - 1
@@ -89,7 +84,7 @@
                 columns = pl.ds(column, wide)
                 a0, a1 = (across[i, rows, columns].astype(F32) for i in range(2))
                 o0, o1 = (own[i, rows, columns].astype(F32) for i in range(2))
-                c0, c1 = (chip[v, i, rows, columns].astype(F32) for i in range(2))
+                c0, c1 = (chip[i, rows, columns].astype(F32) for i in range(2))
                 fifth = (jnp.where(first_core, a1, c1), jnp.where(first_core, c0, a0))
                 for j, blocks in enumerate(((a0, o0, o1, c0, fifth[0]), (a1, o0, o1, c1, fifth[1]))):
                     for k in range(terms):
@@ -123,14 +118,14 @@
                 start = end
 
 
-def partials(v, place, link, across, own, chip, right, left):
+def partials(place, link, across, own, chip, right, left):
     terms, size = right.shape[0], right.shape[1]
     share = size // RING
     whole = pl.BlockSpec(memory_space=pltpu.VMEM)
     scalars = pl.BlockSpec(memory_space=pltpu.SMEM)
     counts = [len(LEADERS)] * 3 + [1]
     return pl.pallas_call(
-        functools.partial(kernel, v),
+        kernel,
         in_specs=[scalars, scalars] + [whole] * 5,
         out_specs=[whole] * 4,
         out_shape=[jax.ShapeDtypeStruct((2, n * share, size), BF16) for n in counts],
@@ -142,7 +137,7 @@
         cost_estimate=pl.CostEstimate(
             flops=8 * terms * size**3, bytes_accessed=8 * 2**20, transcendentals=0
         ),
-    )(place, link, across, own, chip, right, left)
+    )(place, link, chip, own, across, right, left)
 
 
 def shift(x, by):
@@ -161,27 +156,28 @@
 
     facing = [(i, i + 1) for i in range(1, count - 1, 2)]
     facing += [(b, a) for a, b in facing]
-    own = split(psi)
-    across = [lax.ppermute(block, "sec", facing) for block in own]
-    chip = lax.ppermute(psi, "sec", [(i, i ^ 1) for i in range(count)])
+    left, right = arrange(at, left_op, right_op)
+    first = take(psi, 0)
+    across = [lax.ppermute(first, "sec", facing)]
+    second = take(psi, 1, left)
+    across.append(lax.ppermute(second, "sec", facing))
+    own = (first, second)
+    chip = [lax.ppermute(x, "sec", [(i, i ^ 1) for i in range(count)]) for x in own]
 
-    left, right = arrange(at, left_op, right_op)
     link = link.reshape(-1)
-    here, above, below, spares = [], [], [], []
+    totals, spares = [], []
     for v in range(2):
-        up, down, mine, spare = partials(v, at, link, across[v], own[v], chip, right, left)
+        up, down, mine, spare = partials(at, link, across[v], own[v], chip[v], right, left)
         total = mine.astype(F32) + shift(up, 1).astype(F32) + shift(down, -1).astype(F32)
-        total = total.reshape(2, len(LEADERS), share, -1)
-        far_above = shift(total[:, 3].astype(BF16), -3).astype(F32)
-        far_below = shift(total[:, 4].astype(BF16), 3).astype(F32)
-        here.append(total[:, 0])
-        above.append((total[:, 1] + far_above).astype(BF16))
-        below.append((total[:, 2] + far_below).astype(BF16))
+        totals.append(total)
         spares.append(spare)
+    total = jnp.stack(totals).reshape(2, 2, len(LEADERS), share, -1)
     spare = shift(jnp.stack(spares), -SPARE).astype(F32)
-    above = shift(jnp.stack(above), -4).astype(F32)
-    below = shift(jnp.stack(below), 3).astype(F32)
-    return jnp.stack(here) + spare + above + below
+    far_above = shift(total[:, :, 3].astype(BF16), -3).astype(F32)
+    far_below = shift(total[:, :, 4].astype(BF16), 3).astype(F32)
+    above = shift((total[:, :, 1] + far_above).astype(BF16), -4).astype(F32)
+    below = shift((total[:, :, 2] + far_below).astype(BF16), 3).astype(F32)
+    return total[:, :, 0] + spare + above + below
 
 
 def solution(mesh):

time: 100 us -> 97.8 us (0.978)
  the two profiles are of different devices: /device:TPU:40 before, /device:TPU:25 now
where the time goes in v6:
time: 97.8 us; the launch traced here: 97.3 us
  starting transfers between devices  51.4 us (53%)
  waiting for transfers between devices  22.7 us (23%)
  Pallas kernels  17.8 us (18%)
  local copies, waits for them, and re-layouts  3.82 us (4%)
  other arithmetic  1.2 us (1%)
    ppermute x9, starting transfers between devices, shift(): return lax.ppermute(x, ('op', 'sec'), pairs)  39.2 us
    ppermute x9, waiting for transfers between devices, shift(): return lax.ppermute(x, ('op', 'sec'), pairs)  22.7 us
    pallas_call x2, Pallas kernels, partials(): pl.pallas_call(kernel, in_specs=[scalars, scalars] + [whole] * 5, out_spe...  12.1 us
    ppermute x2, starting transfers between devices, shards(): lax.ppermute(x, 'sec', [(i, i ^ 1) for i in range(count)])  6.26 us
    pallas_call x2, Pallas kernels, take(): pl.pallas_call(kernel, in_specs=[pl.BlockSpec(memory_space=pl.ANY)] * len...  4.7 us
    unnamed x18, local copies, waits for them, and re-layouts  3.74 us
    ppermute x1, starting transfers between devices, shards(): across = [lax.ppermute(first, 'sec', facing)]  3.68 us
    ppermute x1, starting transfers between devices, shards(): across.append(lax.ppermute(second, 'sec', facing))  2.23 us
  transfers between devices with their start and end apart: 13, of which 5 were waited for; matrix products, arithmetic and copies ran while one was open for 0% of the time, Pallas kernels for 16%

profile of v6, /device:TPU:25, one launch (start us, length us, event | category | flops | bytes accessed | tf_op | source)
XLA Modules:
  0.0 97.3 jit_solution(10745315308516326803)
XLA Ops:
  0.0 2.4 %shard_map.46.own = bf16[2,512,512]{2,1,0:T(8,128)(2,1)} custom-call(bf16[2,2,512,512]{3,2,1,0:T(8,128)(2,1)} %source.3), custom_call_target="tpu_custom_call" | custom-call | bytes 4194304 | tf_op jit(solution)/shard_map/pallas_call | solution.py:23
  2.4 3.7 %collective-permute-start.1 = (bf16[2,512,512]{2,1,0:T(8,128)(2,1)}, bf16[2,512,512]{2,1,0:T(8,128)(2,1)}, u32[]{:S(2)}, u32[]{:S(2)}) collective-permute-start(bf16[2,512,512]{2,1,0:T(8,128)(2,1)} %shard_map.46.own), channel_id=1, source_target_pairs={{1,2},{3,4},{5,6},{7,8},{9,10},{11,12},{13,14},{15,16},{17,18},{19... | collective-permute-start | bytes 3145736 | tf_op jit(solution)/shard_map/ppermute | solution.py:161
  6.1 3.2 %collective-permute-start = (bf16[2,512,512]{2,1,0:T(8,128)(2,1)}, bf16[2,512,512]{2,1,0:T(8,128)(2,1)}, u32[]{:S(2)}, u32[]{:S(2)}) collective-permute-start(bf16[2,512,512]{2,1,0:T(8,128)(2,1)} %shard_map.46.own), channel_id=1, source_target_pairs={{0,1},{1,0},{2,3},{3,2},{4,5},{5,4},{6,7},{7,6},{8,9},{9,8},{10,11... | collective-permute-start | bytes 3145736 | tf_op jit(solution)/shard_map/ppermute | solution.py:165
  9.3 0.1 pad_add_fusion.at.place
  9.3 1.0 %shard_map.47 = (bf16[512,1536]{1,0:T(8,128)(2,1)S(1)}, bf16[3,512,512]{2,1,0:T(8,128)(2,1)S(1)}) custom-call(s32[3]{0:T(128)S(1)} %pad_add_fusion.at.place, bf16[3,512,512]{2,1,0:T(8,128)(2,1)S(1)} %copy-done, bf16[3,512,512]{2,1,0:T(8,128)(2,1)S(1)} %copy-done.1), custom_call_target="tpu_custom_call" | custom-call | bytes 6291456 | tf_op jit(solution)/shard_map/pallas_call | solution.py:51
  10.4 1.1 %copy-done.2 = bf16[512,1536]{1,0:T(8,128)(2,1)} copy-done((bf16[512,1536]{1,0:T(8,128)(2,1)}, bf16[512,1536]{1,0:T(8,128)(2,1)S(1)}, u32[]{:S(2)}) %copy-start.2) | copy-done | bytes 1572888
  11.5 1.2 %copy-done.6 = bf16[3,512,512]{2,1,0:T(8,128)(2,1)} copy-done((bf16[3,512,512]{2,1,0:T(8,128)(2,1)}, bf16[3,512,512]{2,1,0:T(8,128)(2,1)S(1)}, u32[]{:S(2)}) %copy-start.6) | copy-done | bytes 1572888
  12.7 2.3 %shard_map.49.own = bf16[2,512,512]{2,1,0:T(8,128)(2,1)} custom-call(bf16[2,2,512,512]{3,2,1,0:T(8,128)(2,1)} %source.3, bf16[512,1536]{1,0:T(8,128)(2,1)} %copy-done.2), custom_call_target="tpu_custom_call" | custom-call | bytes 4194304 | tf_op jit(solution)/shard_map/pallas_call | solution.py:23
  15.1 2.2 %collective-permute-start.5 = (bf16[2,512,512]{2,1,0:T(8,128)(2,1)}, bf16[2,512,512]{2,1,0:T(8,128)(2,1)}, u32[]{:S(2)}, u32[]{:S(2)}) collective-permute-start(bf16[2,512,512]{2,1,0:T(8,128)(2,1)} %shard_map.49.own), channel_id=1, source_target_pairs={{1,2},{3,4},{5,6},{7,8},{9,10},{11,12},{13,14},{15,16},{17,18},{19... | collective-permute-start | bytes 3145736 | tf_op jit(solution)/shard_map/ppermute | solution.py:163
  17.3 3.1 %collective-permute-start.4 = (bf16[2,512,512]{2,1,0:T(8,128)(2,1)}, bf16[2,512,512]{2,1,0:T(8,128)(2,1)}, u32[]{:S(2)}, u32[]{:S(2)}) collective-permute-start(bf16[2,512,512]{2,1,0:T(8,128)(2,1)} %shard_map.49.own), channel_id=1, source_target_pairs={{0,1},{1,0},{2,3},{3,2},{4,5},{5,4},{6,7},{7,6},{8,9},{9,8},{10,11... | collective-permute-start | bytes 3145736 | tf_op jit(solution)/shard_map/ppermute | solution.py:165
  20.4 0.1 reshape.10.link
  20.5 1.4 %copy-done.7 = bf16[3,512,512]{2,1,0:T(8,128)(2,1)S(1)} copy-done((bf16[3,512,512]{2,1,0:T(8,128)(2,1)S(1)}, bf16[3,512,512]{2,1,0:T(8,128)(2,1)}, u32[]{:S(2)}) %copy-start.7) | copy-done | bytes 1572888
  21.9 6.1 %shard_map.48 = (bf16[2,160,512]{2,1,0:T(8,128)(2,1)S(1)}, bf16[2,160,512]{2,1,0:T(8,128)(2,1)S(1)}, bf16[2,160,512]{2,1,0:T(8,128)(2,1)S(1)}, bf16[2,32,512]{2,1,0:T(8,128)(2,1)S(1)}) custom-call(s32[3]{0:T(128)S(1)} %pad_add_fusion.at.place, s32[30]{0:T(128)S(1)} %reshape.10.link, bf16[2,512,512]{2,1,0:T(8,128)(2,1)} %collective-permute-done.chip, ...), custom_call_target="tpu_custom_call" | custom-call | flops 3221225472 | bytes 8388608 | tf_op jit(solution)/shard_map/pallas_call | solution.py:127
  28.0 11.1 %collective-permute-start.2 = (bf16[2,160,512]{2,1,0:T(8,128)(2,1)S(1)}, bf16[2,160,512]{2,1,0:T(8,128)(2,1)S(1)}, u32[]{:S(2)}, u32[]{:S(2)}) collective-permute-start(bf16[2,160,512]{2,1,0:T(8,128)(2,1)S(1)} %get-tuple-element.18), channel_id=1, source_target_pairs={{0,32},{1,481},{2,34},{3,483},{4,36},{5,485},{6,38},{7,487},{8,40}... | collective-permute-start | bytes 983048 | tf_op jit(solution)/shard_map/ppermute | solution.py:148
  39.1 1.9 %collective-permute-start.3 = (bf16[2,160,512]{2,1,0:T(8,128)(2,1)S(1)}, bf16[2,160,512]{2,1,0:T(8,128)(2,1)S(1)}, u32[]{:S(2)}, u32[]{:S(2)}) collective-permute-start(bf16[2,160,512]{2,1,0:T(8,128)(2,1)S(1)} %get-tuple-element.19), channel_id=1, source_target_pairs={{0,480},{1,33},{2,482},{3,35},{4,484},{5,37},{6,486},{7,39},{8,488... | collective-permute-start | bytes 983048 | tf_op jit(solution)/shard_map/ppermute | solution.py:148
  41.1 6.0 %shard_map.50 = (bf16[2,160,512]{2,1,0:T(8,128)(2,1)S(1)}, bf16[2,160,512]{2,1,0:T(8,128)(2,1)S(1)}, bf16[2,160,512]{2,1,0:T(8,128)(2,1)S(1)}, bf16[2,32,512]{2,1,0:T(8,128)(2,1)S(1)}) custom-call(s32[3]{0:T(128)S(1)} %pad_add_fusion.at.place, s32[30]{0:T(128)S(1)} %reshape.10.link, bf16[2,512,512]{2,1,0:T(8,128)(2,1)} %collective-permute-done.4.chip, ...), custom_call_target="tpu_custom_call" | custom-call | flops 3221225472 | bytes 8388608 | tf_op jit(solution)/shard_map/pallas_call | solution.py:127
  47.1 4.6 %collective-permute-start.6 = (bf16[2,160,512]{2,1,0:T(8,128)(2,1)S(1)}, bf16[2,160,512]{2,1,0:T(8,128)(2,1)S(1)}, u32[]{:S(2)}, u32[]{:S(2)}) collective-permute-start(bf16[2,160,512]{2,1,0:T(8,128)(2,1)S(1)} %get-tuple-element.21), channel_id=1, source_target_pairs={{0,32},{1,481},{2,34},{3,483},{4,36},{5,485},{6,38},{7,487},{8,40}... | collective-permute-start | bytes 983048 | tf_op jit(solution)/shard_map/ppermute | solution.py:148
  51.7 1.9 %collective-permute-start.7 = (bf16[2,160,512]{2,1,0:T(8,128)(2,1)S(1)}, bf16[2,160,512]{2,1,0:T(8,128)(2,1)S(1)}, u32[]{:S(2)}, u32[]{:S(2)}) collective-permute-start(bf16[2,160,512]{2,1,0:T(8,128)(2,1)S(1)} %get-tuple-element.22), channel_id=1, source_target_pairs={{0,480},{1,33},{2,482},{3,35},{4,484},{5,37},{6,486},{7,39},{8,488... | collective-permute-start | bytes 983048 | tf_op jit(solution)/shard_map/ppermute | solution.py:148
  53.6 0.1 convert_add_fusion.1
  53.8 1.9 %collective-permute-done.6 = bf16[2,160,512]{2,1,0:T(8,128)(2,1)S(1)} collective-permute-done((bf16[2,160,512]{2,1,0:T(8,128)(2,1)S(1)}, bf16[2,160,512]{2,1,0:T(8,128)(2,1)S(1)}, u32[]{:S(2)}, u32[]{:S(2)}) %collective-permute-start.6) | collective-permute-done | bytes 327712 | tf_op jit(solution)/shard_map/ppermute | solution.py:148
  55.7 5.8 %collective-permute-done.7 = bf16[2,160,512]{2,1,0:T(8,128)(2,1)S(1)} collective-permute-done((bf16[2,160,512]{2,1,0:T(8,128)(2,1)S(1)}, bf16[2,160,512]{2,1,0:T(8,128)(2,1)S(1)}, u32[]{:S(2)}, u32[]{:S(2)}) %collective-permute-start.7) | collective-permute-done | bytes 327712 | tf_op jit(solution)/shard_map/ppermute | solution.py:148
  61.5 0.1 convert_add_fusion
  61.6 1.9 %collective-permute-start.9 = (bf16[2,2,32,512]{3,2,1,0:T(8,128)(2,1)S(1)}, bf16[2,2,32,512]{3,2,1,0:T(8,128)(2,1)S(1)}, u32[]{:S(2)}, u32[]{:S(2)}) collective-permute-start(bf16[2,2,32,512]{3,2,1,0:T(8,128)(2,1)S(1)} %get-tuple-element.27), channel_id=1, source_target_pairs={{0,416},{1,97},{2,418},{3,99},{4,420},{5,101},{6,422},{7,103},{8,4... | collective-permute-start | bytes 393224 | tf_op jit(solution)/shard_map/ppermute | solution.py:148
  63.6 6.4 %collective-permute-start.11 = (bf16[2,2,32,512]{3,2,1,0:T(8,128)(2,1)S(1)}, bf16[2,2,32,512]{3,2,1,0:T(8,128)(2,1)S(1)}, u32[]{:S(2)}, u32[]{:S(2)}) collective-permute-start(bf16[2,2,32,512]{3,2,1,0:T(8,128)(2,1)S(1)} %get-tuple-element.28), channel_id=1, source_target_pairs={{0,96},{1,417},{2,98},{3,419},{4,100},{5,421},{6,102},{7,423},{8,1... | collective-permute-start | bytes 393224 | tf_op jit(solution)/shard_map/ppermute | solution.py:148
  70.0 1.9 %collective-permute-start.8 = (bf16[2,2,32,512]{3,2,1,0:T(8,128)(2,1)S(1)}, bf16[2,2,32,512]{3,2,1,0:T(8,128)(2,1)S(1)}, u32[]{:S(2)}, u32[]{:S(2)}) collective-permute-start(bf16[2,2,32,512]{3,2,1,0:T(8,128)(2,1)S(1)} %pad_maximum_fusion.1), channel_id=1, source_target_pairs={{0,448},{1,65},{2,450},{3,67},{4,452},{5,69},{6,454},{7,71},{8,456... | collective-permute-start | bytes 393224 | tf_op jit(solution)/shard_map/ppermute | solution.py:148
  71.9 1.8 %collective-permute-done.11 = bf16[2,2,32,512]{3,2,1,0:T(8,128)(2,1)S(1)} collective-permute-done((bf16[2,2,32,512]{3,2,1,0:T(8,128)(2,1)S(1)}, bf16[2,2,32,512]{3,2,1,0:T(8,128)(2,1)S(1)}, u32[]{:S(2)}, u32[]{:S(2)}) %collective-permute-start.11) | collective-permute-done | bytes 131104 | tf_op jit(solution)/shard_map/ppermute | solution.py:148
  73.7 0.1 fusion.3
  73.8 7.6 %collective-permute-start.10 = (bf16[2,2,32,512]{3,2,1,0:T(8,128)(2,1)S(1)}, bf16[2,2,32,512]{3,2,1,0:T(8,128)(2,1)S(1)}, u32[]{:S(2)}, u32[]{:S(2)}) collective-permute-start(bf16[2,2,32,512]{3,2,1,0:T(8,128)(2,1)S(1)} %get-tuple-element.25), channel_id=1, source_target_pairs={{0,384},{1,129},{2,386},{3,131},{4,388},{5,133},{6,390},{7,135},{8... | collective-permute-start | bytes 393224 | tf_op jit(solution)/shard_map/ppermute | solution.py:148
  81.4 1.9 %collective-permute-start.12 = (bf16[2,2,32,512]{3,2,1,0:T(8,128)(2,1)S(1)}, bf16[2,2,32,512]{3,2,1,0:T(8,128)(2,1)S(1)}, u32[]{:S(2)}, u32[]{:S(2)}) collective-permute-start(bf16[2,2,32,512]{3,2,1,0:T(8,128)(2,1)S(1)} %get-tuple-element.26), channel_id=1, source_target_pairs={{0,96},{1,417},{2,98},{3,419},{4,100},{5,421},{6,102},{7,423},{8,1... | collective-permute-start | bytes 393224 | tf_op jit(solution)/shard_map/ppermute | solution.py:148
  83.3 1.6 %collective-permute-done.10 = bf16[2,2,32,512]{3,2,1,0:T(8,128)(2,1)S(1)} collective-permute-done((bf16[2,2,32,512]{3,2,1,0:T(8,128)(2,1)S(1)}, bf16[2,2,32,512]{3,2,1,0:T(8,128)(2,1)S(1)}, u32[]{:S(2)}, u32[]{:S(2)}) %collective-permute-start.10) | collective-permute-done | bytes 131104 | tf_op jit(solution)/shard_map/ppermute | solution.py:148
  84.9 11.6 %collective-permute-done.12 = bf16[2,2,32,512]{3,2,1,0:T(8,128)(2,1)S(1)} collective-permute-done((bf16[2,2,32,512]{3,2,1,0:T(8,128)(2,1)S(1)}, bf16[2,2,32,512]{3,2,1,0:T(8,128)(2,1)S(1)}, u32[]{:S(2)}, u32[]{:S(2)}) %collective-permute-start.12) | collective-permute-done | bytes 131104 | tf_op jit(solution)/shard_map/ppermute | solution.py:148
  96.5 0.8 fusion.6
  (25 shorter events, 0.1 us)
Async XLA Ops:
  0.0 9.3 %copy-start.1 = (bf16[3,512,512]{2,1,0:T(8,128)(2,1)S(1)}, bf16[3,512,512]{2,1,0:T(8,128)(2,1)}, u32[]{:S(2)}) copy-start(bf16[3,512,512]{2,1,0:T(8,128)(2,1)} %right.1) | copy-start | bytes 4718596
  0.0 9.3 %copy-start = (bf16[3,512,512]{2,1,0:T(8,128)(2,1)S(1)}, bf16[3,512,512]{2,1,0:T(8,128)(2,1)}, u32[]{:S(2)}) copy-start(bf16[3,512,512]{2,1,0:T(8,128)(2,1)} %left.1) | copy-start | bytes 4718596
  2.4 18.1 %collective-permute-start.1 = (bf16[2,512,512]{2,1,0:T(8,128)(2,1)}, bf16[2,512,512]{2,1,0:T(8,128)(2,1)}, u32[]{:S(2)}, u32[]{:S(2)}) collective-permute-start(bf16[2,512,512]{2,1,0:T(8,128)(2,1)} %shard_map.46.own), channel_id=1, source_target_pairs={{1,2},{3,4},{5,6},{7,8},{9,10},{11,12},{13,14},{15,16},{17,18},{19... | collective-permute-start | bytes 3145736 | tf_op jit(solution)/shard_map/ppermute | solution.py:161
  6.1 14.4 %collective-permute-start = (bf16[2,512,512]{2,1,0:T(8,128)(2,1)}, bf16[2,512,512]{2,1,0:T(8,128)(2,1)}, u32[]{:S(2)}, u32[]{:S(2)}) collective-permute-start(bf16[2,512,512]{2,1,0:T(8,128)(2,1)} %shard_map.46.own), channel_id=1, source_target_pairs={{0,1},{1,0},{2,3},{3,2},{4,5},{5,4},{6,7},{7,6},{8,9},{9,8},{10,11... | collective-permute-start | bytes 3145736 | tf_op jit(solution)/shard_map/ppermute | solution.py:165
  10.4 1.1 %copy-start.2 = (bf16[512,1536]{1,0:T(8,128)(2,1)}, bf16[512,1536]{1,0:T(8,128)(2,1)S(1)}, u32[]{:S(2)}) copy-start(bf16[512,1536]{1,0:T(8,128)(2,1)S(1)} %get-tuple-element.16.left.rest_0_) | copy-start | bytes 4718596
  11.5 1.2 %copy-start.6 = (bf16[3,512,512]{2,1,0:T(8,128)(2,1)}, bf16[3,512,512]{2,1,0:T(8,128)(2,1)S(1)}, u32[]{:S(2)}) copy-start(bf16[3,512,512]{2,1,0:T(8,128)(2,1)S(1)} %get-tuple-element.15.right) | copy-start | bytes 4718596
  12.7 7.7 %copy-start.8 = (s32[3,2,5]{2,1,0:T(2,128)S(1)}, s32[3,2,5]{2,1,0:T(2,128)}, u32[]{:S(2)}) copy-start(s32[3,2,5]{2,1,0:T(2,128)} %param.7) | copy-start | bytes 364
  12.7 7.8 %copy-start.3 = (bf16[512,1536]{1,0:T(8,128)(2,1)S(1)}, bf16[512,1536]{1,0:T(8,128)(2,1)}, u32[]{:S(2)}) copy-start(bf16[512,1536]{1,0:T(8,128)(2,1)} %copy-done.2) | copy-start | bytes 4718596
  12.7 7.8 %copy-start.4 = (bf16[2,512,512]{2,1,0:T(8,128)(2,1)S(1)}, bf16[2,512,512]{2,1,0:T(8,128)(2,1)}, u32[]{:S(2)}) copy-start(bf16[2,512,512]{2,1,0:T(8,128)(2,1)} %shard_map.46.own) | copy-start | bytes 3145732
  15.1 26.0 %collective-permute-start.5 = (bf16[2,512,512]{2,1,0:T(8,128)(2,1)}, bf16[2,512,512]{2,1,0:T(8,128)(2,1)}, u32[]{:S(2)}, u32[]{:S(2)}) collective-permute-start(bf16[2,512,512]{2,1,0:T(8,128)(2,1)} %shard_map.49.own), channel_id=1, source_target_pairs={{1,2},{3,4},{5,6},{7,8},{9,10},{11,12},{13,14},{15,16},{17,18},{19... | collective-permute-start | bytes 3145736 | tf_op jit(solution)/shard_map/ppermute | solution.py:163
  17.3 23.7 %collective-permute-start.4 = (bf16[2,512,512]{2,1,0:T(8,128)(2,1)}, bf16[2,512,512]{2,1,0:T(8,128)(2,1)}, u32[]{:S(2)}, u32[]{:S(2)}) collective-permute-start(bf16[2,512,512]{2,1,0:T(8,128)(2,1)} %shard_map.49.own), channel_id=1, source_target_pairs={{0,1},{1,0},{2,3},{3,2},{4,5},{5,4},{6,7},{7,6},{8,9},{9,8},{10,11... | collective-permute-start | bytes 3145736 | tf_op jit(solution)/shard_map/ppermute | solution.py:165
  20.5 1.4 %copy-start.7 = (bf16[3,512,512]{2,1,0:T(8,128)(2,1)S(1)}, bf16[3,512,512]{2,1,0:T(8,128)(2,1)}, u32[]{:S(2)}) copy-start(bf16[3,512,512]{2,1,0:T(8,128)(2,1)} %copy-done.6) | copy-start | bytes 4718596
  21.9 19.1 %copy-start.5 = (bf16[2,512,512]{2,1,0:T(8,128)(2,1)S(1)}, bf16[2,512,512]{2,1,0:T(8,128)(2,1)}, u32[]{:S(2)}) copy-start(bf16[2,512,512]{2,1,0:T(8,128)(2,1)} %shard_map.49.own) | copy-start | bytes 3145732
  28.0 25.6 %collective-permute-start.2 = (bf16[2,160,512]{2,1,0:T(8,128)(2,1)S(1)}, bf16[2,160,512]{2,1,0:T(8,128)(2,1)S(1)}, u32[]{:S(2)}, u32[]{:S(2)}) collective-permute-start(bf16[2,160,512]{2,1,0:T(8,128)(2,1)S(1)} %get-tuple-element.18), channel_id=1, source_target_pairs={{0,32},{1,481},{2,34},{3,483},{4,36},{5,485},{6,38},{7,487},{8,40}... | collective-permute-start | bytes 983048 | tf_op jit(solution)/shard_map/ppermute | solution.py:148
  39.1 14.5 %collective-permute-start.3 = (bf16[2,160,512]{2,1,0:T(8,128)(2,1)S(1)}, bf16[2,160,512]{2,1,0:T(8,128)(2,1)S(1)}, u32[]{:S(2)}, u32[]{:S(2)}) collective-permute-start(bf16[2,160,512]{2,1,0:T(8,128)(2,1)S(1)} %get-tuple-element.19), channel_id=1, source_target_pairs={{0,480},{1,33},{2,482},{3,35},{4,484},{5,37},{6,486},{7,39},{8,488... | collective-permute-start | bytes 983048 | tf_op jit(solution)/shard_map/ppermute | solution.py:148
  47.1 8.6 %collective-permute-start.6 = (bf16[2,160,512]{2,1,0:T(8,128)(2,1)S(1)}, bf16[2,160,512]{2,1,0:T(8,128)(2,1)S(1)}, u32[]{:S(2)}, u32[]{:S(2)}) collective-permute-start(bf16[2,160,512]{2,1,0:T(8,128)(2,1)S(1)} %get-tuple-element.21), channel_id=1, source_target_pairs={{0,32},{1,481},{2,34},{3,483},{4,36},{5,485},{6,38},{7,487},{8,40}... | collective-permute-start | bytes 983048 | tf_op jit(solution)/shard_map/ppermute | solution.py:148
  51.7 9.8 %collective-permute-start.7 = (bf16[2,160,512]{2,1,0:T(8,128)(2,1)S(1)}, bf16[2,160,512]{2,1,0:T(8,128)(2,1)S(1)}, u32[]{:S(2)}, u32[]{:S(2)}) collective-permute-start(bf16[2,160,512]{2,1,0:T(8,128)(2,1)S(1)} %get-tuple-element.22), channel_id=1, source_target_pairs={{0,480},{1,33},{2,482},{3,35},{4,484},{5,37},{6,486},{7,39},{8,488... | collective-permute-start | bytes 983048 | tf_op jit(solution)/shard_map/ppermute | solution.py:148
  61.6 10.3 %collective-permute-start.9 = (bf16[2,2,32,512]{3,2,1,0:T(8,128)(2,1)S(1)}, bf16[2,2,32,512]{3,2,1,0:T(8,128)(2,1)S(1)}, u32[]{:S(2)}, u32[]{:S(2)}) collective-permute-start(bf16[2,2,32,512]{3,2,1,0:T(8,128)(2,1)S(1)} %get-tuple-element.27), channel_id=1, source_target_pairs={{0,416},{1,97},{2,418},{3,99},{4,420},{5,101},{6,422},{7,103},{8,4... | collective-permute-start | bytes 393224 | tf_op jit(solution)/shard_map/ppermute | solution.py:148
  63.6 10.1 %collective-permute-start.11 = (bf16[2,2,32,512]{3,2,1,0:T(8,128)(2,1)S(1)}, bf16[2,2,32,512]{3,2,1,0:T(8,128)(2,1)S(1)}, u32[]{:S(2)}, u32[]{:S(2)}) collective-permute-start(bf16[2,2,32,512]{3,2,1,0:T(8,128)(2,1)S(1)} %get-tuple-element.28), channel_id=1, source_target_pairs={{0,96},{1,417},{2,98},{3,419},{4,100},{5,421},{6,102},{7,423},{8,1... | collective-permute-start | bytes 393224 | tf_op jit(solution)/shard_map/ppermute | solution.py:148
  70.0 13.3 %collective-permute-start.8 = (bf16[2,2,32,512]{3,2,1,0:T(8,128)(2,1)S(1)}, bf16[2,2,32,512]{3,2,1,0:T(8,128)(2,1)S(1)}, u32[]{:S(2)}, u32[]{:S(2)}) collective-permute-start(bf16[2,2,32,512]{3,2,1,0:T(8,128)(2,1)S(1)} %pad_maximum_fusion.1), channel_id=1, source_target_pairs={{0,448},{1,65},{2,450},{3,67},{4,452},{5,69},{6,454},{7,71},{8,456... | collective-permute-start | bytes 393224 | tf_op jit(solution)/shard_map/ppermute | solution.py:148
  73.8 11.1 %collective-permute-start.10 = (bf16[2,2,32,512]{3,2,1,0:T(8,128)(2,1)S(1)}, bf16[2,2,32,512]{3,2,1,0:T(8,128)(2,1)S(1)}, u32[]{:S(2)}, u32[]{:S(2)}) collective-permute-start(bf16[2,2,32,512]{3,2,1,0:T(8,128)(2,1)S(1)} %get-tuple-element.25), channel_id=1, source_target_pairs={{0,384},{1,129},{2,386},{3,131},{4,388},{5,133},{6,390},{7,135},{8... | collective-permute-start | bytes 393224 | tf_op jit(solution)/shard_map/ppermute | solution.py:148
  81.4 15.2 %collective-permute-start.12 = (bf16[2,2,32,512]{3,2,1,0:T(8,128)(2,1)S(1)}, bf16[2,2,32,512]{3,2,1,0:T(8,128)(2,1)S(1)}, u32[]{:S(2)}, u32[]{:S(2)}) collective-permute-start(bf16[2,2,32,512]{3,2,1,0:T(8,128)(2,1)S(1)} %get-tuple-element.26), channel_id=1, source_target_pairs={{0,96},{1,417},{2,98},{3,419},{4,100},{5,421},{6,102},{7,423},{8,1... | collective-permute-start | bytes 393224 | tf_op jit(solution)/shard_map/ppermute | solution.py:148

commit v7 on v3

--- a/solution.py
+++ b/solution.py
@@ -86,7 +86,7 @@
                 columns = pl.ds(column, wide)
                 a0, a1 = (across[i, rows, columns].astype(F32) for i in range(2))
                 o0, o1 = (own[i, rows, columns].astype(F32) for i in range(2))
-                c0, c1 = (chip[v, i, rows, columns].astype(F32) for i in range(2))
+                c0, c1 = (chip[i, rows, columns].astype(F32) for i in range(2))
                 fifth = (jnp.where(first_core, a1, c1), jnp.where(first_core, c0, a0))
                 for j, blocks in enumerate(((a0, o0, o1, c0, fifth[0]), (a1, o0, o1, c1, fifth[1]))):
                     for k in range(terms):
@@ -161,13 +161,13 @@
     facing += [(b, a) for a, b in facing]
     own = split(psi)
     across = [lax.ppermute(block, "sec", facing) for block in own]
-    chip = lax.ppermute(psi, "sec", [(i, i ^ 1) for i in range(count)])
+    chip = [lax.ppermute(block, "sec", [(i, i ^ 1) for i in range(count)]) for block in own]
 
     left, right = arrange(at, left_op, right_op)
     totals, opposites = [], []
     for v in range(vectors):
         up, down, mine, opposite = partials(
-            v, at, link.reshape(-1), across[v], own[v], chip, right, left
+            v, at, link.reshape(-1), across[v], own[v], chip[v], right, left
         )
         total = mine.astype(F32) + shift(up, 1).astype(F32) + shift(down, -1).astype(F32)
         totals.append(total.reshape(2, len(LEADERS), share, -1))

time: 98.6 us -> 95.9 us (0.973)
  the two profiles are of different devices: /device:TPU:14 before, /device:TPU:24 now
where the time goes in v7:
time: 95.9 us; the launch traced here: 95.3 us
  starting transfers between devices  51.3 us (53%)
  waiting for transfers between devices  24.9 us (26%)
  Pallas kernels  16 us (17%)
  local copies, waits for them, and re-layouts  1.71 us (2%)
  other arithmetic  1.18 us (1%)
    ppermute x9, starting transfers between devices, shift(): return lax.ppermute(x, ('op', 'sec'), pairs)  39.8 us
    ppermute x9, waiting for transfers between devices, shift(): return lax.ppermute(x, ('op', 'sec'), pairs)  20.5 us
    pallas_call x2, Pallas kernels, partials(): pl.pallas_call(lambda *refs: kernel(v, *refs), in_specs=[scalars, scalars...  11.9 us
    ppermute x2, starting transfers between devices, shards(): across = [lax.ppermute(block, 'sec', facing) for block in own]  7.67 us
    ppermute x2, waiting for transfers between devices, shards(): across = [lax.ppermute(block, 'sec', facing) for block in own]  4.35 us
    ppermute x2, starting transfers between devices, shards(): lax.ppermute(block, 'sec', [(i, i ^ 1) for i in range(count)])  3.84 us
    pallas_call x1, Pallas kernels, split(): pl.pallas_call(split_kernel, in_specs=[pl.BlockSpec(memory_space=pl.ANY)]...  3 us
  transfers between devices with their start and end apart: 13, of which 6 were waited for; matrix products, arithmetic and copies ran while one was open for 1% of the time, Pallas kernels for 14%

profile of v7, /device:TPU:24, one launch (start us, length us, event | category | flops | bytes accessed | tf_op | source)
XLA Modules:
  0.0 95.3 jit_solution(13607782950973360478)
XLA Ops:
  0.0 3.0 %shard_map.46 = (bf16[2,512,512]{2,1,0:T(8,128)(2,1)}, bf16[2,512,512]{2,1,0:T(8,128)(2,1)}) custom-call(bf16[2,2,512,512]{3,2,1,0:T(8,128)(2,1)} %psi.1), custom_call_target="tpu_custom_call" | custom-call | bytes 4194304 | tf_op jit(solution)/shard_map/pallas_call | solution.py:25
  3.0 4.3 %collective-permute-start = (bf16[2,512,512]{2,1,0:T(8,128)(2,1)}, bf16[2,512,512]{2,1,0:T(8,128)(2,1)}, u32[]{:S(2)}, u32[]{:S(2)}) collective-permute-start(bf16[2,512,512]{2,1,0:T(8,128)(2,1)} %get-tuple-element.17.refs_3_), channel_id=1, source_target_pairs={{1,2},{3,4},{5,6},{7,8},{9,10},{11,12},{13,14},{15,16},{17,18},{19... | collective-permute-start | bytes 3145736 | tf_op jit(solution)/shard_map/ppermute | solution.py:163
  7.3 1.9 %collective-permute-start.1 = (bf16[2,512,512]{2,1,0:T(8,128)(2,1)}, bf16[2,512,512]{2,1,0:T(8,128)(2,1)}, u32[]{:S(2)}, u32[]{:S(2)}) collective-permute-start(bf16[2,512,512]{2,1,0:T(8,128)(2,1)} %get-tuple-element.17.refs_3_), channel_id=1, source_target_pairs={{0,1},{1,0},{2,3},{3,2},{4,5},{5,4},{6,7},{7,6},{8,9},{9,8},{10,11... | collective-permute-start | bytes 3145736 | tf_op jit(solution)/shard_map/ppermute | solution.py:164
  9.2 3.4 %collective-permute-start.4 = (bf16[2,512,512]{2,1,0:T(8,128)(2,1)}, bf16[2,512,512]{2,1,0:T(8,128)(2,1)S(1)}, u32[]{:S(2)}, u32[]{:S(2)}) collective-permute-start(bf16[2,512,512]{2,1,0:T(8,128)(2,1)} %get-tuple-element.23.refs_3_), channel_id=1, source_target_pairs={{1,2},{3,4},{5,6},{7,8},{9,10},{11,12},{13,14},{15,16},{17,18},{19... | collective-permute-start | bytes 3145736 | tf_op jit(solution)/shard_map/ppermute | solution.py:163
  12.6 1.9 %collective-permute-start.5 = (bf16[2,512,512]{2,1,0:T(8,128)(2,1)}, bf16[2,512,512]{2,1,0:T(8,128)(2,1)}, u32[]{:S(2)}, u32[]{:S(2)}) collective-permute-start(bf16[2,512,512]{2,1,0:T(8,128)(2,1)} %get-tuple-element.23.refs_3_), channel_id=1, source_target_pairs={{0,1},{1,0},{2,3},{3,2},{4,5},{5,4},{6,7},{7,6},{8,9},{9,8},{10,11... | collective-permute-start | bytes 3145736 | tf_op jit(solution)/shard_map/ppermute | solution.py:164
  14.6 0.1 reshape.10.refs_1_
  14.7 0.1 pad_add_fusion.at.refs_0_
  14.7 1.4 %copy-done.1 = bf16[3,512,512]{2,1,0:T(8,128)(2,1)S(1)} copy-done((bf16[3,512,512]{2,1,0:T(8,128)(2,1)S(1)}, bf16[3,512,512]{2,1,0:T(8,128)(2,1)}, u32[]{:S(2)}) %copy-start.1) | copy-done | bytes 1572888
  16.2 1.0 %shard_map.47 = (bf16[512,1536]{1,0:T(8,128)(2,1)S(1)}, bf16[3,512,512]{2,1,0:T(8,128)(2,1)S(1)}) custom-call(s32[3]{0:T(128)S(1)} %pad_add_fusion.at.refs_0_, bf16[3,512,512]{2,1,0:T(8,128)(2,1)S(1)} %copy-done, bf16[3,512,512]{2,1,0:T(8,128)(2,1)S(1)} %copy-done.1), custom_call_target="tpu_custom_call" | custom-call | bytes 6291456 | tf_op jit(solution)/shard_map/pallas_call | solution.py:53
  17.2 4.3 %collective-permute-done.refs_2_ = bf16[2,512,512]{2,1,0:T(8,128)(2,1)} collective-permute-done((bf16[2,512,512]{2,1,0:T(8,128)(2,1)}, bf16[2,512,512]{2,1,0:T(8,128)(2,1)}, u32[]{:S(2)}, u32[]{:S(2)}) %collective-permute-start) | collective-permute-done | bytes 1048608 | tf_op jit(solution)/shard_map/ppermute | solution.py:163
  21.6 0.0 collective-permute-done.1.refs_4_
  21.6 6.2 %shard_map.48 = (bf16[2,160,512]{2,1,0:T(8,128)(2,1)S(1)}, bf16[2,160,512]{2,1,0:T(8,128)(2,1)S(1)}, bf16[2,160,512]{2,1,0:T(8,128)(2,1)S(1)}, bf16[2,32,512]{2,1,0:T(8,128)(2,1)S(1)}) custom-call(s32[3]{0:T(128)S(1)} %pad_add_fusion.at.refs_0_, s32[30]{0:T(128)S(1)} %reshape.10.refs_1_, bf16[2,512,512]{2,1,0:T(8,128)(2,1)} %collective-permute-done.refs_2_, ...), custom_call_target="tpu_custom_call" | custom-call | flops 3221225472 | bytes 8388608 | tf_op jit(solution)/shard_map/pallas_call | solution.py:129
  27.7 3.8 %collective-permute-start.2 = (bf16[2,160,512]{2,1,0:T(8,128)(2,1)S(1)}, bf16[2,160,512]{2,1,0:T(8,128)(2,1)S(1)}, u32[]{:S(2)}, u32[]{:S(2)}) collective-permute-start(bf16[2,160,512]{2,1,0:T(8,128)(2,1)S(1)} %get-tuple-element.21), channel_id=1, source_target_pairs={{0,32},{1,481},{2,34},{3,483},{4,36},{5,485},{6,38},{7,487},{8,40}... | collective-permute-start | bytes 983048 | tf_op jit(solution)/shard_map/ppermute | solution.py:150
  31.6 9.5 %collective-permute-start.3 = (bf16[2,160,512]{2,1,0:T(8,128)(2,1)S(1)}, bf16[2,160,512]{2,1,0:T(8,128)(2,1)S(1)}, u32[]{:S(2)}, u32[]{:S(2)}) collective-permute-start(bf16[2,160,512]{2,1,0:T(8,128)(2,1)S(1)} %get-tuple-element.22), channel_id=1, source_target_pairs={{0,480},{1,33},{2,482},{3,35},{4,484},{5,37},{6,486},{7,39},{8,488... | collective-permute-start | bytes 983048 | tf_op jit(solution)/shard_map/ppermute | solution.py:150
  41.1 0.0 collective-permute-done.4.refs_2_
  41.1 0.0 collective-permute-done.5.refs_4_
  41.1 5.8 %shard_map.49 = (bf16[2,160,512]{2,1,0:T(8,128)(2,1)S(1)}, bf16[2,160,512]{2,1,0:T(8,128)(2,1)S(1)}, bf16[2,160,512]{2,1,0:T(8,128)(2,1)S(1)}, bf16[2,32,512]{2,1,0:T(8,128)(2,1)S(1)}) custom-call(s32[3]{0:T(128)S(1)} %pad_add_fusion.at.refs_0_, s32[30]{0:T(128)S(1)} %reshape.10.refs_1_, bf16[2,512,512]{2,1,0:T(8,128)(2,1)S(1)} %collective-permute-done.4.refs_2_, ...), custom_call_target="tpu_custom_call" | custom-call | flops 3221225472 | bytes 8388608 | tf_op jit(solution)/shard_map/pallas_call | solution.py:129
  46.9 1.9 %collective-permute-start.6 = (bf16[2,160,512]{2,1,0:T(8,128)(2,1)S(1)}, bf16[2,160,512]{2,1,0:T(8,128)(2,1)S(1)}, u32[]{:S(2)}, u32[]{:S(2)}) collective-permute-start(bf16[2,160,512]{2,1,0:T(8,128)(2,1)S(1)} %get-tuple-element.25), channel_id=1, source_target_pairs={{0,32},{1,481},{2,34},{3,483},{4,36},{5,485},{6,38},{7,487},{8,40}... | collective-permute-start | bytes 983048 | tf_op jit(solution)/shard_map/ppermute | solution.py:150
  48.8 5.1 %collective-permute-start.7 = (bf16[2,160,512]{2,1,0:T(8,128)(2,1)S(1)}, bf16[2,160,512]{2,1,0:T(8,128)(2,1)S(1)}, u32[]{:S(2)}, u32[]{:S(2)}) collective-permute-start(bf16[2,160,512]{2,1,0:T(8,128)(2,1)S(1)} %get-tuple-element.26), channel_id=1, source_target_pairs={{0,480},{1,33},{2,482},{3,35},{4,484},{5,37},{6,486},{7,39},{8,488... | collective-permute-start | bytes 983048 | tf_op jit(solution)/shard_map/ppermute | solution.py:150
  54.0 3.2 %collective-permute-start.8 = (bf16[2,2,32,512]{3,2,1,0:T(8,128)(2,1)S(1)}, bf16[2,2,32,512]{3,2,1,0:T(8,128)(2,1)S(1)}, u32[]{:S(2)}, u32[]{:S(2)}) collective-permute-start(bf16[2,2,32,512]{3,2,1,0:T(8,128)(2,1)S(1)} %pad_maximum_fusion), channel_id=1, source_target_pairs={{0,448},{1,65},{2,450},{3,67},{4,452},{5,69},{6,454},{7,71},{8,456... | collective-permute-start | bytes 393224 | tf_op jit(solution)/shard_map/ppermute | solution.py:150
  57.2 0.1 convert_add_fusion.1
  57.3 1.8 %collective-permute-done.6 = bf16[2,160,512]{2,1,0:T(8,128)(2,1)S(1)} collective-permute-done((bf16[2,160,512]{2,1,0:T(8,128)(2,1)S(1)}, bf16[2,160,512]{2,1,0:T(8,128)(2,1)S(1)}, u32[]{:S(2)}, u32[]{:S(2)}) %collective-permute-start.6) | collective-permute-done | bytes 327712 | tf_op jit(solution)/shard_map/ppermute | solution.py:150
  59.1 0.1 convert_add_fusion
  59.3 2.5 %collective-permute-done.8 = bf16[2,2,32,512]{3,2,1,0:T(8,128)(2,1)S(1)} collective-permute-done((bf16[2,2,32,512]{3,2,1,0:T(8,128)(2,1)S(1)}, bf16[2,2,32,512]{3,2,1,0:T(8,128)(2,1)S(1)}, u32[]{:S(2)}, u32[]{:S(2)}) %collective-permute-start.8) | collective-permute-done | bytes 131104 | tf_op jit(solution)/shard_map/ppermute | solution.py:150
  61.9 3.7 %collective-permute-start.9 = (bf16[2,2,32,512]{3,2,1,0:T(8,128)(2,1)S(1)}, bf16[2,2,32,512]{3,2,1,0:T(8,128)(2,1)S(1)}, u32[]{:S(2)}, u32[]{:S(2)}) collective-permute-start(bf16[2,2,32,512]{3,2,1,0:T(8,128)(2,1)S(1)} %fusion.2), channel_id=1, source_target_pairs={{0,416},{1,97},{2,418},{3,99},{4,420},{5,101},{6,422},{7,103},{8,4... | collective-permute-start | bytes 393224 | tf_op jit(solution)/shard_map/ppermute | solution.py:150
  65.6 3.9 %collective-permute-start.11 = (bf16[2,2,32,512]{3,2,1,0:T(8,128)(2,1)S(1)}, bf16[2,2,32,512]{3,2,1,0:T(8,128)(2,1)S(1)}, u32[]{:S(2)}, u32[]{:S(2)}) collective-permute-start(bf16[2,2,32,512]{3,2,1,0:T(8,128)(2,1)S(1)} %pad_maximum_fusion.1), channel_id=1, source_target_pairs={{0,96},{1,417},{2,98},{3,419},{4,100},{5,421},{6,102},{7,423},{8,1... | collective-permute-start | bytes 393224 | tf_op jit(solution)/shard_map/ppermute | solution.py:150
  69.6 6.8 %collective-permute-done.9 = bf16[2,2,32,512]{3,2,1,0:T(8,128)(2,1)S(1)} collective-permute-done((bf16[2,2,32,512]{3,2,1,0:T(8,128)(2,1)S(1)}, bf16[2,2,32,512]{3,2,1,0:T(8,128)(2,1)S(1)}, u32[]{:S(2)}, u32[]{:S(2)}) %collective-permute-start.9) | collective-permute-done | bytes 131104 | tf_op jit(solution)/shard_map/ppermute | solution.py:150
  76.4 6.4 %collective-permute-start.10 = (bf16[2,2,32,512]{3,2,1,0:T(8,128)(2,1)S(1)}, bf16[2,2,32,512]{3,2,1,0:T(8,128)(2,1)S(1)}, u32[]{:S(2)}, u32[]{:S(2)}) collective-permute-start(bf16[2,2,32,512]{3,2,1,0:T(8,128)(2,1)S(1)} %fusion.1), channel_id=1, source_target_pairs={{0,416},{1,97},{2,418},{3,99},{4,420},{5,101},{6,422},{7,103},{8,4... | collective-permute-start | bytes 393224 | tf_op jit(solution)/shard_map/ppermute | solution.py:150
  82.8 2.3 %collective-permute-start.12 = (bf16[2,2,32,512]{3,2,1,0:T(8,128)(2,1)S(1)}, bf16[2,2,32,512]{3,2,1,0:T(8,128)(2,1)S(1)}, u32[]{:S(2)}, u32[]{:S(2)}) collective-permute-start(bf16[2,2,32,512]{3,2,1,0:T(8,128)(2,1)S(1)} %fusion.3), channel_id=1, source_target_pairs={{0,96},{1,417},{2,98},{3,419},{4,100},{5,421},{6,102},{7,423},{8,1... | collective-permute-start | bytes 393224 | tf_op jit(solution)/shard_map/ppermute | solution.py:150
  85.1 6.0 %collective-permute-done.10 = bf16[2,2,32,512]{3,2,1,0:T(8,128)(2,1)S(1)} collective-permute-done((bf16[2,2,32,512]{3,2,1,0:T(8,128)(2,1)S(1)}, bf16[2,2,32,512]{3,2,1,0:T(8,128)(2,1)S(1)}, u32[]{:S(2)}, u32[]{:S(2)}) %collective-permute-start.10) | collective-permute-done | bytes 131104 | tf_op jit(solution)/shard_map/ppermute | solution.py:150
  91.1 3.4 %collective-permute-done.12 = bf16[2,2,32,512]{3,2,1,0:T(8,128)(2,1)S(1)} collective-permute-done((bf16[2,2,32,512]{3,2,1,0:T(8,128)(2,1)S(1)}, bf16[2,2,32,512]{3,2,1,0:T(8,128)(2,1)S(1)}, u32[]{:S(2)}, u32[]{:S(2)}) %collective-permute-start.12) | collective-permute-done | bytes 131104 | tf_op jit(solution)/shard_map/ppermute | solution.py:150
  94.6 0.7 fusion
  (25 shorter events, 0.3 us)
Async XLA Ops:
  0.0 14.6 %copy-start.4 = (s32[3,2,5]{2,1,0:T(2,128)S(1)}, s32[3,2,5]{2,1,0:T(2,128)}, u32[]{:S(2)}) copy-start(s32[3,2,5]{2,1,0:T(2,128)} %param.7) | copy-start | bytes 364
  0.0 14.7 %copy-start = (bf16[3,512,512]{2,1,0:T(8,128)(2,1)S(1)}, bf16[3,512,512]{2,1,0:T(8,128)(2,1)}, u32[]{:S(2)}) copy-start(bf16[3,512,512]{2,1,0:T(8,128)(2,1)} %left.1) | copy-start | bytes 4718596
  3.0 18.5 %collective-permute-start = (bf16[2,512,512]{2,1,0:T(8,128)(2,1)}, bf16[2,512,512]{2,1,0:T(8,128)(2,1)}, u32[]{:S(2)}, u32[]{:S(2)}) collective-permute-start(bf16[2,512,512]{2,1,0:T(8,128)(2,1)} %get-tuple-element.17.refs_3_), channel_id=1, source_target_pairs={{1,2},{3,4},{5,6},{7,8},{9,10},{11,12},{13,14},{15,16},{17,18},{19... | collective-permute-start | bytes 3145736 | tf_op jit(solution)/shard_map/ppermute | solution.py:163
  7.3 14.3 %collective-permute-start.1 = (bf16[2,512,512]{2,1,0:T(8,128)(2,1)}, bf16[2,512,512]{2,1,0:T(8,128)(2,1)}, u32[]{:S(2)}, u32[]{:S(2)}) collective-permute-start(bf16[2,512,512]{2,1,0:T(8,128)(2,1)} %get-tuple-element.17.refs_3_), channel_id=1, source_target_pairs={{0,1},{1,0},{2,3},{3,2},{4,5},{5,4},{6,7},{7,6},{8,9},{9,8},{10,11... | collective-permute-start | bytes 3145736 | tf_op jit(solution)/shard_map/ppermute | solution.py:164
  9.2 31.8 %collective-permute-start.4 = (bf16[2,512,512]{2,1,0:T(8,128)(2,1)}, bf16[2,512,512]{2,1,0:T(8,128)(2,1)S(1)}, u32[]{:S(2)}, u32[]{:S(2)}) collective-permute-start(bf16[2,512,512]{2,1,0:T(8,128)(2,1)} %get-tuple-element.23.refs_3_), channel_id=1, source_target_pairs={{1,2},{3,4},{5,6},{7,8},{9,10},{11,12},{13,14},{15,16},{17,18},{19... | collective-permute-start | bytes 3145736 | tf_op jit(solution)/shard_map/ppermute | solution.py:163
  12.6 28.4 %collective-permute-start.5 = (bf16[2,512,512]{2,1,0:T(8,128)(2,1)}, bf16[2,512,512]{2,1,0:T(8,128)(2,1)}, u32[]{:S(2)}, u32[]{:S(2)}) collective-permute-start(bf16[2,512,512]{2,1,0:T(8,128)(2,1)} %get-tuple-element.23.refs_3_), channel_id=1, source_target_pairs={{0,1},{1,0},{2,3},{3,2},{4,5},{5,4},{6,7},{7,6},{8,9},{9,8},{10,11... | collective-permute-start | bytes 3145736 | tf_op jit(solution)/shard_map/ppermute | solution.py:164
  14.7 1.4 %copy-start.1 = (bf16[3,512,512]{2,1,0:T(8,128)(2,1)S(1)}, bf16[3,512,512]{2,1,0:T(8,128)(2,1)}, u32[]{:S(2)}) copy-start(bf16[3,512,512]{2,1,0:T(8,128)(2,1)} %right.1) | copy-start | bytes 4718596
  16.2 5.4 %copy-start.3 = (bf16[2,512,512]{2,1,0:T(8,128)(2,1)S(1)}, bf16[2,512,512]{2,1,0:T(8,128)(2,1)}, u32[]{:S(2)}) copy-start(bf16[2,512,512]{2,1,0:T(8,128)(2,1)} %get-tuple-element.17.refs_3_) | copy-start | bytes 3145732
  21.6 19.5 %copy-start.2 = (bf16[2,512,512]{2,1,0:T(8,128)(2,1)S(1)}, bf16[2,512,512]{2,1,0:T(8,128)(2,1)}, u32[]{:S(2)}) copy-start(bf16[2,512,512]{2,1,0:T(8,128)(2,1)} %get-tuple-element.23.refs_3_) | copy-start | bytes 3145732
  27.7 29.4 %collective-permute-start.2 = (bf16[2,160,512]{2,1,0:T(8,128)(2,1)S(1)}, bf16[2,160,512]{2,1,0:T(8,128)(2,1)S(1)}, u32[]{:S(2)}, u32[]{:S(2)}) collective-permute-start(bf16[2,160,512]{2,1,0:T(8,128)(2,1)S(1)} %get-tuple-element.21), channel_id=1, source_target_pairs={{0,32},{1,481},{2,34},{3,483},{4,36},{5,485},{6,38},{7,487},{8,40}... | collective-permute-start | bytes 983048 | tf_op jit(solution)/shard_map/ppermute | solution.py:150
  31.6 25.6 %collective-permute-start.3 = (bf16[2,160,512]{2,1,0:T(8,128)(2,1)S(1)}, bf16[2,160,512]{2,1,0:T(8,128)(2,1)S(1)}, u32[]{:S(2)}, u32[]{:S(2)}) collective-permute-start(bf16[2,160,512]{2,1,0:T(8,128)(2,1)S(1)} %get-tuple-element.22), channel_id=1, source_target_pairs={{0,480},{1,33},{2,482},{3,35},{4,484},{5,37},{6,486},{7,39},{8,488... | collective-permute-start | bytes 983048 | tf_op jit(solution)/shard_map/ppermute | solution.py:150
  46.9 12.2 %collective-permute-start.6 = (bf16[2,160,512]{2,1,0:T(8,128)(2,1)S(1)}, bf16[2,160,512]{2,1,0:T(8,128)(2,1)S(1)}, u32[]{:S(2)}, u32[]{:S(2)}) collective-permute-start(bf16[2,160,512]{2,1,0:T(8,128)(2,1)S(1)} %get-tuple-element.25), channel_id=1, source_target_pairs={{0,32},{1,481},{2,34},{3,483},{4,36},{5,485},{6,38},{7,487},{8,40}... | collective-permute-start | bytes 983048 | tf_op jit(solution)/shard_map/ppermute | solution.py:150
  48.8 10.3 %collective-permute-start.7 = (bf16[2,160,512]{2,1,0:T(8,128)(2,1)S(1)}, bf16[2,160,512]{2,1,0:T(8,128)(2,1)S(1)}, u32[]{:S(2)}, u32[]{:S(2)}) collective-permute-start(bf16[2,160,512]{2,1,0:T(8,128)(2,1)S(1)} %get-tuple-element.26), channel_id=1, source_target_pairs={{0,480},{1,33},{2,482},{3,35},{4,484},{5,37},{6,486},{7,39},{8,488... | collective-permute-start | bytes 983048 | tf_op jit(solution)/shard_map/ppermute | solution.py:150
  54.0 7.9 %collective-permute-start.8 = (bf16[2,2,32,512]{3,2,1,0:T(8,128)(2,1)S(1)}, bf16[2,2,32,512]{3,2,1,0:T(8,128)(2,1)S(1)}, u32[]{:S(2)}, u32[]{:S(2)}) collective-permute-start(bf16[2,2,32,512]{3,2,1,0:T(8,128)(2,1)S(1)} %pad_maximum_fusion), channel_id=1, source_target_pairs={{0,448},{1,65},{2,450},{3,67},{4,452},{5,69},{6,454},{7,71},{8,456... | collective-permute-start | bytes 393224 | tf_op jit(solution)/shard_map/ppermute | solution.py:150
  61.9 14.5 %collective-permute-start.9 = (bf16[2,2,32,512]{3,2,1,0:T(8,128)(2,1)S(1)}, bf16[2,2,32,512]{3,2,1,0:T(8,128)(2,1)S(1)}, u32[]{:S(2)}, u32[]{:S(2)}) collective-permute-start(bf16[2,2,32,512]{3,2,1,0:T(8,128)(2,1)S(1)} %fusion.2), channel_id=1, source_target_pairs={{0,416},{1,97},{2,418},{3,99},{4,420},{5,101},{6,422},{7,103},{8,4... | collective-permute-start | bytes 393224 | tf_op jit(solution)/shard_map/ppermute | solution.py:150
  65.6 17.2 %collective-permute-start.11 = (bf16[2,2,32,512]{3,2,1,0:T(8,128)(2,1)S(1)}, bf16[2,2,32,512]{3,2,1,0:T(8,128)(2,1)S(1)}, u32[]{:S(2)}, u32[]{:S(2)}) collective-permute-start(bf16[2,2,32,512]{3,2,1,0:T(8,128)(2,1)S(1)} %pad_maximum_fusion.1), channel_id=1, source_target_pairs={{0,96},{1,417},{2,98},{3,419},{4,100},{5,421},{6,102},{7,423},{8,1... | collective-permute-start | bytes 393224 | tf_op jit(solution)/shard_map/ppermute | solution.py:150
  76.4 14.7 %collective-permute-start.10 = (bf16[2,2,32,512]{3,2,1,0:T(8,128)(2,1)S(1)}, bf16[2,2,32,512]{3,2,1,0:T(8,128)(2,1)S(1)}, u32[]{:S(2)}, u32[]{:S(2)}) collective-permute-start(bf16[2,2,32,512]{3,2,1,0:T(8,128)(2,1)S(1)} %fusion.1), channel_id=1, source_target_pairs={{0,416},{1,97},{2,418},{3,99},{4,420},{5,101},{6,422},{7,103},{8,4... | collective-permute-start | bytes 393224 | tf_op jit(solution)/shard_map/ppermute | solution.py:150
  82.8 11.7 %collective-permute-start.12 = (bf16[2,2,32,512]{3,2,1,0:T(8,128)(2,1)S(1)}, bf16[2,2,32,512]{3,2,1,0:T(8,128)(2,1)S(1)}, u32[]{:S(2)}, u32[]{:S(2)}) collective-permute-start(bf16[2,2,32,512]{3,2,1,0:T(8,128)(2,1)S(1)} %fusion.3), channel_id=1, source_target_pairs={{0,96},{1,417},{2,98},{3,419},{4,100},{5,421},{6,102},{7,423},{8,1... | collective-permute-start | bytes 393224 | tf_op jit(solution)/shard_map/ppermute | solution.py:150

commit v8 on v7

--- a/solution.py
+++ b/solution.py
@@ -8,7 +8,7 @@
 F32, BF16 = jnp.float32, jnp.bfloat16
 RING = 16
 LEADERS = (0, 3, -3, 6, -6)
-ORDER = [1 - p for p in LEADERS] + [-1 - p for p in LEADERS] + [-p for p in LEADERS] + [8]
+ORDER = [1 - p for p in LEADERS] + [-1 - p for p in LEADERS] + [8] + [-p for p in LEADERS]
 
 
 def split_kernel(psi, *rest):
@@ -63,11 +63,11 @@
     )(at, left, right)
 
 
-def kernel(v, place, link, across, own, chip, right, left, up, down, mine, opposite, combined, halved):
+def kernel(v, place, link, across, own, chip, right, left, up, down, opposite, halved, combined):
     terms, size = right.shape[0], right.shape[1]
     first_core = place[0] % 2 == 0
     lowest, highest = place[0] == 0, place[0] == place[1] - 1
-    half, tall, wide, high = size // 2, 16, 256, 128
+    half, tall, wide = size // 2, 16, 256
 
     def weight(k, j, if_first, if_second):
         reach = jnp.where(first_core, if_first, if_second)
@@ -106,13 +106,19 @@
     combine(1)
     multiply_right(0)
     multiply_right(1)
+    multiply_left(left, halved, (up, down, opposite), 0)
+
+
+def multiply_left(left, halved, outs, first):
+    last = first + sum(out.shape[1] for out in outs)
     for j in range(2):
-        for top in range(0, size, high):
+        for top in range(first, last, 128):
+            high = min(128, last - top)
             sums = jnp.dot(
                 left[pl.ds(top, high), :], halved[j], preferred_element_type=F32
             ).astype(BF16)
-            start = 0
-            for out in (up, down, mine, opposite):
+            start = first
+            for out in outs:
                 end = start + out.shape[1]
                 low, stop = max(top, start), min(top + high, end)
                 if low < stop:
@@ -120,20 +126,40 @@
                 start = end
 
 
+def mine_kernel(left, halved, out):
+    multiply_left(left, halved, (out,), left.shape[0] - out.shape[1])
+
+
+def mine_shares(left, halved):
+    size = halved.shape[2]
+    rows = len(LEADERS) * (size // RING)
+    whole = pl.BlockSpec(memory_space=pltpu.VMEM)
+    return pl.pallas_call(
+        mine_kernel,
+        in_specs=[whole] * 2,
+        out_specs=whole,
+        out_shape=jax.ShapeDtypeStruct((2, rows, size), BF16),
+        compiler_params=pltpu.CompilerParams(vmem_limit_bytes=16 * 2**20),
+        cost_estimate=pl.CostEstimate(
+            flops=4 * rows * halved.shape[1] * size, bytes_accessed=4 * 2**20, transcendentals=0
+        ),
+    )(left, halved)
+
+
 def partials(v, place, link, across, own, chip, right, left):
     terms, size = right.shape[0], right.shape[1]
     share = size // RING
     whole = pl.BlockSpec(memory_space=pltpu.VMEM)
     scalars = pl.BlockSpec(memory_space=pltpu.SMEM)
-    counts = [len(LEADERS)] * 3 + [1]
+    shapes = [(2, n * share, size) for n in (len(LEADERS), len(LEADERS), 1)]
+    shapes.append((2, terms * size, size))
     return pl.pallas_call(
         lambda *refs: kernel(v, *refs),
         in_specs=[scalars, scalars] + [whole] * 5,
         out_specs=[whole] * 4,
-        out_shape=[jax.ShapeDtypeStruct((2, n * share, size), BF16) for n in counts],
+        out_shape=[jax.ShapeDtypeStruct(shape, BF16) for shape in shapes],
         scratch_shapes=[
             pltpu.VMEM((2, 2 * terms, size // 2, size), BF16),
-            pltpu.VMEM((2, terms * size, size), BF16),
         ],
         compiler_params=pltpu.CompilerParams(vmem_limit_bytes=32 * 2**20),
         cost_estimate=pl.CostEstimate(
@@ -166,9 +192,10 @@
     left, right = arrange(at, left_op, right_op)
     totals, opposites = [], []
     for v in range(vectors):
-        up, down, mine, opposite = partials(
+        up, down, opposite, halved = partials(
             v, at, link.reshape(-1), across[v], own[v], chip[v], right, left
         )
+        mine = mine_shares(left, halved)
         total = mine.astype(F32) + shift(up, 1).astype(F32) + shift(down, -1).astype(F32)
         totals.append(total.reshape(2, len(LEADERS), share, -1))
         opposites.append(opposite)

time: 95.9 us -> 95 us (level)
  waiting for transfers between devices: 24.9 us -> 22.6 us
  Pallas kernels: 16 us -> 17.2 us
    ppermute x9, waiting for transfers between devices: 20.5 us -> 18.3 us  [shift(): return lax.ppermute(x, ('op', 'sec'), pairs)]
    pallas_call x0 -> x2, Pallas kernels: none -> 2.16 us  [mine_shares(): pl.pallas_call(mine_kernel, in_specs=[whole] * 2, out_specs=whole, out_sh...]
  transfers between devices with their start and end apart: 13 -> 13, of which waited for: 6 -> 5; matrix products, arithmetic and copies ran while one was open for 1% -> 1% of each run, Pallas kernels for 14% -> 15%
where the time goes in v8:
time: 95 us; the launch traced here: 94.4 us
  starting transfers between devices  51.4 us (54%)
  waiting for transfers between devices  22.6 us (24%)
  Pallas kernels  17.2 us (18%)
  local copies, waits for them, and re-layouts  1.71 us (2%)
  other arithmetic  1.18 us (1%)
    ppermute x9, starting transfers between devices, shift(): return lax.ppermute(x, ('op', 'sec'), pairs)  39.8 us
    ppermute x9, waiting for transfers between devices, shift(): return lax.ppermute(x, ('op', 'sec'), pairs)  18.3 us
    pallas_call x2, Pallas kernels, partials(): pl.pallas_call(lambda *refs: kernel(v, *refs), in_specs=[scalars, scalars...  11 us
    ppermute x2, starting transfers between devices, shards(): across = [lax.ppermute(block, 'sec', facing) for block in own]  7.67 us
    ppermute x2, waiting for transfers between devices, shards(): across = [lax.ppermute(block, 'sec', facing) for block in own]  4.35 us
    ppermute x2, starting transfers between devices, shards(): lax.ppermute(block, 'sec', [(i, i ^ 1) for i in range(count)])  3.84 us
    pallas_call x1, Pallas kernels, split(): pl.pallas_call(split_kernel, in_specs=[pl.BlockSpec(memory_space=pl.ANY)]...  3 us
    pallas_call x2, Pallas kernels, mine_shares(): pl.pallas_call(mine_kernel, in_specs=[whole] * 2, out_specs=whole, out_sh...  2.16 us
  transfers between devices with their start and end apart: 13, of which 5 were waited for; matrix products, arithmetic and copies ran while one was open for 1% of the time, Pallas kernels for 15%

profile of v8, /device:TPU:24, one launch (start us, length us, event | category | flops | bytes accessed | tf_op | source)
XLA Modules:
  0.0 94.4 jit_solution(14183704373210877999)
XLA Ops:
  0.0 3.0 %shard_map.47 = (bf16[2,512,512]{2,1,0:T(8,128)(2,1)}, bf16[2,512,512]{2,1,0:T(8,128)(2,1)}) custom-call(bf16[2,2,512,512]{3,2,1,0:T(8,128)(2,1)} %psi.1), custom_call_target="tpu_custom_call" | custom-call | bytes 4194304 | tf_op jit(solution)/shard_map/pallas_call | solution.py:25
  3.0 4.3 %collective-permute-start = (bf16[2,512,512]{2,1,0:T(8,128)(2,1)}, bf16[2,512,512]{2,1,0:T(8,128)(2,1)}, u32[]{:S(2)}, u32[]{:S(2)}) collective-permute-start(bf16[2,512,512]{2,1,0:T(8,128)(2,1)} %get-tuple-element.18.refs_3_), channel_id=1, source_target_pairs={{1,2},{3,4},{5,6},{7,8},{9,10},{11,12},{13,14},{15,16},{17,18},{19... | collective-permute-start | bytes 3145736 | tf_op jit(solution)/shard_map/ppermute | solution.py:189
  7.3 1.9 %collective-permute-start.1 = (bf16[2,512,512]{2,1,0:T(8,128)(2,1)}, bf16[2,512,512]{2,1,0:T(8,128)(2,1)}, u32[]{:S(2)}, u32[]{:S(2)}) collective-permute-start(bf16[2,512,512]{2,1,0:T(8,128)(2,1)} %get-tuple-element.18.refs_3_), channel_id=1, source_target_pairs={{0,1},{1,0},{2,3},{3,2},{4,5},{5,4},{6,7},{7,6},{8,9},{9,8},{10,11... | collective-permute-start | bytes 3145736 | tf_op jit(solution)/shard_map/ppermute | solution.py:190
  9.2 3.4 %collective-permute-start.4 = (bf16[2,512,512]{2,1,0:T(8,128)(2,1)}, bf16[2,512,512]{2,1,0:T(8,128)(2,1)S(1)}, u32[]{:S(2)}, u32[]{:S(2)}) collective-permute-start(bf16[2,512,512]{2,1,0:T(8,128)(2,1)} %get-tuple-element.23.refs_3_), channel_id=1, source_target_pairs={{1,2},{3,4},{5,6},{7,8},{9,10},{11,12},{13,14},{15,16},{17,18},{19... | collective-permute-start | bytes 3145736 | tf_op jit(solution)/shard_map/ppermute | solution.py:189
  12.6 1.9 %collective-permute-start.5 = (bf16[2,512,512]{2,1,0:T(8,128)(2,1)}, bf16[2,512,512]{2,1,0:T(8,128)(2,1)}, u32[]{:S(2)}, u32[]{:S(2)}) collective-permute-start(bf16[2,512,512]{2,1,0:T(8,128)(2,1)} %get-tuple-element.23.refs_3_), channel_id=1, source_target_pairs={{0,1},{1,0},{2,3},{3,2},{4,5},{5,4},{6,7},{7,6},{8,9},{9,8},{10,11... | collective-permute-start | bytes 3145736 | tf_op jit(solution)/shard_map/ppermute | solution.py:190
  14.6 0.1 reshape.10.refs_1_
  14.7 0.1 pad_add_fusion.at.refs_0_
  14.7 1.4 %copy-done.1 = bf16[3,512,512]{2,1,0:T(8,128)(2,1)S(1)} copy-done((bf16[3,512,512]{2,1,0:T(8,128)(2,1)S(1)}, bf16[3,512,512]{2,1,0:T(8,128)(2,1)}, u32[]{:S(2)}) %copy-start.1) | copy-done | bytes 1572888
  16.2 1.0 %shard_map.46 = (bf16[512,1536]{1,0:T(8,128)(2,1)S(1)}, bf16[3,512,512]{2,1,0:T(8,128)(2,1)S(1)}) custom-call(s32[3]{0:T(128)S(1)} %pad_add_fusion.at.refs_0_, bf16[3,512,512]{2,1,0:T(8,128)(2,1)S(1)} %copy-done, bf16[3,512,512]{2,1,0:T(8,128)(2,1)S(1)} %copy-done.1), custom_call_target="tpu_custom_call" | custom-call | bytes 6291456 | tf_op jit(solution)/shard_map/pallas_call | solution.py:53
  17.2 4.3 %collective-permute-done.refs_2_ = bf16[2,512,512]{2,1,0:T(8,128)(2,1)} collective-permute-done((bf16[2,512,512]{2,1,0:T(8,128)(2,1)}, bf16[2,512,512]{2,1,0:T(8,128)(2,1)}, u32[]{:S(2)}, u32[]{:S(2)}) %collective-permute-start) | collective-permute-done | bytes 1048608 | tf_op jit(solution)/shard_map/ppermute | solution.py:189
  21.6 0.0 collective-permute-done.1.refs_4_
  21.6 5.7 %shard_map.48 = (bf16[2,160,512]{2,1,0:T(8,128)(2,1)S(1)}, bf16[2,160,512]{2,1,0:T(8,128)(2,1)S(1)}, bf16[2,32,512]{2,1,0:T(8,128)(2,1)S(1)}, bf16[2,1536,512]{2,1,0:T(8,128)(2,1)S(1)}) custom-call(s32[3]{0:T(128)S(1)} %pad_add_fusion.at.refs_0_, s32[30]{0:T(128)S(1)} %reshape.10.refs_1_, bf16[2,512,512]{2,1,0:T(8,128)(2,1)} %collective-permute-done.refs_2_, ...), custom_call_target="tpu_custom_call" | custom-call | flops 3221225472 | bytes 8388608 | tf_op jit(solution)/shard_map/pallas_call | solution.py:156
  27.3 3.8 %collective-permute-start.2 = (bf16[2,160,512]{2,1,0:T(8,128)(2,1)S(1)}, bf16[2,160,512]{2,1,0:T(8,128)(2,1)S(1)}, u32[]{:S(2)}, u32[]{:S(2)}) collective-permute-start(bf16[2,160,512]{2,1,0:T(8,128)(2,1)S(1)} %get-tuple-element.21), channel_id=1, source_target_pairs={{0,32},{1,481},{2,34},{3,483},{4,36},{5,485},{6,38},{7,487},{8,40}... | collective-permute-start | bytes 983048 | tf_op jit(solution)/shard_map/ppermute | solution.py:176
  31.1 9.5 %collective-permute-start.3 = (bf16[2,160,512]{2,1,0:T(8,128)(2,1)S(1)}, bf16[2,160,512]{2,1,0:T(8,128)(2,1)S(1)}, u32[]{:S(2)}, u32[]{:S(2)}) collective-permute-start(bf16[2,160,512]{2,1,0:T(8,128)(2,1)S(1)} %get-tuple-element.22), channel_id=1, source_target_pairs={{0,480},{1,33},{2,482},{3,35},{4,484},{5,37},{6,486},{7,39},{8,488... | collective-permute-start | bytes 983048 | tf_op jit(solution)/shard_map/ppermute | solution.py:176
  40.6 5.3 %shard_map.50 = (bf16[2,160,512]{2,1,0:T(8,128)(2,1)S(1)}, bf16[2,160,512]{2,1,0:T(8,128)(2,1)S(1)}, bf16[2,32,512]{2,1,0:T(8,128)(2,1)S(1)}, bf16[2,1536,512]{2,1,0:T(8,128)(2,1)S(1)}) custom-call(s32[3]{0:T(128)S(1)} %pad_add_fusion.at.refs_0_, s32[30]{0:T(128)S(1)} %reshape.10.refs_1_, bf16[2,512,512]{2,1,0:T(8,128)(2,1)S(1)} %collective-permute-done.4.refs_2_, ...), custom_call_target="tpu_custom_call" | custom-call | flops 3221225472 | bytes 8388608 | tf_op jit(solution)/shard_map/pallas_call | solution.py:156
  46.0 1.9 %collective-permute-start.6 = (bf16[2,160,512]{2,1,0:T(8,128)(2,1)S(1)}, bf16[2,160,512]{2,1,0:T(8,128)(2,1)S(1)}, u32[]{:S(2)}, u32[]{:S(2)}) collective-permute-start(bf16[2,160,512]{2,1,0:T(8,128)(2,1)S(1)} %get-tuple-element.25), channel_id=1, source_target_pairs={{0,32},{1,481},{2,34},{3,483},{4,36},{5,485},{6,38},{7,487},{8,40}... | collective-permute-start | bytes 983048 | tf_op jit(solution)/shard_map/ppermute | solution.py:176
  47.9 5.1 %collective-permute-start.7 = (bf16[2,160,512]{2,1,0:T(8,128)(2,1)S(1)}, bf16[2,160,512]{2,1,0:T(8,128)(2,1)S(1)}, u32[]{:S(2)}, u32[]{:S(2)}) collective-permute-start(bf16[2,160,512]{2,1,0:T(8,128)(2,1)S(1)} %get-tuple-element.26), channel_id=1, source_target_pairs={{0,480},{1,33},{2,482},{3,35},{4,484},{5,37},{6,486},{7,39},{8,488... | collective-permute-start | bytes 983048 | tf_op jit(solution)/shard_map/ppermute | solution.py:176
  53.1 3.2 %collective-permute-start.8 = (bf16[2,2,32,512]{3,2,1,0:T(8,128)(2,1)S(1)}, bf16[2,2,32,512]{3,2,1,0:T(8,128)(2,1)S(1)}, u32[]{:S(2)}, u32[]{:S(2)}) collective-permute-start(bf16[2,2,32,512]{3,2,1,0:T(8,128)(2,1)S(1)} %pad_maximum_fusion), channel_id=1, source_target_pairs={{0,448},{1,65},{2,450},{3,67},{4,452},{5,69},{6,454},{7,71},{8,456... | collective-permute-start | bytes 393224 | tf_op jit(solution)/shard_map/ppermute | solution.py:176
  56.2 1.1 %shard_map.49 = bf16[2,160,512]{2,1,0:T(8,128)(2,1)S(1)} custom-call(bf16[512,1536]{1,0:T(8,128)(2,1)S(1)} %get-tuple-element.17.refs_6_.left, bf16[2,1536,512]{2,1,0:T(8,128)(2,1)S(1)} %get-tuple-element.20.halved), custom_call_target="tpu_custom_call" | custom-call | flops 503316480 | bytes 4194304 | tf_op jit(solution)/shard_map/pallas_call | solution.py:137
  57.3 1.1 %shard_map.51 = bf16[2,160,512]{2,1,0:T(8,128)(2,1)S(1)} custom-call(bf16[512,1536]{1,0:T(8,128)(2,1)S(1)} %get-tuple-element.17.refs_6_.left, bf16[2,1536,512]{2,1,0:T(8,128)(2,1)S(1)} %get-tuple-element.24.halved), custom_call_target="tpu_custom_call" | custom-call | flops 503316480 | bytes 4194304 | tf_op jit(solution)/shard_map/pallas_call | solution.py:137
  58.4 0.0 collective-permute-done.3
  58.4 0.1 convert_add_fusion.1
  58.6 0.1 convert_add_fusion
  58.9 2.1 %collective-permute-done.8 = bf16[2,2,32,512]{3,2,1,0:T(8,128)(2,1)S(1)} collective-permute-done((bf16[2,2,32,512]{3,2,1,0:T(8,128)(2,1)S(1)}, bf16[2,2,32,512]{3,2,1,0:T(8,128)(2,1)S(1)}, u32[]{:S(2)}, u32[]{:S(2)}) %collective-permute-start.8) | collective-permute-done | bytes 131104 | tf_op jit(solution)/shard_map/ppermute | solution.py:176
  61.0 3.7 %collective-permute-start.9 = (bf16[2,2,32,512]{3,2,1,0:T(8,128)(2,1)S(1)}, bf16[2,2,32,512]{3,2,1,0:T(8,128)(2,1)S(1)}, u32[]{:S(2)}, u32[]{:S(2)}) collective-permute-start(bf16[2,2,32,512]{3,2,1,0:T(8,128)(2,1)S(1)} %fusion.2), channel_id=1, source_target_pairs={{0,416},{1,97},{2,418},{3,99},{4,420},{5,101},{6,422},{7,103},{8,4... | collective-permute-start | bytes 393224 | tf_op jit(solution)/shard_map/ppermute | solution.py:176
  64.7 3.9 %collective-permute-start.11 = (bf16[2,2,32,512]{3,2,1,0:T(8,128)(2,1)S(1)}, bf16[2,2,32,512]{3,2,1,0:T(8,128)(2,1)S(1)}, u32[]{:S(2)}, u32[]{:S(2)}) collective-permute-start(bf16[2,2,32,512]{3,2,1,0:T(8,128)(2,1)S(1)} %pad_maximum_fusion.1), channel_id=1, source_target_pairs={{0,96},{1,417},{2,98},{3,419},{4,100},{5,421},{6,102},{7,423},{8,1... | collective-permute-start | bytes 393224 | tf_op jit(solution)/shard_map/ppermute | solution.py:176
  68.7 6.7 %collective-permute-done.9 = bf16[2,2,32,512]{3,2,1,0:T(8,128)(2,1)S(1)} collective-permute-done((bf16[2,2,32,512]{3,2,1,0:T(8,128)(2,1)S(1)}, bf16[2,2,32,512]{3,2,1,0:T(8,128)(2,1)S(1)}, u32[]{:S(2)}, u32[]{:S(2)}) %collective-permute-start.9) | collective-permute-done | bytes 131104 | tf_op jit(solution)/shard_map/ppermute | solution.py:176
  75.4 6.5 %collective-permute-start.10 = (bf16[2,2,32,512]{3,2,1,0:T(8,128)(2,1)S(1)}, bf16[2,2,32,512]{3,2,1,0:T(8,128)(2,1)S(1)}, u32[]{:S(2)}, u32[]{:S(2)}) collective-permute-start(bf16[2,2,32,512]{3,2,1,0:T(8,128)(2,1)S(1)} %fusion.1), channel_id=1, source_target_pairs={{0,416},{1,97},{2,418},{3,99},{4,420},{5,101},{6,422},{7,103},{8,4... | collective-permute-start | bytes 393224 | tf_op jit(solution)/shard_map/ppermute | solution.py:176
  82.0 2.2 %collective-permute-start.12 = (bf16[2,2,32,512]{3,2,1,0:T(8,128)(2,1)S(1)}, bf16[2,2,32,512]{3,2,1,0:T(8,128)(2,1)S(1)}, u32[]{:S(2)}, u32[]{:S(2)}) collective-permute-start(bf16[2,2,32,512]{3,2,1,0:T(8,128)(2,1)S(1)} %fusion.3), channel_id=1, source_target_pairs={{0,96},{1,417},{2,98},{3,419},{4,100},{5,421},{6,102},{7,423},{8,1... | collective-permute-start | bytes 393224 | tf_op jit(solution)/shard_map/ppermute | solution.py:176
  84.2 6.1 %collective-permute-done.10 = bf16[2,2,32,512]{3,2,1,0:T(8,128)(2,1)S(1)} collective-permute-done((bf16[2,2,32,512]{3,2,1,0:T(8,128)(2,1)S(1)}, bf16[2,2,32,512]{3,2,1,0:T(8,128)(2,1)S(1)}, u32[]{:S(2)}, u32[]{:S(2)}) %collective-permute-start.10) | collective-permute-done | bytes 131104 | tf_op jit(solution)/shard_map/ppermute | solution.py:176
  90.3 3.4 %collective-permute-done.12 = bf16[2,2,32,512]{3,2,1,0:T(8,128)(2,1)S(1)} collective-permute-done((bf16[2,2,32,512]{3,2,1,0:T(8,128)(2,1)S(1)}, bf16[2,2,32,512]{3,2,1,0:T(8,128)(2,1)S(1)}, u32[]{:S(2)}, u32[]{:S(2)}) %collective-permute-start.12) | collective-permute-done | bytes 131104 | tf_op jit(solution)/shard_map/ppermute | solution.py:176
  93.7 0.7 fusion
  (27 shorter events, 0.4 us)
Async XLA Ops:
  0.0 14.6 %copy-start.4 = (s32[3,2,5]{2,1,0:T(2,128)S(1)}, s32[3,2,5]{2,1,0:T(2,128)}, u32[]{:S(2)}) copy-start(s32[3,2,5]{2,1,0:T(2,128)} %param.7) | copy-start | bytes 364
  0.0 14.7 %copy-start = (bf16[3,512,512]{2,1,0:T(8,128)(2,1)S(1)}, bf16[3,512,512]{2,1,0:T(8,128)(2,1)}, u32[]{:S(2)}) copy-start(bf16[3,512,512]{2,1,0:T(8,128)(2,1)} %left.1) | copy-start | bytes 4718596
  3.0 18.5 %collective-permute-start = (bf16[2,512,512]{2,1,0:T(8,128)(2,1)}, bf16[2,512,512]{2,1,0:T(8,128)(2,1)}, u32[]{:S(2)}, u32[]{:S(2)}) collective-permute-start(bf16[2,512,512]{2,1,0:T(8,128)(2,1)} %get-tuple-element.18.refs_3_), channel_id=1, source_target_pairs={{1,2},{3,4},{5,6},{7,8},{9,10},{11,12},{13,14},{15,16},{17,18},{19... | collective-permute-start | bytes 3145736 | tf_op jit(solution)/shard_map/ppermute | solution.py:189
  7.3 14.3 %collective-permute-start.1 = (bf16[2,512,512]{2,1,0:T(8,128)(2,1)}, bf16[2,512,512]{2,1,0:T(8,128)(2,1)}, u32[]{:S(2)}, u32[]{:S(2)}) collective-permute-start(bf16[2,512,512]{2,1,0:T(8,128)(2,1)} %get-tuple-element.18.refs_3_), channel_id=1, source_target_pairs={{0,1},{1,0},{2,3},{3,2},{4,5},{5,4},{6,7},{7,6},{8,9},{9,8},{10,11... | collective-permute-start | bytes 3145736 | tf_op jit(solution)/shard_map/ppermute | solution.py:190
  9.2 31.4 %collective-permute-start.4 = (bf16[2,512,512]{2,1,0:T(8,128)(2,1)}, bf16[2,512,512]{2,1,0:T(8,128)(2,1)S(1)}, u32[]{:S(2)}, u32[]{:S(2)}) collective-permute-start(bf16[2,512,512]{2,1,0:T(8,128)(2,1)} %get-tuple-element.23.refs_3_), channel_id=1, source_target_pairs={{1,2},{3,4},{5,6},{7,8},{9,10},{11,12},{13,14},{15,16},{17,18},{19... | collective-permute-start | bytes 3145736 | tf_op jit(solution)/shard_map/ppermute | solution.py:189
  12.6 28.0 %collective-permute-start.5 = (bf16[2,512,512]{2,1,0:T(8,128)(2,1)}, bf16[2,512,512]{2,1,0:T(8,128)(2,1)}, u32[]{:S(2)}, u32[]{:S(2)}) collective-permute-start(bf16[2,512,512]{2,1,0:T(8,128)(2,1)} %get-tuple-element.23.refs_3_), channel_id=1, source_target_pairs={{0,1},{1,0},{2,3},{3,2},{4,5},{5,4},{6,7},{7,6},{8,9},{9,8},{10,11... | collective-permute-start | bytes 3145736 | tf_op jit(solution)/shard_map/ppermute | solution.py:190
  14.7 1.4 %copy-start.1 = (bf16[3,512,512]{2,1,0:T(8,128)(2,1)S(1)}, bf16[3,512,512]{2,1,0:T(8,128)(2,1)}, u32[]{:S(2)}) copy-start(bf16[3,512,512]{2,1,0:T(8,128)(2,1)} %right.1) | copy-start | bytes 4718596
  16.2 5.4 %copy-start.3 = (bf16[2,512,512]{2,1,0:T(8,128)(2,1)S(1)}, bf16[2,512,512]{2,1,0:T(8,128)(2,1)}, u32[]{:S(2)}) copy-start(bf16[2,512,512]{2,1,0:T(8,128)(2,1)} %get-tuple-element.18.refs_3_) | copy-start | bytes 3145732
  21.6 19.1 %copy-start.2 = (bf16[2,512,512]{2,1,0:T(8,128)(2,1)S(1)}, bf16[2,512,512]{2,1,0:T(8,128)(2,1)}, u32[]{:S(2)}) copy-start(bf16[2,512,512]{2,1,0:T(8,128)(2,1)} %get-tuple-element.23.refs_3_) | copy-start | bytes 3145732
  27.3 31.1 %collective-permute-start.2 = (bf16[2,160,512]{2,1,0:T(8,128)(2,1)S(1)}, bf16[2,160,512]{2,1,0:T(8,128)(2,1)S(1)}, u32[]{:S(2)}, u32[]{:S(2)}) collective-permute-start(bf16[2,160,512]{2,1,0:T(8,128)(2,1)S(1)} %get-tuple-element.21), channel_id=1, source_target_pairs={{0,32},{1,481},{2,34},{3,483},{4,36},{5,485},{6,38},{7,487},{8,40}... | collective-permute-start | bytes 983048 | tf_op jit(solution)/shard_map/ppermute | solution.py:176
  31.1 27.3 %collective-permute-start.3 = (bf16[2,160,512]{2,1,0:T(8,128)(2,1)S(1)}, bf16[2,160,512]{2,1,0:T(8,128)(2,1)S(1)}, u32[]{:S(2)}, u32[]{:S(2)}) collective-permute-start(bf16[2,160,512]{2,1,0:T(8,128)(2,1)S(1)} %get-tuple-element.22), channel_id=1, source_target_pairs={{0,480},{1,33},{2,482},{3,35},{4,484},{5,37},{6,486},{7,39},{8,488... | collective-permute-start | bytes 983048 | tf_op jit(solution)/shard_map/ppermute | solution.py:176
  46.0 12.6 %collective-permute-start.6 = (bf16[2,160,512]{2,1,0:T(8,128)(2,1)S(1)}, bf16[2,160,512]{2,1,0:T(8,128)(2,1)S(1)}, u32[]{:S(2)}, u32[]{:S(2)}) collective-permute-start(bf16[2,160,512]{2,1,0:T(8,128)(2,1)S(1)} %get-tuple-element.25), channel_id=1, source_target_pairs={{0,32},{1,481},{2,34},{3,483},{4,36},{5,485},{6,38},{7,487},{8,40}... | collective-permute-start | bytes 983048 | tf_op jit(solution)/shard_map/ppermute | solution.py:176
  47.9 10.7 %collective-permute-start.7 = (bf16[2,160,512]{2,1,0:T(8,128)(2,1)S(1)}, bf16[2,160,512]{2,1,0:T(8,128)(2,1)S(1)}, u32[]{:S(2)}, u32[]{:S(2)}) collective-permute-start(bf16[2,160,512]{2,1,0:T(8,128)(2,1)S(1)} %get-tuple-element.26), channel_id=1, source_target_pairs={{0,480},{1,33},{2,482},{3,35},{4,484},{5,37},{6,486},{7,39},{8,488... | collective-permute-start | bytes 983048 | tf_op jit(solution)/shard_map/ppermute | solution.py:176
  53.1 7.9 %collective-permute-start.8 = (bf16[2,2,32,512]{3,2,1,0:T(8,128)(2,1)S(1)}, bf16[2,2,32,512]{3,2,1,0:T(8,128)(2,1)S(1)}, u32[]{:S(2)}, u32[]{:S(2)}) collective-permute-start(bf16[2,2,32,512]{3,2,1,0:T(8,128)(2,1)S(1)} %pad_maximum_fusion), channel_id=1, source_target_pairs={{0,448},{1,65},{2,450},{3,67},{4,452},{5,69},{6,454},{7,71},{8,456... | collective-permute-start | bytes 393224 | tf_op jit(solution)/shard_map/ppermute | solution.py:176
  61.0 14.4 %collective-permute-start.9 = (bf16[2,2,32,512]{3,2,1,0:T(8,128)(2,1)S(1)}, bf16[2,2,32,512]{3,2,1,0:T(8,128)(2,1)S(1)}, u32[]{:S(2)}, u32[]{:S(2)}) collective-permute-start(bf16[2,2,32,512]{3,2,1,0:T(8,128)(2,1)S(1)} %fusion.2), channel_id=1, source_target_pairs={{0,416},{1,97},{2,418},{3,99},{4,420},{5,101},{6,422},{7,103},{8,4... | collective-permute-start | bytes 393224 | tf_op jit(solution)/shard_map/ppermute | solution.py:176
  64.7 17.2 %collective-permute-start.11 = (bf16[2,2,32,512]{3,2,1,0:T(8,128)(2,1)S(1)}, bf16[2,2,32,512]{3,2,1,0:T(8,128)(2,1)S(1)}, u32[]{:S(2)}, u32[]{:S(2)}) collective-permute-start(bf16[2,2,32,512]{3,2,1,0:T(8,128)(2,1)S(1)} %pad_maximum_fusion.1), channel_id=1, source_target_pairs={{0,96},{1,417},{2,98},{3,419},{4,100},{5,421},{6,102},{7,423},{8,1... | collective-permute-start | bytes 393224 | tf_op jit(solution)/shard_map/ppermute | solution.py:176
  75.4 14.9 %collective-permute-start.10 = (bf16[2,2,32,512]{3,2,1,0:T(8,128)(2,1)S(1)}, bf16[2,2,32,512]{3,2,1,0:T(8,128)(2,1)S(1)}, u32[]{:S(2)}, u32[]{:S(2)}) collective-permute-start(bf16[2,2,32,512]{3,2,1,0:T(8,128)(2,1)S(1)} %fusion.1), channel_id=1, source_target_pairs={{0,416},{1,97},{2,418},{3,99},{4,420},{5,101},{6,422},{7,103},{8,4... | collective-permute-start | bytes 393224 | tf_op jit(solution)/shard_map/ppermute | solution.py:176
  82.0 11.7 %collective-permute-start.12 = (bf16[2,2,32,512]{3,2,1,0:T(8,128)(2,1)S(1)}, bf16[2,2,32,512]{3,2,1,0:T(8,128)(2,1)S(1)}, u32[]{:S(2)}, u32[]{:S(2)}) collective-permute-start(bf16[2,2,32,512]{3,2,1,0:T(8,128)(2,1)S(1)} %fusion.3), channel_id=1, source_target_pairs={{0,96},{1,417},{2,98},{3,419},{4,100},{5,421},{6,102},{7,423},{8,1... | collective-permute-start | bytes 393224 | tf_op jit(solution)/shard_map/ppermute | solution.py:176

commit v9 on v8

--- a/solution.py
+++ b/solution.py
@@ -12,22 +12,41 @@
 
 
 def split_kernel(psi, *rest):
-    outs, sems = rest[:-1], rest[-1]
-    copies = [pltpu.make_async_copy(psi.at[v], out, sems.at[v]) for v, out in enumerate(outs)]
-    for copy in copies:
-        copy.start()
-    for copy in copies:
-        copy.wait()
+    outs, (chunks, came, went) = rest[:-3], rest[-3:]
+    parts = [(v, i, part) for v in range(len(outs)) for i in range(2) for part in range(2)]
+    rows = psi.shape[2] // 2
+    ways = []
+    for n, (v, i, part) in enumerate(parts):
+        at = pl.ds(part * rows, rows)
+        ways.append(
+            (
+                pltpu.make_async_copy(psi.at[v, i, at], chunks.at[n], came.at[n]),
+                pltpu.make_async_copy(chunks.at[n], outs[v].at[i, at], went.at[n]),
+            )
+        )
+    for into, _ in ways:
+        into.start()
+    for into, out in ways:
+        into.wait()
+        out.start()
+    for _, out in ways:
+        out.wait()
 
 
 def split(psi):
-    vectors = psi.shape[0]
+    vectors, _, size, _ = psi.shape
+    count = 4 * vectors
+    anywhere = pl.BlockSpec(memory_space=pl.ANY)
     return pl.pallas_call(
         split_kernel,
-        in_specs=[pl.BlockSpec(memory_space=pl.ANY)],
-        out_specs=[pl.BlockSpec(memory_space=pltpu.VMEM)] * vectors,
+        in_specs=[anywhere],
+        out_specs=[anywhere] * vectors,
         out_shape=[jax.ShapeDtypeStruct(psi.shape[1:], BF16)] * vectors,
-        scratch_shapes=[pltpu.SemaphoreType.DMA((vectors,))],
+        scratch_shapes=[
+            pltpu.VMEM((count, size // 2, size), BF16),
+            pltpu.SemaphoreType.DMA((count,)),
+            pltpu.SemaphoreType.DMA((count,)),
+        ],
         compiler_params=pltpu.CompilerParams(vmem_limit_bytes=60 * 10**6),
         cost_estimate=pl.CostEstimate(flops=0, bytes_accessed=4 * 2**20, transcendentals=0),
     )(psi)

time: 95 us -> 94.5 us (level); the launches traced: 94.4 us -> 92.7 us
  waiting for transfers between devices: 22.6 us -> 18.6 us
  starting transfers between devices: 51.4 us -> 54.1 us
    ppermute x9, waiting for transfers between devices: 18.3 us -> 14.2 us  [shift(): return lax.ppermute(x, ('op', 'sec'), pairs)]
    ppermute x9, starting transfers between devices: 39.8 us -> 42.6 us  [shift(): return lax.ppermute(x, ('op', 'sec'), pairs)]
where the time goes in v9:
time: 94.5 us; the launch traced here: 92.7 us
  starting transfers between devices  54.1 us (57%)
  waiting for transfers between devices  18.6 us (20%)
  Pallas kernels  16.8 us (18%)
  local copies, waits for them, and re-layouts  1.71 us (2%)
  other arithmetic  1.18 us (1%)
    ppermute x9, starting transfers between devices, shift(): return lax.ppermute(x, ('op', 'sec'), pairs)  42.6 us
    ppermute x9, waiting for transfers between devices, shift(): return lax.ppermute(x, ('op', 'sec'), pairs)  14.2 us
    pallas_call x2, Pallas kernels, partials(): pl.pallas_call(lambda *refs: kernel(v, *refs), in_specs=[scalars, scalars...  11 us
    ppermute x2, starting transfers between devices, shards(): across = [lax.ppermute(block, 'sec', facing) for block in own]  7.67 us
    ppermute x2, waiting for transfers between devices, shards(): across = [lax.ppermute(block, 'sec', facing) for block in own]  4.35 us
    ppermute x2, starting transfers between devices, shards(): lax.ppermute(block, 'sec', [(i, i ^ 1) for i in range(count)])  3.84 us
    pallas_call x1, Pallas kernels, split(): pl.pallas_call(split_kernel, in_specs=[anywhere], out_specs=[anywhere] *...  2.54 us
    pallas_call x2, Pallas kernels, mine_shares(): pl.pallas_call(mine_kernel, in_specs=[whole] * 2, out_specs=whole, out_sh...  2.16 us
  transfers between devices with their start and end apart: 13, of which 5 were waited for; matrix products, arithmetic and copies ran while one was open for 1% of the time, Pallas kernels for 15%

profile of v9, /device:TPU:24, one launch (start us, length us, event | category | flops | bytes accessed | tf_op | source)
XLA Modules:
  0.0 92.7 jit_solution(1620218071317715538)
XLA Ops:
  0.0 2.5 %shard_map.47 = (bf16[2,512,512]{2,1,0:T(8,128)(2,1)}, bf16[2,512,512]{2,1,0:T(8,128)(2,1)}) custom-call(bf16[2,2,512,512]{3,2,1,0:T(8,128)(2,1)} %psi.1), custom_call_target="tpu_custom_call" | custom-call | bytes 4194304 | tf_op jit(solution)/shard_map/pallas_call | solution.py:40
  2.5 4.3 %collective-permute-start = (bf16[2,512,512]{2,1,0:T(8,128)(2,1)}, bf16[2,512,512]{2,1,0:T(8,128)(2,1)}, u32[]{:S(2)}, u32[]{:S(2)}) collective-permute-start(bf16[2,512,512]{2,1,0:T(8,128)(2,1)} %get-tuple-element.18.refs_3_), channel_id=1, source_target_pairs={{1,2},{3,4},{5,6},{7,8},{9,10},{11,12},{13,14},{15,16},{17,18},{19... | collective-permute-start | bytes 3145736 | tf_op jit(solution)/shard_map/ppermute | solution.py:208
  6.8 1.9 %collective-permute-start.1 = (bf16[2,512,512]{2,1,0:T(8,128)(2,1)}, bf16[2,512,512]{2,1,0:T(8,128)(2,1)}, u32[]{:S(2)}, u32[]{:S(2)}) collective-permute-start(bf16[2,512,512]{2,1,0:T(8,128)(2,1)} %get-tuple-element.18.refs_3_), channel_id=1, source_target_pairs={{0,1},{1,0},{2,3},{3,2},{4,5},{5,4},{6,7},{7,6},{8,9},{9,8},{10,11... | collective-permute-start | bytes 3145736 | tf_op jit(solution)/shard_map/ppermute | solution.py:209
  8.8 3.4 %collective-permute-start.4 = (bf16[2,512,512]{2,1,0:T(8,128)(2,1)}, bf16[2,512,512]{2,1,0:T(8,128)(2,1)S(1)}, u32[]{:S(2)}, u32[]{:S(2)}) collective-permute-start(bf16[2,512,512]{2,1,0:T(8,128)(2,1)} %get-tuple-element.23.refs_3_), channel_id=1, source_target_pairs={{1,2},{3,4},{5,6},{7,8},{9,10},{11,12},{13,14},{15,16},{17,18},{19... | collective-permute-start | bytes 3145736 | tf_op jit(solution)/shard_map/ppermute | solution.py:208
  12.2 1.9 %collective-permute-start.5 = (bf16[2,512,512]{2,1,0:T(8,128)(2,1)}, bf16[2,512,512]{2,1,0:T(8,128)(2,1)}, u32[]{:S(2)}, u32[]{:S(2)}) collective-permute-start(bf16[2,512,512]{2,1,0:T(8,128)(2,1)} %get-tuple-element.23.refs_3_), channel_id=1, source_target_pairs={{0,1},{1,0},{2,3},{3,2},{4,5},{5,4},{6,7},{7,6},{8,9},{9,8},{10,11... | collective-permute-start | bytes 3145736 | tf_op jit(solution)/shard_map/ppermute | solution.py:209
  14.1 0.1 reshape.10.refs_1_
  14.2 0.1 pad_add_fusion.at.refs_0_
  14.3 1.4 %copy-done.1 = bf16[3,512,512]{2,1,0:T(8,128)(2,1)S(1)} copy-done((bf16[3,512,512]{2,1,0:T(8,128)(2,1)S(1)}, bf16[3,512,512]{2,1,0:T(8,128)(2,1)}, u32[]{:S(2)}) %copy-start.1) | copy-done | bytes 1572888
  15.7 1.0 %shard_map.46 = (bf16[512,1536]{1,0:T(8,128)(2,1)S(1)}, bf16[3,512,512]{2,1,0:T(8,128)(2,1)S(1)}) custom-call(s32[3]{0:T(128)S(1)} %pad_add_fusion.at.refs_0_, bf16[3,512,512]{2,1,0:T(8,128)(2,1)S(1)} %copy-done, bf16[3,512,512]{2,1,0:T(8,128)(2,1)S(1)} %copy-done.1), custom_call_target="tpu_custom_call" | custom-call | bytes 6291456 | tf_op jit(solution)/shard_map/pallas_call | solution.py:72
  16.7 4.3 %collective-permute-done.refs_2_ = bf16[2,512,512]{2,1,0:T(8,128)(2,1)} collective-permute-done((bf16[2,512,512]{2,1,0:T(8,128)(2,1)}, bf16[2,512,512]{2,1,0:T(8,128)(2,1)}, u32[]{:S(2)}, u32[]{:S(2)}) %collective-permute-start) | collective-permute-done | bytes 1048608 | tf_op jit(solution)/shard_map/ppermute | solution.py:208
  21.1 0.0 collective-permute-done.1.refs_4_
  21.1 5.7 %shard_map.48 = (bf16[2,160,512]{2,1,0:T(8,128)(2,1)S(1)}, bf16[2,160,512]{2,1,0:T(8,128)(2,1)S(1)}, bf16[2,32,512]{2,1,0:T(8,128)(2,1)S(1)}, bf16[2,1536,512]{2,1,0:T(8,128)(2,1)S(1)}) custom-call(s32[3]{0:T(128)S(1)} %pad_add_fusion.at.refs_0_, s32[30]{0:T(128)S(1)} %reshape.10.refs_1_, bf16[2,512,512]{2,1,0:T(8,128)(2,1)} %collective-permute-done.refs_2_, ...), custom_call_target="tpu_custom_call" | custom-call | flops 3221225472 | bytes 8388608 | tf_op jit(solution)/shard_map/pallas_call | solution.py:175
  26.8 3.8 %collective-permute-start.2 = (bf16[2,160,512]{2,1,0:T(8,128)(2,1)S(1)}, bf16[2,160,512]{2,1,0:T(8,128)(2,1)S(1)}, u32[]{:S(2)}, u32[]{:S(2)}) collective-permute-start(bf16[2,160,512]{2,1,0:T(8,128)(2,1)S(1)} %get-tuple-element.21), channel_id=1, source_target_pairs={{0,32},{1,481},{2,34},{3,483},{4,36},{5,485},{6,38},{7,487},{8,40}... | collective-permute-start | bytes 983048 | tf_op jit(solution)/shard_map/ppermute | solution.py:195
  30.6 9.5 %collective-permute-start.3 = (bf16[2,160,512]{2,1,0:T(8,128)(2,1)S(1)}, bf16[2,160,512]{2,1,0:T(8,128)(2,1)S(1)}, u32[]{:S(2)}, u32[]{:S(2)}) collective-permute-start(bf16[2,160,512]{2,1,0:T(8,128)(2,1)S(1)} %get-tuple-element.22), channel_id=1, source_target_pairs={{0,480},{1,33},{2,482},{3,35},{4,484},{5,37},{6,486},{7,39},{8,488... | collective-permute-start | bytes 983048 | tf_op jit(solution)/shard_map/ppermute | solution.py:195
  40.2 5.3 %shard_map.50 = (bf16[2,160,512]{2,1,0:T(8,128)(2,1)S(1)}, bf16[2,160,512]{2,1,0:T(8,128)(2,1)S(1)}, bf16[2,32,512]{2,1,0:T(8,128)(2,1)S(1)}, bf16[2,1536,512]{2,1,0:T(8,128)(2,1)S(1)}) custom-call(s32[3]{0:T(128)S(1)} %pad_add_fusion.at.refs_0_, s32[30]{0:T(128)S(1)} %reshape.10.refs_1_, bf16[2,512,512]{2,1,0:T(8,128)(2,1)S(1)} %collective-permute-done.4.refs_2_, ...), custom_call_target="tpu_custom_call" | custom-call | flops 3221225472 | bytes 8388608 | tf_op jit(solution)/shard_map/pallas_call | solution.py:175
  45.5 1.9 %collective-permute-start.6 = (bf16[2,160,512]{2,1,0:T(8,128)(2,1)S(1)}, bf16[2,160,512]{2,1,0:T(8,128)(2,1)S(1)}, u32[]{:S(2)}, u32[]{:S(2)}) collective-permute-start(bf16[2,160,512]{2,1,0:T(8,128)(2,1)S(1)} %get-tuple-element.25), channel_id=1, source_target_pairs={{0,32},{1,481},{2,34},{3,483},{4,36},{5,485},{6,38},{7,487},{8,40}... | collective-permute-start | bytes 983048 | tf_op jit(solution)/shard_map/ppermute | solution.py:195
  47.5 5.1 %collective-permute-start.7 = (bf16[2,160,512]{2,1,0:T(8,128)(2,1)S(1)}, bf16[2,160,512]{2,1,0:T(8,128)(2,1)S(1)}, u32[]{:S(2)}, u32[]{:S(2)}) collective-permute-start(bf16[2,160,512]{2,1,0:T(8,128)(2,1)S(1)} %get-tuple-element.26), channel_id=1, source_target_pairs={{0,480},{1,33},{2,482},{3,35},{4,484},{5,37},{6,486},{7,39},{8,488... | collective-permute-start | bytes 983048 | tf_op jit(solution)/shard_map/ppermute | solution.py:195
  52.6 3.2 %collective-permute-start.8 = (bf16[2,2,32,512]{3,2,1,0:T(8,128)(2,1)S(1)}, bf16[2,2,32,512]{3,2,1,0:T(8,128)(2,1)S(1)}, u32[]{:S(2)}, u32[]{:S(2)}) collective-permute-start(bf16[2,2,32,512]{3,2,1,0:T(8,128)(2,1)S(1)} %pad_maximum_fusion), channel_id=1, source_target_pairs={{0,448},{1,65},{2,450},{3,67},{4,452},{5,69},{6,454},{7,71},{8,456... | collective-permute-start | bytes 393224 | tf_op jit(solution)/shard_map/ppermute | solution.py:195
  55.8 1.1 %shard_map.49 = bf16[2,160,512]{2,1,0:T(8,128)(2,1)S(1)} custom-call(bf16[512,1536]{1,0:T(8,128)(2,1)S(1)} %get-tuple-element.17.refs_6_.left, bf16[2,1536,512]{2,1,0:T(8,128)(2,1)S(1)} %get-tuple-element.20.halved), custom_call_target="tpu_custom_call" | custom-call | flops 503316480 | bytes 4194304 | tf_op jit(solution)/shard_map/pallas_call | solution.py:156
  56.9 1.1 %shard_map.51 = bf16[2,160,512]{2,1,0:T(8,128)(2,1)S(1)} custom-call(bf16[512,1536]{1,0:T(8,128)(2,1)S(1)} %get-tuple-element.17.refs_6_.left, bf16[2,1536,512]{2,1,0:T(8,128)(2,1)S(1)} %get-tuple-element.24.halved), custom_call_target="tpu_custom_call" | custom-call | flops 503316480 | bytes 4194304 | tf_op jit(solution)/shard_map/pallas_call | solution.py:156
  58.0 0.0 collective-permute-done.3
  58.0 0.1 convert_add_fusion.1
  58.2 0.1 convert_add_fusion
  58.4 2.1 %collective-permute-done.8 = bf16[2,2,32,512]{3,2,1,0:T(8,128)(2,1)S(1)} collective-permute-done((bf16[2,2,32,512]{3,2,1,0:T(8,128)(2,1)S(1)}, bf16[2,2,32,512]{3,2,1,0:T(8,128)(2,1)S(1)}, u32[]{:S(2)}, u32[]{:S(2)}) %collective-permute-start.8) | collective-permute-done | bytes 131104 | tf_op jit(solution)/shard_map/ppermute | solution.py:195
  60.5 3.7 %collective-permute-start.9 = (bf16[2,2,32,512]{3,2,1,0:T(8,128)(2,1)S(1)}, bf16[2,2,32,512]{3,2,1,0:T(8,128)(2,1)S(1)}, u32[]{:S(2)}, u32[]{:S(2)}) collective-permute-start(bf16[2,2,32,512]{3,2,1,0:T(8,128)(2,1)S(1)} %fusion.2), channel_id=1, source_target_pairs={{0,416},{1,97},{2,418},{3,99},{4,420},{5,101},{6,422},{7,103},{8,4... | collective-permute-start | bytes 393224 | tf_op jit(solution)/shard_map/ppermute | solution.py:195
  64.2 3.9 %collective-permute-start.11 = (bf16[2,2,32,512]{3,2,1,0:T(8,128)(2,1)S(1)}, bf16[2,2,32,512]{3,2,1,0:T(8,128)(2,1)S(1)}, u32[]{:S(2)}, u32[]{:S(2)}) collective-permute-start(bf16[2,2,32,512]{3,2,1,0:T(8,128)(2,1)S(1)} %pad_maximum_fusion.1), channel_id=1, source_target_pairs={{0,96},{1,417},{2,98},{3,419},{4,100},{5,421},{6,102},{7,423},{8,1... | collective-permute-start | bytes 393224 | tf_op jit(solution)/shard_map/ppermute | solution.py:195
  68.3 3.9 %collective-permute-done.9 = bf16[2,2,32,512]{3,2,1,0:T(8,128)(2,1)S(1)} collective-permute-done((bf16[2,2,32,512]{3,2,1,0:T(8,128)(2,1)S(1)}, bf16[2,2,32,512]{3,2,1,0:T(8,128)(2,1)S(1)}, u32[]{:S(2)}, u32[]{:S(2)}) %collective-permute-start.9) | collective-permute-done | bytes 131104 | tf_op jit(solution)/shard_map/ppermute | solution.py:195
  72.2 9.2 %collective-permute-start.10 = (bf16[2,2,32,512]{3,2,1,0:T(8,128)(2,1)S(1)}, bf16[2,2,32,512]{3,2,1,0:T(8,128)(2,1)S(1)}, u32[]{:S(2)}, u32[]{:S(2)}) collective-permute-start(bf16[2,2,32,512]{3,2,1,0:T(8,128)(2,1)S(1)} %fusion.1), channel_id=1, source_target_pairs={{0,416},{1,97},{2,418},{3,99},{4,420},{5,101},{6,422},{7,103},{8,4... | collective-permute-start | bytes 393224 | tf_op jit(solution)/shard_map/ppermute | solution.py:195
  81.5 2.2 %collective-permute-start.12 = (bf16[2,2,32,512]{3,2,1,0:T(8,128)(2,1)S(1)}, bf16[2,2,32,512]{3,2,1,0:T(8,128)(2,1)S(1)}, u32[]{:S(2)}, u32[]{:S(2)}) collective-permute-start(bf16[2,2,32,512]{3,2,1,0:T(8,128)(2,1)S(1)} %fusion.3), channel_id=1, source_target_pairs={{0,96},{1,417},{2,98},{3,419},{4,100},{5,421},{6,102},{7,423},{8,1... | collective-permute-start | bytes 393224 | tf_op jit(solution)/shard_map/ppermute | solution.py:195
  83.7 6.1 %collective-permute-done.10 = bf16[2,2,32,512]{3,2,1,0:T(8,128)(2,1)S(1)} collective-permute-done((bf16[2,2,32,512]{3,2,1,0:T(8,128)(2,1)S(1)}, bf16[2,2,32,512]{3,2,1,0:T(8,128)(2,1)S(1)}, u32[]{:S(2)}, u32[]{:S(2)}) %collective-permute-start.10) | collective-permute-done | bytes 131104 | tf_op jit(solution)/shard_map/ppermute | solution.py:195
  89.8 2.1 %collective-permute-done.12 = bf16[2,2,32,512]{3,2,1,0:T(8,128)(2,1)S(1)} collective-permute-done((bf16[2,2,32,512]{3,2,1,0:T(8,128)(2,1)S(1)}, bf16[2,2,32,512]{3,2,1,0:T(8,128)(2,1)S(1)}, u32[]{:S(2)}, u32[]{:S(2)}) %collective-permute-start.12) | collective-permute-done | bytes 131104 | tf_op jit(solution)/shard_map/ppermute | solution.py:195
  91.9 0.7 fusion
  (27 shorter events, 0.4 us)
Async XLA Ops:
  0.0 14.1 %copy-start.4 = (s32[3,2,5]{2,1,0:T(2,128)S(1)}, s32[3,2,5]{2,1,0:T(2,128)}, u32[]{:S(2)}) copy-start(s32[3,2,5]{2,1,0:T(2,128)} %param.7) | copy-start | bytes 364
  0.0 14.3 %copy-start = (bf16[3,512,512]{2,1,0:T(8,128)(2,1)S(1)}, bf16[3,512,512]{2,1,0:T(8,128)(2,1)}, u32[]{:S(2)}) copy-start(bf16[3,512,512]{2,1,0:T(8,128)(2,1)} %left.1) | copy-start | bytes 4718596
  2.5 18.5 %collective-permute-start = (bf16[2,512,512]{2,1,0:T(8,128)(2,1)}, bf16[2,512,512]{2,1,0:T(8,128)(2,1)}, u32[]{:S(2)}, u32[]{:S(2)}) collective-permute-start(bf16[2,512,512]{2,1,0:T(8,128)(2,1)} %get-tuple-element.18.refs_3_), channel_id=1, source_target_pairs={{1,2},{3,4},{5,6},{7,8},{9,10},{11,12},{13,14},{15,16},{17,18},{19... | collective-permute-start | bytes 3145736 | tf_op jit(solution)/shard_map/ppermute | solution.py:208
  6.8 14.3 %collective-permute-start.1 = (bf16[2,512,512]{2,1,0:T(8,128)(2,1)}, bf16[2,512,512]{2,1,0:T(8,128)(2,1)}, u32[]{:S(2)}, u32[]{:S(2)}) collective-permute-start(bf16[2,512,512]{2,1,0:T(8,128)(2,1)} %get-tuple-element.18.refs_3_), channel_id=1, source_target_pairs={{0,1},{1,0},{2,3},{3,2},{4,5},{5,4},{6,7},{7,6},{8,9},{9,8},{10,11... | collective-permute-start | bytes 3145736 | tf_op jit(solution)/shard_map/ppermute | solution.py:209
  8.8 31.4 %collective-permute-start.4 = (bf16[2,512,512]{2,1,0:T(8,128)(2,1)}, bf16[2,512,512]{2,1,0:T(8,128)(2,1)S(1)}, u32[]{:S(2)}, u32[]{:S(2)}) collective-permute-start(bf16[2,512,512]{2,1,0:T(8,128)(2,1)} %get-tuple-element.23.refs_3_), channel_id=1, source_target_pairs={{1,2},{3,4},{5,6},{7,8},{9,10},{11,12},{13,14},{15,16},{17,18},{19... | collective-permute-start | bytes 3145736 | tf_op jit(solution)/shard_map/ppermute | solution.py:208
  12.2 28.0 %collective-permute-start.5 = (bf16[2,512,512]{2,1,0:T(8,128)(2,1)}, bf16[2,512,512]{2,1,0:T(8,128)(2,1)}, u32[]{:S(2)}, u32[]{:S(2)}) collective-permute-start(bf16[2,512,512]{2,1,0:T(8,128)(2,1)} %get-tuple-element.23.refs_3_), channel_id=1, source_target_pairs={{0,1},{1,0},{2,3},{3,2},{4,5},{5,4},{6,7},{7,6},{8,9},{9,8},{10,11... | collective-permute-start | bytes 3145736 | tf_op jit(solution)/shard_map/ppermute | solution.py:209
  14.3 1.4 %copy-start.1 = (bf16[3,512,512]{2,1,0:T(8,128)(2,1)S(1)}, bf16[3,512,512]{2,1,0:T(8,128)(2,1)}, u32[]{:S(2)}) copy-start(bf16[3,512,512]{2,1,0:T(8,128)(2,1)} %right.1) | copy-start | bytes 4718596
  15.7 5.4 %copy-start.3 = (bf16[2,512,512]{2,1,0:T(8,128)(2,1)S(1)}, bf16[2,512,512]{2,1,0:T(8,128)(2,1)}, u32[]{:S(2)}) copy-start(bf16[2,512,512]{2,1,0:T(8,128)(2,1)} %get-tuple-element.18.refs_3_) | copy-start | bytes 3145732
  21.1 19.1 %copy-start.2 = (bf16[2,512,512]{2,1,0:T(8,128)(2,1)S(1)}, bf16[2,512,512]{2,1,0:T(8,128)(2,1)}, u32[]{:S(2)}) copy-start(bf16[2,512,512]{2,1,0:T(8,128)(2,1)} %get-tuple-element.23.refs_3_) | copy-start | bytes 3145732
  26.8 31.2 %collective-permute-start.2 = (bf16[2,160,512]{2,1,0:T(8,128)(2,1)S(1)}, bf16[2,160,512]{2,1,0:T(8,128)(2,1)S(1)}, u32[]{:S(2)}, u32[]{:S(2)}) collective-permute-start(bf16[2,160,512]{2,1,0:T(8,128)(2,1)S(1)} %get-tuple-element.21), channel_id=1, source_target_pairs={{0,32},{1,481},{2,34},{3,483},{4,36},{5,485},{6,38},{7,487},{8,40}... | collective-permute-start | bytes 983048 | tf_op jit(solution)/shard_map/ppermute | solution.py:195
  30.6 27.3 %collective-permute-start.3 = (bf16[2,160,512]{2,1,0:T(8,128)(2,1)S(1)}, bf16[2,160,512]{2,1,0:T(8,128)(2,1)S(1)}, u32[]{:S(2)}, u32[]{:S(2)}) collective-permute-start(bf16[2,160,512]{2,1,0:T(8,128)(2,1)S(1)} %get-tuple-element.22), channel_id=1, source_target_pairs={{0,480},{1,33},{2,482},{3,35},{4,484},{5,37},{6,486},{7,39},{8,488... | collective-permute-start | bytes 983048 | tf_op jit(solution)/shard_map/ppermute | solution.py:195
  45.5 12.6 %collective-permute-start.6 = (bf16[2,160,512]{2,1,0:T(8,128)(2,1)S(1)}, bf16[2,160,512]{2,1,0:T(8,128)(2,1)S(1)}, u32[]{:S(2)}, u32[]{:S(2)}) collective-permute-start(bf16[2,160,512]{2,1,0:T(8,128)(2,1)S(1)} %get-tuple-element.25), channel_id=1, source_target_pairs={{0,32},{1,481},{2,34},{3,483},{4,36},{5,485},{6,38},{7,487},{8,40}... | collective-permute-start | bytes 983048 | tf_op jit(solution)/shard_map/ppermute | solution.py:195
  47.5 10.7 %collective-permute-start.7 = (bf16[2,160,512]{2,1,0:T(8,128)(2,1)S(1)}, bf16[2,160,512]{2,1,0:T(8,128)(2,1)S(1)}, u32[]{:S(2)}, u32[]{:S(2)}) collective-permute-start(bf16[2,160,512]{2,1,0:T(8,128)(2,1)S(1)} %get-tuple-element.26), channel_id=1, source_target_pairs={{0,480},{1,33},{2,482},{3,35},{4,484},{5,37},{6,486},{7,39},{8,488... | collective-permute-start | bytes 983048 | tf_op jit(solution)/shard_map/ppermute | solution.py:195
  52.6 7.9 %collective-permute-start.8 = (bf16[2,2,32,512]{3,2,1,0:T(8,128)(2,1)S(1)}, bf16[2,2,32,512]{3,2,1,0:T(8,128)(2,1)S(1)}, u32[]{:S(2)}, u32[]{:S(2)}) collective-permute-start(bf16[2,2,32,512]{3,2,1,0:T(8,128)(2,1)S(1)} %pad_maximum_fusion), channel_id=1, source_target_pairs={{0,448},{1,65},{2,450},{3,67},{4,452},{5,69},{6,454},{7,71},{8,456... | collective-permute-start | bytes 393224 | tf_op jit(solution)/shard_map/ppermute | solution.py:195
  60.5 11.6 %collective-permute-start.9 = (bf16[2,2,32,512]{3,2,1,0:T(8,128)(2,1)S(1)}, bf16[2,2,32,512]{3,2,1,0:T(8,128)(2,1)S(1)}, u32[]{:S(2)}, u32[]{:S(2)}) collective-permute-start(bf16[2,2,32,512]{3,2,1,0:T(8,128)(2,1)S(1)} %fusion.2), channel_id=1, source_target_pairs={{0,416},{1,97},{2,418},{3,99},{4,420},{5,101},{6,422},{7,103},{8,4... | collective-permute-start | bytes 393224 | tf_op jit(solution)/shard_map/ppermute | solution.py:195
  64.2 17.2 %collective-permute-start.11 = (bf16[2,2,32,512]{3,2,1,0:T(8,128)(2,1)S(1)}, bf16[2,2,32,512]{3,2,1,0:T(8,128)(2,1)S(1)}, u32[]{:S(2)}, u32[]{:S(2)}) collective-permute-start(bf16[2,2,32,512]{3,2,1,0:T(8,128)(2,1)S(1)} %pad_maximum_fusion.1), channel_id=1, source_target_pairs={{0,96},{1,417},{2,98},{3,419},{4,100},{5,421},{6,102},{7,423},{8,1... | collective-permute-start | bytes 393224 | tf_op jit(solution)/shard_map/ppermute | solution.py:195
  72.2 17.6 %collective-permute-start.10 = (bf16[2,2,32,512]{3,2,1,0:T(8,128)(2,1)S(1)}, bf16[2,2,32,512]{3,2,1,0:T(8,128)(2,1)S(1)}, u32[]{:S(2)}, u32[]{:S(2)}) collective-permute-start(bf16[2,2,32,512]{3,2,1,0:T(8,128)(2,1)S(1)} %fusion.1), channel_id=1, source_target_pairs={{0,416},{1,97},{2,418},{3,99},{4,420},{5,101},{6,422},{7,103},{8,4... | collective-permute-start | bytes 393224 | tf_op jit(solution)/shard_map/ppermute | solution.py:195
  81.5 10.4 %collective-permute-start.12 = (bf16[2,2,32,512]{3,2,1,0:T(8,128)(2,1)S(1)}, bf16[2,2,32,512]{3,2,1,0:T(8,128)(2,1)S(1)}, u32[]{:S(2)}, u32[]{:S(2)}) collective-permute-start(bf16[2,2,32,512]{3,2,1,0:T(8,128)(2,1)S(1)} %fusion.3), channel_id=1, source_target_pairs={{0,96},{1,417},{2,98},{3,419},{4,100},{5,421},{6,102},{7,423},{8,1... | collective-permute-start | bytes 393224 | tf_op jit(solution)/shard_map/ppermute | solution.py:195

commit v10 on v8

--- a/solution.py
+++ b/solution.py
@@ -11,25 +11,42 @@
 ORDER = [1 - p for p in LEADERS] + [-1 - p for p in LEADERS] + [8] + [-p for p in LEADERS]
 
 
-def split_kernel(psi, *rest):
-    outs, sems = rest[:-1], rest[-1]
-    copies = [pltpu.make_async_copy(psi.at[v], out, sems.at[v]) for v, out in enumerate(outs)]
-    for copy in copies:
-        copy.start()
-    for copy in copies:
-        copy.wait()
-
-
-def split(psi):
-    vectors = psi.shape[0]
-    return pl.pallas_call(
-        split_kernel,
-        in_specs=[pl.BlockSpec(memory_space=pl.ANY)],
-        out_specs=[pl.BlockSpec(memory_space=pltpu.VMEM)] * vectors,
-        out_shape=[jax.ShapeDtypeStruct(psi.shape[1:], BF16)] * vectors,
-        scratch_shapes=[pltpu.SemaphoreType.DMA((vectors,))],
+def take(psi, v):
+    size = psi.shape[2]
+    count = 4
+    rows = 2 * size // count
+
+    def kernel(source, out, chunks, came, went):
+        ways = []
+        for n in range(count):
+            at = (n * rows // size, pl.ds(n * rows % size, rows))
+            ways.append(
+                (
+                    pltpu.make_async_copy(source.at[(v,) + at], chunks.at[n], came.at[n]),
+                    pltpu.make_async_copy(chunks.at[n], out.at[at], went.at[n]),
+                )
+            )
+        for into, _ in ways:
+            into.start()
+        for into, way in ways:
+            into.wait()
+            way.start()
+        for _, way in ways:
+            way.wait()
+
+    anywhere = pl.BlockSpec(memory_space=pl.ANY)
+    return pl.pallas_call(
+        kernel,
+        in_specs=[anywhere],
+        out_specs=anywhere,
+        out_shape=jax.ShapeDtypeStruct(psi.shape[1:], BF16),
+        scratch_shapes=[
+            pltpu.VMEM((count, rows, size), BF16),
+            pltpu.SemaphoreType.DMA((count,)),
+            pltpu.SemaphoreType.DMA((count,)),
+        ],
         compiler_params=pltpu.CompilerParams(vmem_limit_bytes=60 * 10**6),
-        cost_estimate=pl.CostEstimate(flops=0, bytes_accessed=4 * 2**20, transcendentals=0),
+        cost_estimate=pl.CostEstimate(flops=0, bytes_accessed=2 * 2**20, transcendentals=0),
     )(psi)
 
 
@@ -185,7 +202,7 @@
 
     facing = [(i, i + 1) for i in range(1, count - 1, 2)]
     facing += [(b, a) for a, b in facing]
-    own = split(psi)
+    own = [take(psi, v) for v in range(vectors)]
     across = [lax.ppermute(block, "sec", facing) for block in own]
     chip = [lax.ppermute(block, "sec", [(i, i ^ 1) for i in range(count)]) for block in own]
 

time: 95 us -> 95.3 us (level)
  Pallas kernels: 17.2 us -> 19.3 us
  local copies, waits for them, and re-layouts: 1.71 us -> 0.3 us
    unnamed x10, local copies, waits for them, and re-layouts: 1.43 us -> 0.03 us
    pallas_call x2, Pallas kernels: 11 us -> 12.1 us  [partials(): pl.pallas_call(lambda *refs: kernel(v, *refs), in_specs=[scalars, scalars...]
    pallas_call x1 -> x2, Pallas kernels: 3 us -> 4.01 us  [take(): pl.pallas_call(kernel, in_specs=[anywhere], out_specs=anywhere, out_shape...]
  transfers between devices with their start and end apart: 13 -> 13, of which waited for: 5 -> 5; matrix products, arithmetic and copies ran while one was open for 1% -> 1% of each run, Pallas kernels for 15% -> 18%
where the time goes in v10:
time: 95.3 us; the launch traced here: 94.8 us
  starting transfers between devices  51.6 us (54%)
  waiting for transfers between devices  22 us (23%)
  Pallas kernels  19.3 us (20%)
  other arithmetic  1.19 us (1%)
    ppermute x9, starting transfers between devices, shift(): return lax.ppermute(x, ('op', 'sec'), pairs)  39.8 us
    ppermute x9, waiting for transfers between devices, shift(): return lax.ppermute(x, ('op', 'sec'), pairs)  18.3 us
    pallas_call x2, Pallas kernels, partials(): pl.pallas_call(lambda *refs: kernel(v, *refs), in_specs=[scalars, scalars...  12.1 us
    ppermute x2, starting transfers between devices, shards(): across = [lax.ppermute(block, 'sec', facing) for block in own]  7.94 us
    pallas_call x2, Pallas kernels, take(): pl.pallas_call(kernel, in_specs=[anywhere], out_specs=anywhere, out_shape...  4.01 us
    ppermute x2, starting transfers between devices, shards(): lax.ppermute(block, 'sec', [(i, i ^ 1) for i in range(count)])  3.84 us
    ppermute x2, waiting for transfers between devices, shards(): across = [lax.ppermute(block, 'sec', facing) for block in own]  3.72 us
    pallas_call x2, Pallas kernels, mine_shares(): pl.pallas_call(mine_kernel, in_specs=[whole] * 2, out_specs=whole, out_sh...  2.16 us
  transfers between devices with their start and end apart: 13, of which 5 were waited for; matrix products, arithmetic and copies ran while one was open for 1% of the time, Pallas kernels for 18%

profile of v10, /device:TPU:24, one launch (start us, length us, event | category | flops | bytes accessed | tf_op | source)
XLA Modules:
  0.0 94.8 jit_solution(3358963352774681216)
XLA Ops:
  0.0 2.0 %shard_map.47.refs_3_ = bf16[2,512,512]{2,1,0:T(8,128)(2,1)} custom-call(bf16[2,2,512,512]{3,2,1,0:T(8,128)(2,1)} %source.3), custom_call_target="tpu_custom_call" | custom-call | bytes 2097152 | tf_op jit(solution)/shard_map/pallas_call | solution.py:38
  2.0 0.0 copy-start.1
  2.0 4.5 %collective-permute-start = (bf16[2,512,512]{2,1,0:T(8,128)(2,1)}, bf16[2,512,512]{2,1,0:T(8,128)(2,1)}, u32[]{:S(2)}, u32[]{:S(2)}) collective-permute-start(bf16[2,512,512]{2,1,0:T(8,128)(2,1)} %shard_map.47.refs_3_), channel_id=1, source_target_pairs={{1,2},{3,4},{5,6},{7,8},{9,10},{11,12},{13,14},{15,16},{17,18},{19... | collective-permute-start | bytes 3145736 | tf_op jit(solution)/shard_map/ppermute | solution.py:206
  6.6 1.9 %collective-permute-start.1 = (bf16[2,512,512]{2,1,0:T(8,128)(2,1)}, bf16[2,512,512]{2,1,0:T(8,128)(2,1)}, u32[]{:S(2)}, u32[]{:S(2)}) collective-permute-start(bf16[2,512,512]{2,1,0:T(8,128)(2,1)} %shard_map.47.refs_3_), channel_id=1, source_target_pairs={{0,1},{1,0},{2,3},{3,2},{4,5},{5,4},{6,7},{7,6},{8,9},{9,8},{10,11... | collective-permute-start | bytes 3145736 | tf_op jit(solution)/shard_map/ppermute | solution.py:207
  8.5 2.0 %shard_map.50.refs_3_ = bf16[2,512,512]{2,1,0:T(8,128)(2,1)} custom-call(bf16[2,2,512,512]{3,2,1,0:T(8,128)(2,1)} %source.3), custom_call_target="tpu_custom_call" | custom-call | bytes 2097152 | tf_op jit(solution)/shard_map/pallas_call | solution.py:38
  10.5 3.4 %collective-permute-start.4 = (bf16[2,512,512]{2,1,0:T(8,128)(2,1)}, bf16[2,512,512]{2,1,0:T(8,128)(2,1)}, u32[]{:S(2)}, u32[]{:S(2)}) collective-permute-start(bf16[2,512,512]{2,1,0:T(8,128)(2,1)} %shard_map.50.refs_3_), channel_id=1, source_target_pairs={{1,2},{3,4},{5,6},{7,8},{9,10},{11,12},{13,14},{15,16},{17,18},{19... | collective-permute-start | bytes 3145736 | tf_op jit(solution)/shard_map/ppermute | solution.py:206
  13.9 1.9 %collective-permute-start.5 = (bf16[2,512,512]{2,1,0:T(8,128)(2,1)}, bf16[2,512,512]{2,1,0:T(8,128)(2,1)}, u32[]{:S(2)}, u32[]{:S(2)}) collective-permute-start(bf16[2,512,512]{2,1,0:T(8,128)(2,1)} %shard_map.50.refs_3_), channel_id=1, source_target_pairs={{0,1},{1,0},{2,3},{3,2},{4,5},{5,4},{6,7},{7,6},{8,9},{9,8},{10,11... | collective-permute-start | bytes 3145736 | tf_op jit(solution)/shard_map/ppermute | solution.py:207
  15.9 0.1 reshape.10.refs_1_
  16.0 0.1 pad_add_fusion.at.refs_0_
  16.1 1.0 %shard_map.46 = (bf16[512,1536]{1,0:T(8,128)(2,1)S(1)}, bf16[3,512,512]{2,1,0:T(8,128)(2,1)S(1)}) custom-call(s32[3]{0:T(128)S(1)} %pad_add_fusion.at.refs_0_, bf16[3,512,512]{2,1,0:T(8,128)(2,1)S(1)} %copy-done, bf16[3,512,512]{2,1,0:T(8,128)(2,1)S(1)} %copy-done.1), custom_call_target="tpu_custom_call" | custom-call | bytes 6291456 | tf_op jit(solution)/shard_map/pallas_call | solution.py:70
  17.1 3.7 %collective-permute-done.refs_2_ = bf16[2,512,512]{2,1,0:T(8,128)(2,1)} collective-permute-done((bf16[2,512,512]{2,1,0:T(8,128)(2,1)}, bf16[2,512,512]{2,1,0:T(8,128)(2,1)}, u32[]{:S(2)}, u32[]{:S(2)}) %collective-permute-start) | collective-permute-done | bytes 1048608 | tf_op jit(solution)/shard_map/ppermute | solution.py:206
  20.8 6.1 %shard_map.48 = (bf16[2,160,512]{2,1,0:T(8,128)(2,1)S(1)}, bf16[2,160,512]{2,1,0:T(8,128)(2,1)S(1)}, bf16[2,32,512]{2,1,0:T(8,128)(2,1)S(1)}, bf16[2,1536,512]{2,1,0:T(8,128)(2,1)S(1)}) custom-call(s32[3]{0:T(128)S(1)} %pad_add_fusion.at.refs_0_, s32[30]{0:T(128)S(1)} %reshape.10.refs_1_, bf16[2,512,512]{2,1,0:T(8,128)(2,1)} %collective-permute-done.refs_2_, ...), custom_call_target="tpu_custom_call" | custom-call | flops 3221225472 | bytes 8388608 | tf_op jit(solution)/shard_map/pallas_call | solution.py:173
  26.9 3.8 %collective-permute-start.2 = (bf16[2,160,512]{2,1,0:T(8,128)(2,1)S(1)}, bf16[2,160,512]{2,1,0:T(8,128)(2,1)S(1)}, u32[]{:S(2)}, u32[]{:S(2)}) collective-permute-start(bf16[2,160,512]{2,1,0:T(8,128)(2,1)S(1)} %get-tuple-element.18), channel_id=1, source_target_pairs={{0,32},{1,481},{2,34},{3,483},{4,36},{5,485},{6,38},{7,487},{8,40}... | collective-permute-start | bytes 983048 | tf_op jit(solution)/shard_map/ppermute | solution.py:193
  30.8 9.5 %collective-permute-start.3 = (bf16[2,160,512]{2,1,0:T(8,128)(2,1)S(1)}, bf16[2,160,512]{2,1,0:T(8,128)(2,1)S(1)}, u32[]{:S(2)}, u32[]{:S(2)}) collective-permute-start(bf16[2,160,512]{2,1,0:T(8,128)(2,1)S(1)} %get-tuple-element.19), channel_id=1, source_target_pairs={{0,480},{1,33},{2,482},{3,35},{4,484},{5,37},{6,486},{7,39},{8,488... | collective-permute-start | bytes 983048 | tf_op jit(solution)/shard_map/ppermute | solution.py:193
  40.3 6.0 %shard_map.51 = (bf16[2,160,512]{2,1,0:T(8,128)(2,1)S(1)}, bf16[2,160,512]{2,1,0:T(8,128)(2,1)S(1)}, bf16[2,32,512]{2,1,0:T(8,128)(2,1)S(1)}, bf16[2,1536,512]{2,1,0:T(8,128)(2,1)S(1)}) custom-call(s32[3]{0:T(128)S(1)} %pad_add_fusion.at.refs_0_, s32[30]{0:T(128)S(1)} %reshape.10.refs_1_, bf16[2,512,512]{2,1,0:T(8,128)(2,1)} %collective-permute-done.4.refs_2_, ...), custom_call_target="tpu_custom_call" | custom-call | flops 3221225472 | bytes 8388608 | tf_op jit(solution)/shard_map/pallas_call | solution.py:173
  46.3 1.9 %collective-permute-start.6 = (bf16[2,160,512]{2,1,0:T(8,128)(2,1)S(1)}, bf16[2,160,512]{2,1,0:T(8,128)(2,1)S(1)}, u32[]{:S(2)}, u32[]{:S(2)}) collective-permute-start(bf16[2,160,512]{2,1,0:T(8,128)(2,1)S(1)} %get-tuple-element.21), channel_id=1, source_target_pairs={{0,32},{1,481},{2,34},{3,483},{4,36},{5,485},{6,38},{7,487},{8,40}... | collective-permute-start | bytes 983048 | tf_op jit(solution)/shard_map/ppermute | solution.py:193
  48.3 5.1 %collective-permute-start.7 = (bf16[2,160,512]{2,1,0:T(8,128)(2,1)S(1)}, bf16[2,160,512]{2,1,0:T(8,128)(2,1)S(1)}, u32[]{:S(2)}, u32[]{:S(2)}) collective-permute-start(bf16[2,160,512]{2,1,0:T(8,128)(2,1)S(1)} %get-tuple-element.22), channel_id=1, source_target_pairs={{0,480},{1,33},{2,482},{3,35},{4,484},{5,37},{6,486},{7,39},{8,488... | collective-permute-start | bytes 983048 | tf_op jit(solution)/shard_map/ppermute | solution.py:193
  53.4 3.2 %collective-permute-start.8 = (bf16[2,2,32,512]{3,2,1,0:T(8,128)(2,1)S(1)}, bf16[2,2,32,512]{3,2,1,0:T(8,128)(2,1)S(1)}, u32[]{:S(2)}, u32[]{:S(2)}) collective-permute-start(bf16[2,2,32,512]{3,2,1,0:T(8,128)(2,1)S(1)} %pad_maximum_fusion), channel_id=1, source_target_pairs={{0,448},{1,65},{2,450},{3,67},{4,452},{5,69},{6,454},{7,71},{8,456... | collective-permute-start | bytes 393224 | tf_op jit(solution)/shard_map/ppermute | solution.py:193
  56.6 1.1 %shard_map.49 = bf16[2,160,512]{2,1,0:T(8,128)(2,1)S(1)} custom-call(bf16[512,1536]{1,0:T(8,128)(2,1)S(1)} %get-tuple-element.15.refs_6_.left, bf16[2,1536,512]{2,1,0:T(8,128)(2,1)S(1)} %get-tuple-element.17.halved), custom_call_target="tpu_custom_call" | custom-call | flops 503316480 | bytes 4194304 | tf_op jit(solution)/shard_map/pallas_call | solution.py:154
  57.7 1.1 %shard_map.52 = bf16[2,160,512]{2,1,0:T(8,128)(2,1)S(1)} custom-call(bf16[512,1536]{1,0:T(8,128)(2,1)S(1)} %get-tuple-element.15.refs_6_.left, bf16[2,1536,512]{2,1,0:T(8,128)(2,1)S(1)} %get-tuple-element.20.halved), custom_call_target="tpu_custom_call" | custom-call | flops 503316480 | bytes 4194304 | tf_op jit(solution)/shard_map/pallas_call | solution.py:154
  58.8 0.0 collective-permute-done.3
  58.8 0.1 convert_add_fusion.1
  59.0 0.1 convert_add_fusion
  59.2 2.1 %collective-permute-done.8 = bf16[2,2,32,512]{3,2,1,0:T(8,128)(2,1)S(1)} collective-permute-done((bf16[2,2,32,512]{3,2,1,0:T(8,128)(2,1)S(1)}, bf16[2,2,32,512]{3,2,1,0:T(8,128)(2,1)S(1)}, u32[]{:S(2)}, u32[]{:S(2)}) %collective-permute-start.8) | collective-permute-done | bytes 131104 | tf_op jit(solution)/shard_map/ppermute | solution.py:193
  61.3 3.7 %collective-permute-start.9 = (bf16[2,2,32,512]{3,2,1,0:T(8,128)(2,1)S(1)}, bf16[2,2,32,512]{3,2,1,0:T(8,128)(2,1)S(1)}, u32[]{:S(2)}, u32[]{:S(2)}) collective-permute-start(bf16[2,2,32,512]{3,2,1,0:T(8,128)(2,1)S(1)} %fusion.2), channel_id=1, source_target_pairs={{0,416},{1,97},{2,418},{3,99},{4,420},{5,101},{6,422},{7,103},{8,4... | collective-permute-start | bytes 393224 | tf_op jit(solution)/shard_map/ppermute | solution.py:193
  65.1 3.9 %collective-permute-start.11 = (bf16[2,2,32,512]{3,2,1,0:T(8,128)(2,1)S(1)}, bf16[2,2,32,512]{3,2,1,0:T(8,128)(2,1)S(1)}, u32[]{:S(2)}, u32[]{:S(2)}) collective-permute-start(bf16[2,2,32,512]{3,2,1,0:T(8,128)(2,1)S(1)} %pad_maximum_fusion.1), channel_id=1, source_target_pairs={{0,96},{1,417},{2,98},{3,419},{4,100},{5,421},{6,102},{7,423},{8,1... | collective-permute-start | bytes 393224 | tf_op jit(solution)/shard_map/ppermute | solution.py:193
  69.1 6.7 %collective-permute-done.9 = bf16[2,2,32,512]{3,2,1,0:T(8,128)(2,1)S(1)} collective-permute-done((bf16[2,2,32,512]{3,2,1,0:T(8,128)(2,1)S(1)}, bf16[2,2,32,512]{3,2,1,0:T(8,128)(2,1)S(1)}, u32[]{:S(2)}, u32[]{:S(2)}) %collective-permute-start.9) | collective-permute-done | bytes 131104 | tf_op jit(solution)/shard_map/ppermute | solution.py:193
  75.8 6.4 %collective-permute-start.10 = (bf16[2,2,32,512]{3,2,1,0:T(8,128)(2,1)S(1)}, bf16[2,2,32,512]{3,2,1,0:T(8,128)(2,1)S(1)}, u32[]{:S(2)}, u32[]{:S(2)}) collective-permute-start(bf16[2,2,32,512]{3,2,1,0:T(8,128)(2,1)S(1)} %fusion.1), channel_id=1, source_target_pairs={{0,416},{1,97},{2,418},{3,99},{4,420},{5,101},{6,422},{7,103},{8,4... | collective-permute-start | bytes 393224 | tf_op jit(solution)/shard_map/ppermute | solution.py:193
  82.3 2.2 %collective-permute-start.12 = (bf16[2,2,32,512]{3,2,1,0:T(8,128)(2,1)S(1)}, bf16[2,2,32,512]{3,2,1,0:T(8,128)(2,1)S(1)}, u32[]{:S(2)}, u32[]{:S(2)}) collective-permute-start(bf16[2,2,32,512]{3,2,1,0:T(8,128)(2,1)S(1)} %fusion.3), channel_id=1, source_target_pairs={{0,96},{1,417},{2,98},{3,419},{4,100},{5,421},{6,102},{7,423},{8,1... | collective-permute-start | bytes 393224 | tf_op jit(solution)/shard_map/ppermute | solution.py:193
  84.6 6.1 %collective-permute-done.10 = bf16[2,2,32,512]{3,2,1,0:T(8,128)(2,1)S(1)} collective-permute-done((bf16[2,2,32,512]{3,2,1,0:T(8,128)(2,1)S(1)}, bf16[2,2,32,512]{3,2,1,0:T(8,128)(2,1)S(1)}, u32[]{:S(2)}, u32[]{:S(2)}) %collective-permute-start.10) | collective-permute-done | bytes 131104 | tf_op jit(solution)/shard_map/ppermute | solution.py:193
  90.7 3.4 %collective-permute-done.12 = bf16[2,2,32,512]{3,2,1,0:T(8,128)(2,1)S(1)} collective-permute-done((bf16[2,2,32,512]{3,2,1,0:T(8,128)(2,1)S(1)}, bf16[2,2,32,512]{3,2,1,0:T(8,128)(2,1)S(1)}, u32[]{:S(2)}, u32[]{:S(2)}) %collective-permute-start.12) | collective-permute-done | bytes 131104 | tf_op jit(solution)/shard_map/ppermute | solution.py:193
  94.0 0.7 fusion
  (28 shorter events, 0.4 us)
Async XLA Ops:
  2.0 13.9 %copy-start.4 = (s32[3,2,5]{2,1,0:T(2,128)S(1)}, s32[3,2,5]{2,1,0:T(2,128)}, u32[]{:S(2)}) copy-start(s32[3,2,5]{2,1,0:T(2,128)} %param.7) | copy-start | bytes 364
  2.0 14.1 %copy-start = (bf16[3,512,512]{2,1,0:T(8,128)(2,1)S(1)}, bf16[3,512,512]{2,1,0:T(8,128)(2,1)}, u32[]{:S(2)}) copy-start(bf16[3,512,512]{2,1,0:T(8,128)(2,1)} %left.1) | copy-start | bytes 4718596
  2.0 14.0 %copy-start.1 = (bf16[3,512,512]{2,1,0:T(8,128)(2,1)S(1)}, bf16[3,512,512]{2,1,0:T(8,128)(2,1)}, u32[]{:S(2)}) copy-start(bf16[3,512,512]{2,1,0:T(8,128)(2,1)} %right.1) | copy-start | bytes 4718596
  2.0 18.8 %collective-permute-start = (bf16[2,512,512]{2,1,0:T(8,128)(2,1)}, bf16[2,512,512]{2,1,0:T(8,128)(2,1)}, u32[]{:S(2)}, u32[]{:S(2)}) collective-permute-start(bf16[2,512,512]{2,1,0:T(8,128)(2,1)} %shard_map.47.refs_3_), channel_id=1, source_target_pairs={{1,2},{3,4},{5,6},{7,8},{9,10},{11,12},{13,14},{15,16},{17,18},{19... | collective-permute-start | bytes 3145736 | tf_op jit(solution)/shard_map/ppermute | solution.py:206
  6.6 14.3 %collective-permute-start.1 = (bf16[2,512,512]{2,1,0:T(8,128)(2,1)}, bf16[2,512,512]{2,1,0:T(8,128)(2,1)}, u32[]{:S(2)}, u32[]{:S(2)}) collective-permute-start(bf16[2,512,512]{2,1,0:T(8,128)(2,1)} %shard_map.47.refs_3_), channel_id=1, source_target_pairs={{0,1},{1,0},{2,3},{3,2},{4,5},{5,4},{6,7},{7,6},{8,9},{9,8},{10,11... | collective-permute-start | bytes 3145736 | tf_op jit(solution)/shard_map/ppermute | solution.py:207
  10.5 29.7 %collective-permute-start.4 = (bf16[2,512,512]{2,1,0:T(8,128)(2,1)}, bf16[2,512,512]{2,1,0:T(8,128)(2,1)}, u32[]{:S(2)}, u32[]{:S(2)}) collective-permute-start(bf16[2,512,512]{2,1,0:T(8,128)(2,1)} %shard_map.50.refs_3_), channel_id=1, source_target_pairs={{1,2},{3,4},{5,6},{7,8},{9,10},{11,12},{13,14},{15,16},{17,18},{19... | collective-permute-start | bytes 3145736 | tf_op jit(solution)/shard_map/ppermute | solution.py:206
  13.9 26.4 %collective-permute-start.5 = (bf16[2,512,512]{2,1,0:T(8,128)(2,1)}, bf16[2,512,512]{2,1,0:T(8,128)(2,1)}, u32[]{:S(2)}, u32[]{:S(2)}) collective-permute-start(bf16[2,512,512]{2,1,0:T(8,128)(2,1)} %shard_map.50.refs_3_), channel_id=1, source_target_pairs={{0,1},{1,0},{2,3},{3,2},{4,5},{5,4},{6,7},{7,6},{8,9},{9,8},{10,11... | collective-permute-start | bytes 3145736 | tf_op jit(solution)/shard_map/ppermute | solution.py:207
  16.1 4.8 %copy-start.3 = (bf16[2,512,512]{2,1,0:T(8,128)(2,1)S(1)}, bf16[2,512,512]{2,1,0:T(8,128)(2,1)}, u32[]{:S(2)}) copy-start(bf16[2,512,512]{2,1,0:T(8,128)(2,1)} %shard_map.47.refs_3_) | copy-start | bytes 3145732
  20.8 19.5 %copy-start.2 = (bf16[2,512,512]{2,1,0:T(8,128)(2,1)S(1)}, bf16[2,512,512]{2,1,0:T(8,128)(2,1)}, u32[]{:S(2)}) copy-start(bf16[2,512,512]{2,1,0:T(8,128)(2,1)} %shard_map.50.refs_3_) | copy-start | bytes 3145732
  26.9 31.8 %collective-permute-start.2 = (bf16[2,160,512]{2,1,0:T(8,128)(2,1)S(1)}, bf16[2,160,512]{2,1,0:T(8,128)(2,1)S(1)}, u32[]{:S(2)}, u32[]{:S(2)}) collective-permute-start(bf16[2,160,512]{2,1,0:T(8,128)(2,1)S(1)} %get-tuple-element.18), channel_id=1, source_target_pairs={{0,32},{1,481},{2,34},{3,483},{4,36},{5,485},{6,38},{7,487},{8,40}... | collective-permute-start | bytes 983048 | tf_op jit(solution)/shard_map/ppermute | solution.py:193
  30.8 28.0 %collective-permute-start.3 = (bf16[2,160,512]{2,1,0:T(8,128)(2,1)S(1)}, bf16[2,160,512]{2,1,0:T(8,128)(2,1)S(1)}, u32[]{:S(2)}, u32[]{:S(2)}) collective-permute-start(bf16[2,160,512]{2,1,0:T(8,128)(2,1)S(1)} %get-tuple-element.19), channel_id=1, source_target_pairs={{0,480},{1,33},{2,482},{3,35},{4,484},{5,37},{6,486},{7,39},{8,488... | collective-permute-start | bytes 983048 | tf_op jit(solution)/shard_map/ppermute | solution.py:193
  46.3 12.6 %collective-permute-start.6 = (bf16[2,160,512]{2,1,0:T(8,128)(2,1)S(1)}, bf16[2,160,512]{2,1,0:T(8,128)(2,1)S(1)}, u32[]{:S(2)}, u32[]{:S(2)}) collective-permute-start(bf16[2,160,512]{2,1,0:T(8,128)(2,1)S(1)} %get-tuple-element.21), channel_id=1, source_target_pairs={{0,32},{1,481},{2,34},{3,483},{4,36},{5,485},{6,38},{7,487},{8,40}... | collective-permute-start | bytes 983048 | tf_op jit(solution)/shard_map/ppermute | solution.py:193
  48.3 10.7 %collective-permute-start.7 = (bf16[2,160,512]{2,1,0:T(8,128)(2,1)S(1)}, bf16[2,160,512]{2,1,0:T(8,128)(2,1)S(1)}, u32[]{:S(2)}, u32[]{:S(2)}) collective-permute-start(bf16[2,160,512]{2,1,0:T(8,128)(2,1)S(1)} %get-tuple-element.22), channel_id=1, source_target_pairs={{0,480},{1,33},{2,482},{3,35},{4,484},{5,37},{6,486},{7,39},{8,488... | collective-permute-start | bytes 983048 | tf_op jit(solution)/shard_map/ppermute | solution.py:193
  53.4 7.9 %collective-permute-start.8 = (bf16[2,2,32,512]{3,2,1,0:T(8,128)(2,1)S(1)}, bf16[2,2,32,512]{3,2,1,0:T(8,128)(2,1)S(1)}, u32[]{:S(2)}, u32[]{:S(2)}) collective-permute-start(bf16[2,2,32,512]{3,2,1,0:T(8,128)(2,1)S(1)} %pad_maximum_fusion), channel_id=1, source_target_pairs={{0,448},{1,65},{2,450},{3,67},{4,452},{5,69},{6,454},{7,71},{8,456... | collective-permute-start | bytes 393224 | tf_op jit(solution)/shard_map/ppermute | solution.py:193
  61.3 14.4 %collective-permute-start.9 = (bf16[2,2,32,512]{3,2,1,0:T(8,128)(2,1)S(1)}, bf16[2,2,32,512]{3,2,1,0:T(8,128)(2,1)S(1)}, u32[]{:S(2)}, u32[]{:S(2)}) collective-permute-start(bf16[2,2,32,512]{3,2,1,0:T(8,128)(2,1)S(1)} %fusion.2), channel_id=1, source_target_pairs={{0,416},{1,97},{2,418},{3,99},{4,420},{5,101},{6,422},{7,103},{8,4... | collective-permute-start | bytes 393224 | tf_op jit(solution)/shard_map/ppermute | solution.py:193
  65.1 17.2 %collective-permute-start.11 = (bf16[2,2,32,512]{3,2,1,0:T(8,128)(2,1)S(1)}, bf16[2,2,32,512]{3,2,1,0:T(8,128)(2,1)S(1)}, u32[]{:S(2)}, u32[]{:S(2)}) collective-permute-start(bf16[2,2,32,512]{3,2,1,0:T(8,128)(2,1)S(1)} %pad_maximum_fusion.1), channel_id=1, source_target_pairs={{0,96},{1,417},{2,98},{3,419},{4,100},{5,421},{6,102},{7,423},{8,1... | collective-permute-start | bytes 393224 | tf_op jit(solution)/shard_map/ppermute | solution.py:193
  75.8 14.9 %collective-permute-start.10 = (bf16[2,2,32,512]{3,2,1,0:T(8,128)(2,1)S(1)}, bf16[2,2,32,512]{3,2,1,0:T(8,128)(2,1)S(1)}, u32[]{:S(2)}, u32[]{:S(2)}) collective-permute-start(bf16[2,2,32,512]{3,2,1,0:T(8,128)(2,1)S(1)} %fusion.1), channel_id=1, source_target_pairs={{0,416},{1,97},{2,418},{3,99},{4,420},{5,101},{6,422},{7,103},{8,4... | collective-permute-start | bytes 393224 | tf_op jit(solution)/shard_map/ppermute | solution.py:193
  82.3 11.7 %collective-permute-start.12 = (bf16[2,2,32,512]{3,2,1,0:T(8,128)(2,1)S(1)}, bf16[2,2,32,512]{3,2,1,0:T(8,128)(2,1)S(1)}, u32[]{:S(2)}, u32[]{:S(2)}) collective-permute-start(bf16[2,2,32,512]{3,2,1,0:T(8,128)(2,1)S(1)} %fusion.3), channel_id=1, source_target_pairs={{0,96},{1,417},{2,98},{3,419},{4,100},{5,421},{6,102},{7,423},{8,1... | collective-permute-start | bytes 393224 | tf_op jit(solution)/shard_map/ppermute | solution.py:193
